TPU v7x, 32 devices: a whole 2x2x4 slice. The times are simulated.
32 devices in a mesh: groups: 2 (over x), tensor: 8 (over z, y), request: 2 (over core).
Axes of the slice: x: 2, y: 2, z: 4, core: 2. Of those that a mesh axis runs over, the one named last changes fastest.
Arguments:
- queries: bfloat16 [256, 1024], P(('groups', 'request'), 'tensor'), parts along dimension 0, may hold values from -120 to 120
- fresh_kv: bfloat16 [2, 256, 1024], P(None, ('groups', 'request'), 'tensor'), parts along dimension 1, may hold values from -5 to 5
- kv_cache: bfloat16 [2, 256, 128, 1024], P(None, ('groups', 'request'), None, 'tensor'), parts along dimension 1, may hold values from -5 to 5
- lengths: int32 [256], P(('groups', 'request')), parts along dimension 0, may hold values from 16 to 128, as said below
- stream: bfloat16 [256, 6144], P(('groups', 'request'), 'tensor'), parts along dimension 0, may hold values from -6 to 6
- out_weight: bfloat16 [1024, 6144], P('tensor'), may hold values from -0.25 to 0.25
- block_ids: int32 [256, 3], P('groups'), parts along dimension 0, may hold values from 0 to 31, all different within a row; in each aligned block of 128 rows (0 to 127, 128 to 255, ...) at most 48 rows name the same one
- up_weight: bfloat16 [6144, 4096], P(None, ('tensor', 'request')), may hold values from -0.078125 to 0.078125
- down_weight: bfloat16 [4096, 6144], P(('tensor', 'request')), may hold values from -0.3125 to 0.3125
Outputs:
- layer_out: bfloat16 [256, 6144], P(('groups', 'request'), 'tensor'), parts along dimension 0
There are 2 independent parts, one for each index of `groups`. A program takes and returns all parts, laid end to end along the dimension named above; an argument that names none is the same for every part. Nothing has to cross between parts.
Inputs may be any that keep to these rules, and one draw needn't show every extreme that they name: `block_ids`: each row names 3 different blocks; every block is named by some row; no block is named by more than 48 rows of the batch, and some block by exactly 48. `lengths`: some row of the batch uses all 128 positions.
All inputs are finite; a program needn't handle non-finite values.
Results may differ from a plain program's by a relative error of at most 0.0055.
Values may be sent and summed in bfloat16 or wider, within the bound.
No kernel may reach another device: no remote copies, remote signals or barrier semaphores. Data moves between devices by JAX's collectives and lax.ppermute only.
A program may use at most 64 MiB of HBM per device.

v0:
```python
import math

import jax
import jax.numpy as jnp
from jax import lax
from jax.sharding import PartitionSpec as P

HS = 128
BLOCK = 128
CACHE = 128


EPSILON = 1e-05


def attend_rows(queries, fresh_kv, kv_cache, lengths):
    row_count, width = queries.shape
    heads_here = width // HS
    shaped_q = queries.reshape(row_count, heads_here, HS)
    cache_keys = kv_cache[0].reshape(row_count, CACHE, heads_here, HS)
    cache_values = kv_cache[1].reshape(row_count, CACHE, heads_here, HS)
    scale = 1.0 / math.sqrt(HS)
    scores = (
        jnp.einsum("rhd,rphd->rhp", shaped_q, cache_keys, preferred_element_type=jnp.float32)
        * scale
    )
    positions = jnp.arange(CACHE)
    visible = positions[None, None, :] < lengths[:, None, None]
    scores = jnp.where(visible, scores, -jnp.inf)
    own_score = (
        jnp.einsum(
            "rhd,rhd->rh",
            shaped_q,
            fresh_kv[0].reshape(row_count, heads_here, HS),
            preferred_element_type=jnp.float32,
        )
        * scale
    )
    top = jnp.maximum(jnp.max(scores, axis=2), own_score)
    weights = jnp.exp(scores - top[:, :, None])
    own_weight = jnp.exp(own_score - top)
    total = jnp.sum(weights, axis=2) + own_weight
    probs = (weights / total[:, :, None]).astype(jnp.bfloat16)
    own_prob = (own_weight / total).astype(jnp.bfloat16)
    result = jnp.einsum("rhp,rphd->rhd", probs, cache_values, preferred_element_type=jnp.float32)
    result = result + own_prob.astype(jnp.float32)[:, :, None] * fresh_kv[1].reshape(
        row_count, heads_here, HS
    ).astype(jnp.float32)
    return result.astype(jnp.bfloat16).reshape(row_count, width)


def per_device(
    queries, fresh_kv, kv_cache, lengths, stream, out_weight, block_ids, up_weight, down_weight
):
    attended = attend_rows(queries, fresh_kv, kv_cache, lengths)
    partial_value = jnp.dot(attended, out_weight, preferred_element_type=jnp.float32)
    share_width = stream.shape[1]
    share_start = lax.axis_index("tensor") * share_width
    placed = lax.dynamic_update_slice_in_dim(
        jnp.zeros_like(partial_value), stream.astype(jnp.float32), share_start, 1
    )
    mixed_full = lax.psum(partial_value + placed, "tensor")
    center = jnp.mean(mixed_full, axis=1, keepdims=True)
    spread = jnp.mean(mixed_full * mixed_full, axis=1, keepdims=True) - center * center
    normed = ((mixed_full - center) * lax.rsqrt(spread + EPSILON)).astype(jnp.bfloat16)
    mixed_share = lax.dynamic_slice_in_dim(mixed_full, share_start, share_width, 1)
    normed_all = lax.all_gather(normed, "request", axis=0, tiled=True)
    total_rows = normed_all.shape[0]
    request_count = lax.axis_size("request")
    tensor_count = lax.axis_size("tensor")
    local_blocks = up_weight.shape[1] // BLOCK
    owner = lax.axis_index("tensor") * request_count + lax.axis_index("request")
    owned = owner * local_blocks + jnp.arange(local_blocks, dtype=jnp.int32)
    active = jnp.any(block_ids[:, :, None] == owned[None, None, :], axis=1)
    neuron_mask = jnp.repeat(active.astype(jnp.float32), BLOCK, axis=1)
    upward = jnp.dot(normed_all, up_weight, preferred_element_type=jnp.float32)
    hidden = (jax.nn.relu(upward) * neuron_mask).astype(jnp.bfloat16)
    partial_ffn = jnp.dot(hidden, down_weight, preferred_element_type=jnp.float32)
    own_rows = total_rows // request_count
    feature_width = partial_ffn.shape[1] // tensor_count
    blocked = partial_ffn.reshape(request_count, own_rows, tensor_count, feature_width)
    group_ids = jnp.arange(own_rows * lax.axis_size(("tensor", "request")) // own_rows)
    picked = blocked[group_ids % request_count, :, group_ids // request_count, :]
    ffn_share = lax.psum_scatter(
        picked.reshape(own_rows * lax.axis_size(("tensor", "request")), feature_width),
        ("tensor", "request"),
        scatter_dimension=0,
        tiled=True,
    )
    return (mixed_share + ffn_share).astype(jnp.bfloat16)


def solution(mesh):
    in_specs = (
        P(("groups", "request"), "tensor"),
        P(None, ("groups", "request"), "tensor"),
        P(None, ("groups", "request"), None, "tensor"),
        P(("groups", "request")),
        P(("groups", "request"), "tensor"),
        P("tensor", None),
        P("groups", None),
        P(None, ("tensor", "request")),
        P(("tensor", "request"), None),
    )
    out_specs = P(("groups", "request"), "tensor")
    return jax.shard_map(
        per_device, mesh=mesh, in_specs=in_specs, out_specs=out_specs, check_vma=False
    )
```

profile of v0, /device:TPU:0, one launch (start us, length us, event | category | flops | bytes accessed | tf_op | source)
XLA Modules:
  0.0 212.9 jit_solution(17063477790009390138)
XLA Ops:
  6.5 0.0 copy-start
  6.5 0.0 copy-start.4
  6.5 0.0 copy-start.5
  6.5 0.0 copy-start.3
  6.5 0.0 all-reduce.2.cloned.1.call-start
  6.6 2.9 %fusion.2 = f32[64,1,128]{2,1,0:T(1,128)S(1)} fusion(bf16[2,64,128,128]{3,2,1,0:T(8,128)(2,1)} %param.11, bf16[64,128,1]{1,0,2:T(8,128)(2,1)} %bitcast.45), kind=kOutput, calls=%fused_computation.3 | convolution fusion | flops 2097152 | bytes 2146304 | tf_op jit(solution)/shard_map/rhd,rphd->rhp/dot_general | solution.py:24
  9.5 0.0 copy-done.4
  9.5 0.0 copy-done.5
  9.5 0.0 copy-done.3
  9.6 0.2 fusion.14
  9.7 0.2 fusion.17
  9.9 0.1 fusion.24
  10.1 2.2 %fusion = f32[64,1,128]{2,1,0:T(1,128)S(1)} fusion(bf16[2,64,128,128]{3,2,1,0:T(8,128)(2,1)} %param.11, bf16[64,128,1]{1,0,2:T(8,128)(2,1)S(1)} %fusion.24), kind=kOutput, calls=%fused_computation.1 | convolution fusion | flops 2097152 | bytes 2146304 | tf_op jit(solution)/shard_map/rhp,rphd->rhd/dot_general | solution.py:45
  12.3 0.0 copy-start.2
  12.3 3.0 %fusion.19 = f32[64,6144]{1,0:T(8,128)} fusion(bf16[128,6144]{1,0:T(8,128)(2,1)} %param.14, f32[64,128]{1,0:T(8,128)S(1)} %bitcast.44, bf16[2,64,128]{2,1,0:T(8,128)(2,1)S(1)} %copy-done.3, f32[64]{0:T(128)S(1)} %get-tuple-element.7), kind=kOutput, calls=%fused_computation.31 | convolution fusion | flops 100696064 | bytes 3195392 | tf_op jit(solution)/shard_map/dot_general | solution.py:56
  15.3 0.0 copy-done.2
  15.3 1.6 add_dynamic-update-slice_fusion
  17.0 0.0 all-reduce.2.cloned.1.call-update
  17.0 0.0 copy-start.6
  17.0 0.0 all-gather.2.cloned.1.call-start
  17.1 91.8 %all-reduce.2.cloned.1.call-done = f32[64,6144]{1,0:T(8,128)} async-done(((f32[64,6144]{1,0:T(8,128)}), f32[64,6144]{1,0:T(8,128)}) %all-reduce.2.cloned.1.call-update) | async-done | bytes 1572880 | tf_op jit(solution)/shard_map/psum | solution.py:62
  108.8 0.0 copy-start.1
  108.8 1.8 fusion.33
  110.6 0.1 copy-done.1
  110.7 1.1 multiply_convert_fusion
  111.8 0.0 all-gather.2.cloned.1.call-update
  111.8 0.0 reduce-scatter.2.cloned.1.call-start
  111.9 0.0 copy-done.6
  111.9 0.1 compare_reduce_fusion
  112.0 0.1 copy.13
  112.1 9.0 %all-gather.2.cloned.1.call-done = bf16[128,6144]{1,0:T(8,128)(2,1)} async-done(((bf16[64,6144]{1,0:T(8,128)(2,1)}), bf16[128,6144]{1,0:T(8,128)(2,1)}) %all-gather.2.cloned.1.call-update) | async-done | bytes 1572880 | tf_op jit(solution)/shard_map/all_gather | solution.py:67
  121.2 0.2 broadcast_in_dim.7
  121.4 0.0 copy-done
  121.4 5.9 %fusion.8 = f32[128,6144]{1,0:T(8,128)} fusion(bf16[256,6144]{1,0:T(8,128)(2,1)S(1)} %copy-done, bf16[128,6144]{1,0:T(8,128)(2,1)} %all-gather.2.cloned.1.call-done, bf16[6144,256]{1,0:T(8,128)(2,1)} %param.16, f32[16,8,2,128]{3,2,1,0:T(2,128)S(1)} %bitcast.40), kind=kOutput, calls=%fused_computation.12 | convolution fusion | flops 805404672 | bytes 11141120 | tf_op jit(solution)/shard_map/dot_general | solution.py:78
  127.3 2.9 %copy.24 = f32[16,8,8,768]{3,2,1,0:T(8,128)S(1)} copy(f32[16,8,8,768]{3,1,2,0:T(8,128)} %bitcast.39) | data formatting | bytes 6291456
  130.2 2.6 %copy.14 = f32[2,64,8,768]{3,1,2,0:T(8,128)} copy(f32[2,64,8,768]{3,2,1,0:T(8,128)S(1)} %bitcast.38) | data formatting | bytes 6291456 | tf_op jit(solution)/shard_map/reshape | solution.py:81
  132.8 4.3 %gather_fusion = f32[16,64,768]{2,1,0:T(8,128)} fusion(f32[2,64,8,768]{3,1,2,0:T(8,128)} %copy.14, s32[16]{0:T(128)S(1)} %fusion.30), kind=kCustom, calls=%fused_computation | custom fusion | bytes 6291584 | tf_op jit(solution)/shard_map/gather | solution.py:83
  137.1 0.0 reduce-scatter.2.cloned.1.call-update
  137.1 67.6 %reduce-scatter.2.cloned.1.call-done = f32[64,768]{1,0:T(8,128)} async-done(((f32[1024,768]{1,0:T(8,128)}), f32[64,768]{1,0:T(8,128)}) %reduce-scatter.2.cloned.1.call-update) | async-done | bytes 196624 | tf_op jit(solution)/shard_map/reduce_scatter | solution.py:84
  204.7 1.7 add_convert_fusion
  (6 shorter events, 0.1 us)
Async XLA Ops:
  6.5 114.8 %copy-start = (bf16[256,6144]{1,0:T(8,128)(2,1)S(1)}, bf16[256,6144]{1,0:T(8,128)(2,1)}, u32[]{:S(2)}) copy-start(bf16[256,6144]{1,0:T(8,128)(2,1)} %param.17) | copy-start | bytes 9437188
  6.5 3.0 %copy-start.4 = (bf16[64,128]{1,0:T(8,128)(2,1)S(1)}, bf16[64,128]{1,0:T(8,128)(2,1)}, u32[]{:S(2)}) copy-start(bf16[64,128]{1,0:T(8,128)(2,1)} %param.9) | copy-start | bytes 49156
  6.5 3.0 %copy-start.5 = (s32[64]{0:T(128)S(1)}, s32[64]{0:T(128)}, u32[]{:S(2)}) copy-start(s32[64]{0:T(128)} %param.12) | copy-start | bytes 772
  6.5 3.0 %copy-start.3 = (bf16[2,64,128]{2,1,0:T(8,128)(2,1)S(1)}, bf16[2,64,128]{2,1,0:T(8,128)(2,1)}, u32[]{:S(2)}) copy-start(bf16[2,64,128]{2,1,0:T(8,128)(2,1)} %param.10) | copy-start | bytes 98308
  6.5 102.3 %all-reduce.2.cloned.1.call-start = ((), (), s32[]{:S(2)}) async-start(), calls=%async_computation.1 | async-start | bytes 3145728 | tf_op jit(solution)/shard_map/psum | solution.py:62
  12.3 3.0 %copy-start.2 = (bf16[64,768]{1,0:T(8,128)(2,1)S(1)}, bf16[64,768]{1,0:T(8,128)(2,1)}, u32[]{:S(2)}) copy-start(bf16[64,768]{1,0:T(8,128)(2,1)} %param.13) | copy-start | bytes 294916
  17.0 94.9 %copy-start.6 = (s32[128,3]{0,1:T(4,128)S(1)}, s32[128,3]{0,1:T(4,128)}, u32[]{:S(2)}) copy-start(s32[128,3]{0,1:T(4,128)} %param.15) | copy-start | bytes 4612
  17.0 104.2 %all-gather.2.cloned.1.call-start = ((), (), s32[]{:S(2)}) async-start(), calls=%async_computation.2 | async-start | bytes 2359296 | tf_op jit(solution)/shard_map/all_gather | solution.py:67
  108.8 1.9 copy-start.1
  111.8 92.8 %reduce-scatter.2.cloned.1.call-start = ((), (), s32[]{:S(2)}) async-start(), calls=%async_computation.3 | async-start | bytes 3342336 | tf_op jit(solution)/shard_map/reduce_scatter | solution.py:84
Sparse Core Ops, SparseCore 0:
  17.1 91.6 all-reduce.1
  112.0 9.1 all-gather.1
  137.2 67.3 reduce-scatter.1
where the time goes:
time: 213 us
  waiting for transfers between devices  168 us (79%)
  matrix products  14.1 us (7%)
  between operations  13.2 us (6%)
  local copies, waits for them, and re-layouts  10.3 us (5%)
  other arithmetic  6.8 us (3%)
    psum x1, waiting for transfers between devices, per_device(): mixed_full = lax.psum(partial_value + placed, 'tensor')  91.8 us
    reduce_scatter x1, waiting for transfers between devices, per_device(): lax.psum_scatter(picked.reshape(own_rows * lax.axis_size(('tensor', 'requ...  67.6 us
    all_gather x1, waiting for transfers between devices, per_device(): normed_all = lax.all_gather(normed, 'request', axis=0, tiled=True)  9.04 us
    dot_general x1, matrix products, per_device(): jnp.dot(hidden, down_weight, preferred_element_type=jnp.float32)  5.9 us
    gather x1, local copies, waits for them, and re-layouts, per_device(): blocked[group_ids % request_count, :, group_ids // request_count, :]  4.3 us
  transfers between devices with their start and end apart: 3, of which 3 were waited for; matrix products, arithmetic and copies ran while one was open for 0% of the time, Pallas kernels for 0%

commit v1 on v0

v1 whole, which is shorter than its diff:
```python
import math

import jax
import jax.numpy as jnp
from jax import lax
from jax.experimental import pallas as pl
from jax.experimental.pallas import tpu as pltpu
from jax.sharding import PartitionSpec as P

HS = 128
BLOCK = 128
EPSILON = 1e-05
CHUNKS = 1
F32 = jnp.float32
BF16 = jnp.bfloat16


def attend_rows(queries, fresh_kv, kv_cache, lengths):
    row_count, width = queries.shape
    heads_here = width // HS
    cache = kv_cache.shape[2]
    shaped_q = queries.reshape(row_count, heads_here, HS)
    cache_keys = kv_cache[0].reshape(row_count, cache, heads_here, HS)
    cache_values = kv_cache[1].reshape(row_count, cache, heads_here, HS)
    scale = 1.0 / math.sqrt(HS)
    scores = jnp.einsum("rhd,rphd->rhp", shaped_q, cache_keys, preferred_element_type=F32) * scale
    positions = jnp.arange(cache)
    visible = positions[None, None, :] < lengths[:, None, None]
    scores = jnp.where(visible, scores, -jnp.inf)
    own_score = (
        jnp.einsum(
            "rhd,rhd->rh",
            shaped_q,
            fresh_kv[0].reshape(row_count, heads_here, HS),
            preferred_element_type=F32,
        )
        * scale
    )
    top = jnp.maximum(jnp.max(scores, axis=2), own_score)
    weights = jnp.exp(scores - top[:, :, None])
    own_weight = jnp.exp(own_score - top)
    total = jnp.sum(weights, axis=2) + own_weight
    probs = (weights / total[:, :, None]).astype(BF16)
    own_prob = (own_weight / total).astype(BF16)
    result = jnp.einsum("rhp,rphd->rhd", probs, cache_values, preferred_element_type=F32)
    result = result + own_prob.astype(F32)[:, :, None] * fresh_kv[1].reshape(
        row_count, heads_here, HS
    ).astype(F32)
    return result.astype(BF16).reshape(row_count, width)


def project_kernel(places, attended, weight, stream, keep, send):
    half, _, width = keep.shape
    values = attended[...]
    for p in range(2 * half):
        columns = pl.ds(pl.multiple_of(places[p] * width, width), width)
        piece = jnp.dot(values, weight[:, columns], preferred_element_type=F32)
        if p == 0:
            piece = piece + stream[...].astype(F32)
        if p < half:
            keep[p] = piece
        else:
            send[p - half] = piece.astype(BF16)


def project(places, attended, weight, stream):
    count, (rows, width) = places.shape[0], stream.shape
    half = count // 2
    if width % 128:
        ordered = weight.reshape(weight.shape[0], count, width)[:, places]
        pieces = jnp.einsum("rk,kpw->prw", attended, ordered, preferred_element_type=F32)
        pieces = pieces.at[0].add(stream.astype(F32))
        return pieces[:half], pieces[half:].astype(BF16)
    return pl.pallas_call(
        project_kernel,
        in_specs=[pl.BlockSpec(memory_space=pltpu.SMEM)] + [pl.BlockSpec(memory_space=pltpu.VMEM)] * 3,
        out_specs=[pl.BlockSpec(memory_space=pltpu.VMEM)] * 2,
        out_shape=[
            jax.ShapeDtypeStruct((half, rows, width), F32),
            jax.ShapeDtypeStruct((half, rows, width), BF16),
        ],
        compiler_params=pltpu.CompilerParams(vmem_limit_bytes=16 * 1024 * 1024),
        cost_estimate=pl.CostEstimate(
            flops=2 * attended.size * count * width, bytes_accessed=weight.size * 2, transcendentals=0
        ),
        name="project",
    )(places, attended, weight, stream)


def feed_kernel(places, first, second, up_own, up_other, down_own, down_other, ids, owners, keep, send):
    half, rows, width = keep.shape
    pieces = [first[p].astype(F32) for p in range(half)] + [second[p].astype(F32) for p in range(half)]
    features = 2 * half * width
    total = sum(jnp.sum(piece, axis=1, keepdims=True) for piece in pieces)
    squares = sum(jnp.sum(piece * piece, axis=1, keepdims=True) for piece in pieces)
    center = total * (1.0 / features)
    spread = squares * (1.0 / features) - center * center
    scale = lax.rsqrt(spread + EPSILON)
    neurons = up_own.shape[1]
    own = jnp.zeros((rows, neurons), F32)
    other = jnp.zeros((rows, neurons), F32)
    for p in range(2 * half):
        normed = ((pieces[p] - center) * scale).astype(BF16)
        span = pl.ds(pl.multiple_of(places[p] * width, width), width)
        own += jnp.dot(normed, up_own[span, :], preferred_element_type=F32)
        other += jnp.dot(normed, up_other[span, :], preferred_element_type=F32)
    named = ids[...]
    blocks = owners[...]
    active = named[:, 0:1] == blocks
    for k in range(1, named.shape[1]):
        active = active | (named[:, k : k + 1] == blocks)
    own = jnp.where(active[:, :neurons], jnp.maximum(own, 0.0), 0.0).astype(BF16)
    other = jnp.where(active[:, neurons:], jnp.maximum(other, 0.0), 0.0).astype(BF16)
    for p in range(2 * half):
        span = pl.ds(pl.multiple_of(places[p] * width, width), width)
        piece = jnp.dot(own, down_own[:, span], preferred_element_type=F32)
        piece += jnp.dot(other, down_other[:, span], preferred_element_type=F32)
        if p < half:
            keep[p] = piece
        else:
            send[p - half] = piece.astype(BF16)


def feed(places, first, second, ups, downs, ids, owners):
    half, rows, width = first.shape
    count = 2 * half
    if width % 128:
        mixed = jnp.concatenate([first, second]).astype(F32)
        center = jnp.mean(mixed, axis=(0, 2), keepdims=True)
        spread = jnp.mean(mixed * mixed, axis=(0, 2), keepdims=True) - center * center
        normed = ((mixed - center) * lax.rsqrt(spread + EPSILON)).astype(BF16)
        upward = [
            jnp.einsum("prw,pwn->rn", normed, up.reshape(count, width, -1)[places], preferred_element_type=F32)
            for up in ups
        ]
        active = jnp.any(ids[:, :, None] == owners[0][None, None, :], axis=1)
        hidden = jnp.where(active, jax.nn.relu(jnp.concatenate(upward, axis=1)), 0.0).astype(BF16)
        down = jnp.concatenate(downs, axis=0).reshape(-1, count, width)[:, places]
        pieces = jnp.einsum("rn,npw->prw", hidden, down, preferred_element_type=F32)
        return pieces[:half], pieces[half:].astype(BF16)
    return pl.pallas_call(
        feed_kernel,
        in_specs=[pl.BlockSpec(memory_space=pltpu.SMEM)] + [pl.BlockSpec(memory_space=pltpu.VMEM)] * 8,
        out_specs=[pl.BlockSpec(memory_space=pltpu.VMEM)] * 2,
        out_shape=[
            jax.ShapeDtypeStruct((half, rows, width), F32),
            jax.ShapeDtypeStruct((half, rows, width), BF16),
        ],
        compiler_params=pltpu.CompilerParams(vmem_limit_bytes=32 * 1024 * 1024),
        cost_estimate=pl.CostEstimate(
            flops=8 * rows * ups[0].size, bytes_accessed=ups[0].size * 8, transcendentals=0
        ),
        name="feed",
    )(places, first, second, *ups, *downs, ids, owners)


def per_device(
    queries, fresh_kv, kv_cache, lengths, stream, out_weight, block_ids, up_weight, down_weight
):
    tensor_count = lax.axis_size("tensor")
    cores = lax.axis_size("request")
    rounds = tensor_count.bit_length() - 1
    tensor, core = lax.axis_index("tensor"), lax.axis_index("request")
    orders = [list(range(rounds)) for _ in range(cores)]
    for c in range(cores):
        if c % 2 and rounds > 1:
            orders[c][0], orders[c][1] = orders[c][1], orders[c][0]

    def swap(array, step):
        pairs = [
            (t * cores + c, (t ^ (1 << orders[c][step])) * cores + c)
            for t in range(tensor_count)
            for c in range(cores)
        ]
        return lax.ppermute(array, ("tensor", "request"), pairs)

    spots = jnp.array(
        [
            [
                sum(((p >> (rounds - 1 - j)) & 1) << orders[c][j] for j in range(rounds))
                for p in range(tensor_count)
            ]
            for c in range(cores)
        ],
        jnp.int32,
    )
    places = spots[core] ^ tensor
    across = [(c, c ^ 1) for c in range(cores)]
    up_other = lax.ppermute(up_weight, "request", across)
    down_other = lax.ppermute(down_weight, "request", across)
    local_blocks = up_weight.shape[1] // BLOCK
    neurons = jnp.arange(local_blocks * BLOCK, dtype=jnp.int32) // BLOCK
    owners = jnp.concatenate(
        [
            (tensor * cores + core) * local_blocks + neurons,
            (tensor * cores + (core ^ 1)) * local_blocks + neurons,
        ]
    )[None, :]
    row_count = queries.shape[0]
    own_ids = lax.dynamic_slice_in_dim(block_ids, core * row_count, row_count, 0)
    attended = attend_rows(queries, fresh_kv, kv_cache, lengths)

    outs = []
    size = row_count // CHUNKS
    for chunk in range(CHUNKS):
        rows = slice(chunk * size, (chunk + 1) * size)
        keep, send = project(places, attended[rows], out_weight, stream[rows])
        for step in range(rounds - 1):
            total = keep + swap(send, step).astype(F32)
            half = total.shape[0] // 2
            if step < rounds - 2:
                keep, send = total[:half], total[half:].astype(BF16)
        got = swap(total.astype(BF16), rounds - 1)
        mixed = total + got[::-1].astype(F32)
        share = mixed[0]
        parts = mixed.astype(BF16)
        for step in range(rounds - 2, 0, -1):
            parts = jnp.concatenate([parts, swap(parts, step)])
        second = swap(parts, 0)
        keep, send = feed(places, parts, second, (up_weight, up_other), (down_weight, down_other), own_ids[rows], owners)
        for step in range(rounds):
            total = keep + swap(send, step).astype(F32)
            half = total.shape[0] // 2
            if half:
                keep, send = total[:half], total[half:].astype(BF16)
        outs.append((share + total[0]).astype(BF16))
    return jnp.concatenate(outs) if CHUNKS > 1 else outs[0]


def solution(mesh):
    in_specs = (
        P(("groups", "request"), "tensor"),
        P(None, ("groups", "request"), "tensor"),
        P(None, ("groups", "request"), None, "tensor"),
        P(("groups", "request")),
        P(("groups", "request"), "tensor"),
        P("tensor", None),
        P("groups", None),
        P(None, ("tensor", "request")),
        P(("tensor", "request"), None),
    )
    out_specs = P(("groups", "request"), "tensor")
    return jax.shard_map(
        per_device, mesh=mesh, in_specs=in_specs, out_specs=out_specs, check_vma=False
    )
```

time: 213 us -> 80.7 us (0.38)
  waiting for transfers between devices: 168 us -> 45.3 us
  starting transfers between devices: 0.12 us -> 14.5 us
  between operations: 13.2 us -> 0.16 us
  matrix products: 14.1 us -> 5.01 us
  local copies, waits for them, and re-layouts: 10.3 us -> 3.51 us
  Pallas kernels: 0 us -> 6.57 us
    psum x1 -> x0, waiting for transfers between devices: 91.8 us -> none  [per_device(): mixed_full = lax.psum(partial_value + placed, 'tensor')]
    reduce_scatter x1 -> x0, waiting for transfers between devices: 67.6 us -> none  [per_device(): lax.psum_scatter(picked.reshape(own_rows * lax.axis_size(('tensor', 'requ...]
    ppermute x0 -> x10, waiting for transfers between devices: none -> 45.3 us  [the longest x8 45.3 us: swap(): return lax.ppermute(array, ('tensor', 'request'), pairs)]
    ppermute x0 -> x10, starting transfers between devices: none -> 14.5 us  [the longest x8 13.9 us: swap(): return lax.ppermute(array, ('tensor', 'request'), pairs)]
    all_gather x1 -> x0, waiting for transfers between devices: 9.04 us -> none  [per_device(): normed_all = lax.all_gather(normed, 'request', axis=0, tiled=True)]
    dot_general x3 -> x1, matrix products: 11.2 us -> 2.24 us  [attend_rows(): jnp.einsum('rhp,rphd->rhd', probs, cache_values, preferred_element_type=F32)]
    pallas_call x0 -> x2, Pallas kernels: none -> 6.57 us  [the longest x1 5.64 us: feed(): pl.pallas_call(feed_kernel, in_specs=[pl.BlockSpec(memory_space=pltpu.SME...]
    gather x1 -> x0, local copies, waits for them, and re-layouts: 4.3 us -> none  [per_device(): blocked[group_ids % request_count, :, group_ids // request_count, :]]
  transfers between devices with their start and end apart: 3 -> 10, of which waited for: 3 -> 8; matrix products, arithmetic and copies ran while one was open for 0% -> 13% of each run, Pallas kernels for 0% -> 1%
where the time goes in v1:
time: 80.7 us; the launch traced here: 80.3 us
  waiting for transfers between devices  45.3 us (56%)
  starting transfers between devices  14.5 us (18%)
  Pallas kernels  6.57 us (8%)
  other arithmetic  5.26 us (7%)
  matrix products  5.01 us (6%)
  local copies, waits for them, and re-layouts  3.51 us (4%)
    ppermute x8, waiting for transfers between devices, swap(): return lax.ppermute(array, ('tensor', 'request'), pairs)  45.3 us
    ppermute x8, starting transfers between devices, swap(): return lax.ppermute(array, ('tensor', 'request'), pairs)  13.9 us
    pallas_call x1, Pallas kernels, feed(): pl.pallas_call(feed_kernel, in_specs=[pl.BlockSpec(memory_space=pltpu.SME...  5.64 us
    unnamed x17, local copies, waits for them, and re-layouts  3.38 us
    dot_general x1, matrix products, attend_rows(): jnp.einsum('rhd,rphd->rhp', shaped_q, cache_keys, preferred_element_type=...  2.77 us
    dot_general x1, matrix products, attend_rows(): jnp.einsum('rhp,rphd->rhd', probs, cache_values, preferred_element_type=F32)  2.24 us
  transfers between devices with their start and end apart: 10, of which 8 were waited for; matrix products, arithmetic and copies ran while one was open for 13% of the time, Pallas kernels for 1%

profile of v1, /device:TPU:0, one launch (start us, length us, event | category | flops | bytes accessed | tf_op | source)
XLA Modules:
  0.0 80.3 jit_solution(2376778822523111759)
XLA Ops:
  0.0 0.0 copy-start
  0.0 0.0 copy-start.7
  0.0 0.5 collective-permute-start.5
  0.5 0.1 collective-permute-start.6
  0.6 2.8 %fusion.2 = f32[64,1,128]{2,1,0:T(1,128)S(1)} fusion(bf16[2,64,128,128]{3,2,1,0:T(8,128)(2,1)} %param.12, bf16[64,128,1]{1,0,2:T(8,128)(2,1)} %bitcast.28), kind=kOutput, calls=%fused_computation.2 | convolution fusion | flops 2097152 | bytes 2146304 | tf_op jit(solution)/shard_map/rhd,rphd->rhp/dot_general | solution.py:26
  3.4 0.9 %fusion.12 = (f32[64]{0:T(128)S(1)}, f32[64]{0:T(128)S(1)}) fusion(bf16[64,128]{1,0:T(8,128)(2,1)} %param.10, bf16[2,64,128]{2,1,0:T(8,128)(2,1)} %param.11, f32[64,128]{1,0:T(8,128)S(1)} %bitcast.24, s32[64]{0:T(128)} %param.13), kind=kLoop, calls=%fused_computation.24 | loop fusion | flops 65408 | bytes 66304 | tf_op jit(solution)/shard_map/rhd,rhd->rh/dot_general | solution.py:31
  4.3 0.9 %fusion.15 = f32[64]{0:T(128)S(1)} fusion(f32[64,128]{1,0:T(8,128)S(1)} %bitcast.25, f32[64]{0:T(128)S(1)} %multiply_maximum_fusion, s32[64]{0:T(128)} %param.13), kind=kLoop, calls=%fused_computation.31 | loop fusion | flops 40896 | bytes 33536 | tf_op jit(solution)/shard_map/reduce_sum | solution.py:42
  5.2 0.0 copy-start.3
  5.2 0.8 %xor_bitcast_fusion.places = s32[8]{0:T(128)S(1)} fusion(s32[2,8]{1,0:T(2,128)} %constant.42.clone, s32[]{:T(128)S(6)} %select_n.18, s32[]{:T(128)S(6)} %axis_index.25), kind=kLoop, calls=%fused_computation.43 | loop fusion | flops 8 | bytes 72 | tf_op jit(solution)/shard_map/xor | solution.py:187
  6.0 0.8 fusion.17
  6.8 2.2 %fusion = f32[64,1,128]{2,1,0:T(1,128)S(1)} fusion(bf16[2,64,128,128]{3,2,1,0:T(8,128)(2,1)} %param.12, bf16[64,128,1]{1,0,2:T(8,128)(2,1)S(1)} %fusion.17), kind=kOutput, calls=%fused_computation | convolution fusion | flops 2097152 | bytes 2146304 | tf_op jit(solution)/shard_map/rhp,rphd->rhd/dot_general | solution.py:45
  9.0 0.0 copy-done.7
  9.0 0.1 fusion.11.attended
  9.1 0.0 copy-done.5
  9.1 0.0 copy-done.3
  9.1 0.0 copy-start.1
  9.2 0.9 %project.1 = (f32[4,64,768]{2,1,0:T(8,128)S(1)}, bf16[4,64,768]{2,1,0:T(8,128)(2,1)S(1)}) custom-call(s32[8]{0:T(128)S(1)} %xor_bitcast_fusion.places, bf16[64,128]{1,0:T(8,128)(2,1)S(1)} %fusion.11.attended, bf16[128,6144]{1,0:T(8,128)(2,1)S(1)} %copy-done.3, bf16[64,768]{1,0:T(8,128)(2,1)S(1)} %copy-done.5), custom_call_target="tpu_custom_call" | custom-call | flops 100663296 | bytes 1572864 | tf_op jit(solution)/shard_map/project/pallas_call | solution.py:74
  10.1 3.0 %collective-permute-start = (bf16[4,64,768]{2,1,0:T(8,128)(2,1)S(1)}, bf16[4,64,768]{2,1,0:T(8,128)(2,1)S(1)}, u32[]{:S(2)}, u32[]{:S(2)}) collective-permute-start(bf16[4,64,768]{2,1,0:T(8,128)(2,1)S(1)} %get-tuple-element.10), channel_id=1, source_target_pairs={{0,2},{1,5},{2,0},{3,7},{4,6},{5,1},{6,4},{7,3},{8,10},{9,13},{10,... | collective-permute-start | bytes 1179656 | tf_op jit(solution)/shard_map/ppermute | solution.py:175
  13.1 5.8 %collective-permute-done = bf16[4,64,768]{2,1,0:T(8,128)(2,1)S(1)} collective-permute-done((bf16[4,64,768]{2,1,0:T(8,128)(2,1)S(1)}, bf16[4,64,768]{2,1,0:T(8,128)(2,1)S(1)}, u32[]{:S(2)}, u32[]{:S(2)}) %collective-permute-start) | collective-permute-done | bytes 393248 | tf_op jit(solution)/shard_map/ppermute | solution.py:175
  18.8 0.1 convert_add_fusion.1
  19.0 2.2 %collective-permute-start.1 = (bf16[2,64,768]{2,1,0:T(8,128)(2,1)S(1)}, bf16[2,64,768]{2,1,0:T(8,128)(2,1)S(1)}, u32[]{:S(2)}, u32[]{:S(2)}) collective-permute-start(bf16[2,64,768]{2,1,0:T(8,128)(2,1)S(1)} %slice.84), channel_id=1, source_target_pairs={{0,4},{1,3},{2,6},{3,1},{4,0},{5,7},{6,2},{7,5},{8,12},{9,11},{10,... | collective-permute-start | bytes 589832 | tf_op jit(solution)/shard_map/ppermute | solution.py:175
  21.1 3.6 %collective-permute-done.1 = bf16[2,64,768]{2,1,0:T(8,128)(2,1)S(1)} collective-permute-done((bf16[2,64,768]{2,1,0:T(8,128)(2,1)S(1)}, bf16[2,64,768]{2,1,0:T(8,128)(2,1)S(1)}, u32[]{:S(2)}, u32[]{:S(2)}) %collective-permute-start.1) | collective-permute-done | bytes 196640 | tf_op jit(solution)/shard_map/ppermute | solution.py:175
  24.8 3.1 %collective-permute-start.2 = (bf16[2,64,768]{2,1,0:T(8,128)(2,1)S(1)}, bf16[2,64,768]{2,1,0:T(8,128)(2,1)S(1)}, u32[]{:S(2)}, u32[]{:S(2)}) collective-permute-start(bf16[2,64,768]{2,1,0:T(8,128)(2,1)S(1)} %fusion.6), channel_id=1, source_target_pairs={{0,8},{1,9},{2,10},{3,11},{4,12},{5,13},{6,14},{7,15},{8,0},{9,1},... | collective-permute-start | bytes 589832 | tf_op jit(solution)/shard_map/ppermute | solution.py:175
  27.9 7.6 %collective-permute-done.2 = bf16[2,64,768]{2,1,0:T(8,128)(2,1)S(1)} collective-permute-done((bf16[2,64,768]{2,1,0:T(8,128)(2,1)S(1)}, bf16[2,64,768]{2,1,0:T(8,128)(2,1)S(1)}, u32[]{:S(2)}, u32[]{:S(2)}) %collective-permute-start.2) | collective-permute-done | bytes 196640 | tf_op jit(solution)/shard_map/ppermute | solution.py:175
  35.5 0.8 %fusion.20 = (bf16[2,64,768]{2,1,0:T(8,128)(2,1)S(1)}, f32[2,64,768]{2,1,0:T(8,128)}) fusion(bf16[2,64,768]{2,1,0:T(8,128)(2,1)S(1)} %collective-permute-done.2, bf16[2,64,768]{2,1,0:T(8,128)(2,1)S(1)} %collective-permute-done.1, f32[4,64,768]{2,1,0:T(8,128)S(1)} %convert_add_fusion.1), kind=kLoop, calls=%fused_computation.47 | loop fusion | flops 491520 | bytes 1376256 | tf_op jit(solution)/shard_map/convert_element_type | solution.py:216
  36.4 0.7 collective-permute-start.3
  37.1 4.9 %collective-permute-done.3 = bf16[2,64,768]{2,1,0:T(8,128)(2,1)S(1)} collective-permute-done((bf16[2,64,768]{2,1,0:T(8,128)(2,1)S(1)}, bf16[2,64,768]{2,1,0:T(8,128)(2,1)S(1)}, u32[]{:S(2)}, u32[]{:S(2)}) %collective-permute-start.3) | collective-permute-done | bytes 196640 | tf_op jit(solution)/shard_map/ppermute | solution.py:175
  42.1 1.7 %collective-permute-start.4 = (bf16[4,64,768]{2,1,0:T(8,128)(2,1)S(1)}, bf16[4,64,768]{2,1,0:T(8,128)(2,1)}, u32[]{:S(2)}, u32[]{:S(2)}) collective-permute-start(bf16[4,64,768]{2,1,0:T(8,128)(2,1)S(1)} %pad_maximum_fusion.first), channel_id=1, source_target_pairs={{0,2},{1,5},{2,0},{3,7},{4,6},{5,1},{6,4},{7,3},{8,10},{9,13},{10,... | collective-permute-start | bytes 1179656 | tf_op jit(solution)/shard_map/ppermute | solution.py:175
  43.7 0.0 copy-done
  43.8 0.1 constant_dynamic-slice_fusion
  43.8 0.7 copy.21.ids
  44.6 5.5 %collective-permute-done.4.second = bf16[4,64,768]{2,1,0:T(8,128)(2,1)} collective-permute-done((bf16[4,64,768]{2,1,0:T(8,128)(2,1)S(1)}, bf16[4,64,768]{2,1,0:T(8,128)(2,1)}, u32[]{:S(2)}, u32[]{:S(2)}) %collective-permute-start.4) | collective-permute-done | bytes 393248 | tf_op jit(solution)/shard_map/ppermute | solution.py:175
  50.0 0.0 collective-permute-done.5.up_other
  50.0 0.0 collective-permute-done.6.down_other
  50.0 0.0 copy-done.1
  50.1 0.0 copy-start.2
  50.1 1.9 %copy-done.2 = bf16[256,6144]{1,0:T(8,128)(2,1)S(1)} copy-done((bf16[256,6144]{1,0:T(8,128)(2,1)S(1)}, bf16[256,6144]{1,0:T(8,128)(2,1)}, u32[]{:S(2)}) %copy-start.2) | copy-done | bytes 3145752
  51.9 0.8 copy-done.4
  52.7 5.6 %feed.1 = (f32[4,64,768]{2,1,0:T(8,128)S(1)}, bf16[4,64,768]{2,1,0:T(8,128)(2,1)S(1)}) custom-call(s32[8]{0:T(128)S(1)} %xor_bitcast_fusion.places, bf16[4,64,768]{2,1,0:T(8,128)(2,1)S(1)} %pad_maximum_fusion.first, bf16[4,64,768]{2,1,0:T(8,128)(2,1)} %collective-permute-done.4.second, bf16[6144,256]{1,0:T(8,128)(2,1)S(1)} %copy-done.1, ...), custom_call_target="tpu_custom_call" | custom-call | flops 805306368 | bytes 12582912 | tf_op jit(solution)/shard_map/feed/pallas_call | solution.py:141
  58.4 1.7 %collective-permute-start.7 = (bf16[4,64,768]{2,1,0:T(8,128)(2,1)S(1)}, bf16[4,64,768]{2,1,0:T(8,128)(2,1)S(1)}, u32[]{:S(2)}, u32[]{:S(2)}) collective-permute-start(bf16[4,64,768]{2,1,0:T(8,128)(2,1)S(1)} %get-tuple-element.12), channel_id=1, source_target_pairs={{0,2},{1,5},{2,0},{3,7},{4,6},{5,1},{6,4},{7,3},{8,10},{9,13},{10,... | collective-permute-start | bytes 1179656 | tf_op jit(solution)/shard_map/ppermute | solution.py:175
  60.0 7.0 %collective-permute-done.7 = bf16[4,64,768]{2,1,0:T(8,128)(2,1)S(1)} collective-permute-done((bf16[4,64,768]{2,1,0:T(8,128)(2,1)S(1)}, bf16[4,64,768]{2,1,0:T(8,128)(2,1)S(1)}, u32[]{:S(2)}, u32[]{:S(2)}) %collective-permute-start.7) | collective-permute-done | bytes 393248 | tf_op jit(solution)/shard_map/ppermute | solution.py:175
  67.0 0.1 convert_add_fusion
  67.2 0.1 collective-permute-start.8
  67.3 6.7 %collective-permute-done.8 = bf16[2,64,768]{2,1,0:T(8,128)(2,1)S(1)} collective-permute-done((bf16[2,64,768]{2,1,0:T(8,128)(2,1)S(1)}, bf16[2,64,768]{2,1,0:T(8,128)(2,1)S(1)}, u32[]{:S(2)}, u32[]{:S(2)}) %collective-permute-start.8) | collective-permute-done | bytes 196640 | tf_op jit(solution)/shard_map/ppermute | solution.py:175
  74.0 1.5 %collective-permute-start.9 = (bf16[1,64,768]{2,1,0:T(8,128)(2,1)S(1)}, bf16[1,64,768]{2,1,0:T(8,128)(2,1)S(1)}, u32[]{:S(2)}, u32[]{:S(2)}) collective-permute-start(bf16[1,64,768]{2,1,0:T(8,128)(2,1)S(1)} %slice.85), channel_id=1, source_target_pairs={{0,8},{1,9},{2,10},{3,11},{4,12},{5,13},{6,14},{7,15},{8,0},{9,1},... | collective-permute-start | bytes 294920 | tf_op jit(solution)/shard_map/ppermute | solution.py:175
  75.5 4.1 %collective-permute-done.9 = bf16[1,64,768]{2,1,0:T(8,128)(2,1)S(1)} collective-permute-done((bf16[1,64,768]{2,1,0:T(8,128)(2,1)S(1)}, bf16[1,64,768]{2,1,0:T(8,128)(2,1)S(1)}, u32[]{:S(2)}, u32[]{:S(2)}) %collective-permute-start.9) | collective-permute-done | bytes 98336 | tf_op jit(solution)/shard_map/ppermute | solution.py:175
  79.6 0.0 copy-done.6
  79.6 0.7 fusion.9
  (13 shorter events, 0.2 us)
Async XLA Ops:
  0.0 43.8 %copy-start = (s32[128,3]{0,1:T(4,128)S(1)}, s32[128,3]{0,1:T(4,128)}, u32[]{:S(2)}) copy-start(s32[128,3]{0,1:T(4,128)} %param.16) | copy-start | bytes 4612
  0.0 9.0 %copy-start.7 = (bf16[2,64,128]{2,1,0:T(8,128)(2,1)S(1)}, bf16[2,64,128]{2,1,0:T(8,128)(2,1)}, u32[]{:S(2)}) copy-start(bf16[2,64,128]{2,1,0:T(8,128)(2,1)} %param.11) | copy-start | bytes 98308
  0.0 9.1 %copy-start.5 = (bf16[64,768]{1,0:T(8,128)(2,1)S(1)}, bf16[64,768]{1,0:T(8,128)(2,1)}, u32[]{:S(2)}) copy-start(bf16[64,768]{1,0:T(8,128)(2,1)} %stream.1) | copy-start | bytes 294916
  0.0 50.0 %collective-permute-start.5 = (bf16[6144,256]{1,0:T(8,128)(2,1)}, bf16[6144,256]{1,0:T(8,128)(2,1)}, u32[]{:S(2)}, u32[]{:S(2)}) collective-permute-start(bf16[6144,256]{1,0:T(8,128)(2,1)} %up_own.1), channel_id=1, source_target_pairs={{0,1},{1,0},{2,3},{3,2},{4,5},{5,4},{6,7},{7,6},{8,9},{9,8},{10,11... | collective-permute-start | bytes 9437192 | tf_op jit(solution)/shard_map/ppermute | solution.py:189
  0.5 49.5 %collective-permute-start.6 = (bf16[256,6144]{1,0:T(8,128)(2,1)}, bf16[256,6144]{1,0:T(8,128)(2,1)}, u32[]{:S(2)}, u32[]{:S(2)}) collective-permute-start(bf16[256,6144]{1,0:T(8,128)(2,1)} %down_own.1), channel_id=1, source_target_pairs={{0,1},{1,0},{2,3},{3,2},{4,5},{5,4},{6,7},{7,6},{8,9},{9,8},{10,11... | collective-permute-start | bytes 9437192 | tf_op jit(solution)/shard_map/ppermute | solution.py:190
  5.2 3.9 %copy-start.3 = (bf16[128,6144]{1,0:T(8,128)(2,1)S(1)}, bf16[128,6144]{1,0:T(8,128)(2,1)}, u32[]{:S(2)}) copy-start(bf16[128,6144]{1,0:T(8,128)(2,1)} %weight.1) | copy-start | bytes 4718596
  9.1 40.9 %copy-start.1 = (bf16[6144,256]{1,0:T(8,128)(2,1)S(1)}, bf16[6144,256]{1,0:T(8,128)(2,1)}, u32[]{:S(2)}) copy-start(bf16[6144,256]{1,0:T(8,128)(2,1)} %up_own.1) | copy-start | bytes 9437188
  10.1 8.8 %collective-permute-start = (bf16[4,64,768]{2,1,0:T(8,128)(2,1)S(1)}, bf16[4,64,768]{2,1,0:T(8,128)(2,1)S(1)}, u32[]{:S(2)}, u32[]{:S(2)}) collective-permute-start(bf16[4,64,768]{2,1,0:T(8,128)(2,1)S(1)} %get-tuple-element.10), channel_id=1, source_target_pairs={{0,2},{1,5},{2,0},{3,7},{4,6},{5,1},{6,4},{7,3},{8,10},{9,13},{10,... | collective-permute-start | bytes 1179656 | tf_op jit(solution)/shard_map/ppermute | solution.py:175
  19.0 5.8 %collective-permute-start.1 = (bf16[2,64,768]{2,1,0:T(8,128)(2,1)S(1)}, bf16[2,64,768]{2,1,0:T(8,128)(2,1)S(1)}, u32[]{:S(2)}, u32[]{:S(2)}) collective-permute-start(bf16[2,64,768]{2,1,0:T(8,128)(2,1)S(1)} %slice.84), channel_id=1, source_target_pairs={{0,4},{1,3},{2,6},{3,1},{4,0},{5,7},{6,2},{7,5},{8,12},{9,11},{10,... | collective-permute-start | bytes 589832 | tf_op jit(solution)/shard_map/ppermute | solution.py:175
  24.8 10.7 %collective-permute-start.2 = (bf16[2,64,768]{2,1,0:T(8,128)(2,1)S(1)}, bf16[2,64,768]{2,1,0:T(8,128)(2,1)S(1)}, u32[]{:S(2)}, u32[]{:S(2)}) collective-permute-start(bf16[2,64,768]{2,1,0:T(8,128)(2,1)S(1)} %fusion.6), channel_id=1, source_target_pairs={{0,8},{1,9},{2,10},{3,11},{4,12},{5,13},{6,14},{7,15},{8,0},{9,1},... | collective-permute-start | bytes 589832 | tf_op jit(solution)/shard_map/ppermute | solution.py:175
  36.4 5.7 %collective-permute-start.3 = (bf16[2,64,768]{2,1,0:T(8,128)(2,1)S(1)}, bf16[2,64,768]{2,1,0:T(8,128)(2,1)S(1)}, u32[]{:S(2)}, u32[]{:S(2)}) collective-permute-start(bf16[2,64,768]{2,1,0:T(8,128)(2,1)S(1)} %get-tuple-element.13), channel_id=1, source_target_pairs={{0,4},{1,3},{2,6},{3,1},{4,0},{5,7},{6,2},{7,5},{8,12},{9,11},{10,... | collective-permute-start | bytes 589832 | tf_op jit(solution)/shard_map/ppermute | solution.py:175
  42.1 7.9 %collective-permute-start.4 = (bf16[4,64,768]{2,1,0:T(8,128)(2,1)S(1)}, bf16[4,64,768]{2,1,0:T(8,128)(2,1)}, u32[]{:S(2)}, u32[]{:S(2)}) collective-permute-start(bf16[4,64,768]{2,1,0:T(8,128)(2,1)S(1)} %pad_maximum_fusion.first), channel_id=1, source_target_pairs={{0,2},{1,5},{2,0},{3,7},{4,6},{5,1},{6,4},{7,3},{8,10},{9,13},{10,... | collective-permute-start | bytes 1179656 | tf_op jit(solution)/shard_map/ppermute | solution.py:175
  50.1 1.9 %copy-start.2 = (bf16[256,6144]{1,0:T(8,128)(2,1)S(1)}, bf16[256,6144]{1,0:T(8,128)(2,1)}, u32[]{:S(2)}) copy-start(bf16[256,6144]{1,0:T(8,128)(2,1)} %down_own.1) | copy-start | bytes 9437188
  51.9 0.8 copy-start.4
  58.3 21.3 %copy-start.6 = (f32[2,64,768]{2,1,0:T(8,128)S(1)}, f32[2,64,768]{2,1,0:T(8,128)}, u32[]{:S(2)}) copy-start(f32[2,64,768]{2,1,0:T(8,128)} %get-tuple-element.14) | copy-start | bytes 1179652
  58.4 8.7 %collective-permute-start.7 = (bf16[4,64,768]{2,1,0:T(8,128)(2,1)S(1)}, bf16[4,64,768]{2,1,0:T(8,128)(2,1)S(1)}, u32[]{:S(2)}, u32[]{:S(2)}) collective-permute-start(bf16[4,64,768]{2,1,0:T(8,128)(2,1)S(1)} %get-tuple-element.12), channel_id=1, source_target_pairs={{0,2},{1,5},{2,0},{3,7},{4,6},{5,1},{6,4},{7,3},{8,10},{9,13},{10,... | collective-permute-start | bytes 1179656 | tf_op jit(solution)/shard_map/ppermute | solution.py:175
  67.2 6.8 %collective-permute-start.8 = (bf16[2,64,768]{2,1,0:T(8,128)(2,1)S(1)}, bf16[2,64,768]{2,1,0:T(8,128)(2,1)S(1)}, u32[]{:S(2)}, u32[]{:S(2)}) collective-permute-start(bf16[2,64,768]{2,1,0:T(8,128)(2,1)S(1)} %slice.83), channel_id=1, source_target_pairs={{0,4},{1,3},{2,6},{3,1},{4,0},{5,7},{6,2},{7,5},{8,12},{9,11},{10,... | collective-permute-start | bytes 589832 | tf_op jit(solution)/shard_map/ppermute | solution.py:175
  74.0 5.6 %collective-permute-start.9 = (bf16[1,64,768]{2,1,0:T(8,128)(2,1)S(1)}, bf16[1,64,768]{2,1,0:T(8,128)(2,1)S(1)}, u32[]{:S(2)}, u32[]{:S(2)}) collective-permute-start(bf16[1,64,768]{2,1,0:T(8,128)(2,1)S(1)} %slice.85), channel_id=1, source_target_pairs={{0,8},{1,9},{2,10},{3,11},{4,12},{5,13},{6,14},{7,15},{8,0},{9,1},... | collective-permute-start | bytes 294920 | tf_op jit(solution)/shard_map/ppermute | solution.py:175

commit v2 on v0

v2 whole, which is shorter than its diff:
```python
import functools
import math

import jax
import jax.numpy as jnp
from jax import lax
from jax.experimental import pallas as pl
from jax.experimental.pallas import tpu as pltpu
from jax.sharding import PartitionSpec as P

HS = 128
BLOCK = 128
EPSILON = 1e-05
FOLDS = 2
ONES = 16
MIB = 1024 * 1024
F32 = jnp.float32
BF16 = jnp.bfloat16


def attend_rows(queries, fresh_kv, kv_cache, lengths):
    row_count, width = queries.shape
    heads_here = width // HS
    cache = kv_cache.shape[2]
    shaped_q = queries.reshape(row_count, heads_here, HS)
    cache_keys = kv_cache[0].reshape(row_count, cache, heads_here, HS)
    cache_values = kv_cache[1].reshape(row_count, cache, heads_here, HS)
    scale = 1.0 / math.sqrt(HS)
    scores = jnp.einsum("rhd,rphd->rhp", shaped_q, cache_keys, preferred_element_type=F32) * scale
    positions = jnp.arange(cache)
    visible = positions[None, None, :] < lengths[:, None, None]
    scores = jnp.where(visible, scores, -jnp.inf)
    own_score = (
        jnp.einsum(
            "rhd,rhd->rh",
            shaped_q,
            fresh_kv[0].reshape(row_count, heads_here, HS),
            preferred_element_type=F32,
        )
        * scale
    )
    top = jnp.maximum(jnp.max(scores, axis=2), own_score)
    weights = jnp.exp(scores - top[:, :, None])
    own_weight = jnp.exp(own_score - top)
    total = jnp.sum(weights, axis=2) + own_weight
    probs = (weights / total[:, :, None]).astype(BF16)
    own_prob = (own_weight / total).astype(BF16)
    result = jnp.einsum("rhp,rphd->rhd", probs, cache_values, preferred_element_type=F32)
    result = result + own_prob.astype(F32)[:, :, None] * fresh_kv[1].reshape(
        row_count, heads_here, HS
    ).astype(F32)
    return result.astype(BF16).reshape(row_count, width)


def spot(core, p, count):
    rounds = count.bit_length() - 1
    bits = [(p >> (rounds - 1 - j)) & 1 for j in range(rounds)]
    plain = sum(bit << j for j, bit in enumerate(bits))
    if rounds < 2:
        return plain
    turned = sum(bit << j for j, bit in enumerate([bits[1], bits[0]] + bits[2:]))
    if plain == turned:
        return plain
    return jnp.where(lax.rem(core, 2) == 0, plain, turned)


def span_of(p, fold, count, width):
    place = lax.bitwise_xor(lax.axis_index("tensor"), spot(lax.axis_index("request"), p, count))
    part = width // FOLDS
    return pl.ds(pl.multiple_of(place * width + fold * part, part), part)


def pick(array, axis, p, fold, count, width):
    place = lax.axis_index("tensor") ^ spot(lax.axis_index("request"), p, count)
    part = width // FOLDS
    return lax.dynamic_slice_in_dim(array, place * width + fold * part, part, axis)


def whole(count):
    return [pl.BlockSpec(memory_space=pltpu.VMEM)] * count


def attend_block(queries, fresh_key, fresh_value, keys, values, lengths, base):
    rows, positions = keys.shape[0], keys.shape[1]
    scale = 1.0 / math.sqrt(HS)
    row = lax.broadcasted_iota(jnp.int32, (rows, positions), 0)
    keys = keys.reshape(rows * positions, HS)
    wide = lax.dot_general(queries, keys, (((1,), (1,)), ((), ())), preferred_element_type=F32)
    scores = wide[:, :positions]
    length = jnp.full((rows, positions), lengths[base], jnp.int32)
    for r in range(1, rows):
        scores = jnp.where(row == r, wide[:, r * positions : (r + 1) * positions], scores)
        length = jnp.where(row == r, lengths[base + r], length)
    visible = lax.broadcasted_iota(jnp.int32, (rows, positions), 1) < length
    scores = jnp.where(visible, scores * scale, -jnp.inf)
    own_score = jnp.sum(queries.astype(F32) * fresh_key.astype(F32), axis=1, keepdims=True) * scale
    top = jnp.maximum(jnp.max(scores, axis=1, keepdims=True), own_score)
    weights = jnp.exp(scores - top)
    own_weight = jnp.exp(own_score - top)
    total = jnp.sum(weights, axis=1, keepdims=True) + own_weight
    probs = (weights / total).astype(BF16).astype(F32)
    own_prob = (own_weight / total).astype(BF16).astype(F32)
    spread = jnp.concatenate([jnp.where(row == r, probs, 0.0).astype(BF16) for r in range(rows)], axis=1)
    result = jnp.dot(spread, values.reshape(rows * positions, HS), preferred_element_type=F32)
    return (result + own_prob * fresh_value.astype(F32)).astype(BF16)


def head_kernel(count, step, *refs):
    sources, refs = refs[:7], refs[7:]
    sends, keeps, mask, refs = refs[:FOLDS], refs[FOLDS : 2 * FOLDS], refs[2 * FOLDS], refs[2 * FOLDS + 1 :]
    lengths, queries, fresh, stream, weight, named, cache, turned, sems = refs
    rows, width = stream.shape
    small = [
        pltpu.make_async_copy(source, target, sems.at[i])
        for i, (source, target) in enumerate(zip(sources[:6], (lengths, queries, fresh, stream, weight, named)))
    ]
    blocks = [
        pltpu.make_async_copy(
            sources[6].at[:, pl.ds(i * step, step)], cache.at[:, pl.ds(i * step, step)], sems.at[6 + i]
        )
        for i in range(rows // step)
    ]
    for copy in small[:3] + blocks + small[3:]:
        copy.start()
    for copy in small[:3]:
        copy.wait()
    parts = []
    for i, copy in enumerate(blocks):
        copy.wait()
        span = slice(i * step, (i + 1) * step)
        parts.append(
            attend_block(
                queries[span, :], fresh[0, span, :], fresh[1, span, :], cache[0, span], cache[1, span], lengths, i * step
            )
        )
    attended = jnp.concatenate(parts, axis=0)
    for copy in small[3:]:
        copy.wait()
    half, part = count // 2, width // FOLDS
    for first, outs in ((half, sends), (0, keeps)):
        for fold, out in enumerate(outs):
            for i in range(half):
                span = span_of(first + i, fold, count, width)
                piece = jnp.dot(attended, weight[:, span], preferred_element_type=F32)
                if first + i == 0:
                    piece = piece + stream[:, fold * part : (fold + 1) * part].astype(F32)
                out[i] = piece.astype(out.dtype)
    acts, batch = named.shape
    spare = turned.shape[1] - acts
    ids = named[...].astype(F32)
    if spare:
        ids = jnp.concatenate([ids, jnp.full((spare, batch), -1.0, F32)], axis=0)
    turned[...] = jnp.transpose(ids)
    core, cores = lax.axis_index("request"), lax.axis_size("request")
    own = turned[pl.ds(pl.multiple_of(core * rows, rows), rows), :]
    neurons = mask.shape[1] // 2
    lane = lax.broadcasted_iota(jnp.int32, (rows, neurons), 1) // BLOCK
    for start, place in ((0, core), (neurons, lax.bitwise_xor(core, 1))):
        owner = lax.axis_index("tensor") * cores + place
        blocks = (lane + owner * (neurons // BLOCK)).astype(F32)
        active = own[:, 0:1] == blocks
        for k in range(1, acts):
            active = active | (own[:, k : k + 1] == blocks)
        mask[:, start : start + neurons] = jnp.where(active, 1.0, 0.0)


def head(count, queries, fresh_kv, kv_cache, lengths, stream, weight, block_ids, neurons):
    rows, width = stream.shape
    positions = kv_cache.shape[2]
    half, part = count // 2, width // FOLDS
    step = 16
    if part % 128 or queries.shape[1] != HS or rows % step or positions % 128:
        attended = attend_rows(queries, fresh_kv, kv_cache, lengths)
        sends, keeps = [], []
        for fold in range(FOLDS):
            pieces = [
                jnp.dot(attended, pick(weight, 1, i, fold, count, width), preferred_element_type=F32)
                for i in range(count)
            ]
            pieces[0] = pieces[0] + stream[:, fold * part : (fold + 1) * part].astype(F32)
            keeps.append(jnp.stack(pieces[:half]))
            sends.append(jnp.stack(pieces[half:]).astype(BF16))
        core, cores = lax.axis_index("request"), lax.axis_size("request")
        local = jnp.arange(neurons, dtype=jnp.int32) // BLOCK
        base = lax.axis_index("tensor") * cores
        owners = jnp.concatenate([(base + place) * (neurons // BLOCK) + local for place in (core, core ^ 1)])
        named = lax.dynamic_slice_in_dim(block_ids, core * rows, rows, 0)
        mask = jnp.any(named[:, :, None] == owners[None, None, :], axis=1).astype(F32)
        return sends, keeps, mask
    shapes = [(half, rows, part)] * FOLDS
    operands = [
        pltpu.with_memory_space_constraint(array, pltpu.HBM)
        for array in (lengths, queries, fresh_kv, stream, weight, block_ids.T, kv_cache)
    ]
    batch, acts = block_ids.shape
    outs = pl.pallas_call(
        functools.partial(head_kernel, count, step),
        in_specs=[pl.BlockSpec(memory_space=pltpu.HBM)] * 7,
        out_specs=whole(2 * FOLDS + 1),
        out_shape=[jax.ShapeDtypeStruct(shape, kind) for kind in (BF16, F32) for shape in shapes]
        + [jax.ShapeDtypeStruct((rows, 2 * neurons), F32)],
        scratch_shapes=[
            pltpu.SMEM(lengths.shape, lengths.dtype),
            pltpu.VMEM(queries.shape, BF16),
            pltpu.VMEM(fresh_kv.shape, BF16),
            pltpu.VMEM(stream.shape, BF16),
            pltpu.VMEM(weight.shape, BF16),
            pltpu.VMEM((acts, batch), block_ids.dtype),
            pltpu.VMEM(kv_cache.shape, BF16),
            pltpu.VMEM((batch, -(-acts // 8) * 8), F32),
            pltpu.SemaphoreType.DMA((6 + rows // step,)),
        ],
        compiler_params=pltpu.CompilerParams(vmem_limit_bytes=16 * MIB),
        cost_estimate=pl.CostEstimate(
            flops=4 * rows * positions * HS + 2 * rows * weight.size,
            bytes_accessed=2 * (kv_cache.size + weight.size),
            transcendentals=rows * positions,
        ),
        name="head",
    )(*operands)
    return list(outs[:FOLDS]), list(outs[FOLDS : 2 * FOLDS]), outs[2 * FOLDS]


def up_kernel(first, folds, count, width, last, rows, *refs):
    pieces = refs[: len(folds)]
    up_own, up_other = refs[len(folds) : len(folds) + 2]
    refs = refs[len(folds) + 2 :]
    neurons = up_own.shape[1]
    extra = jnp.ones((ONES, width // FOLDS), BF16)
    total = squares = own = other = None
    for fold, ref in zip(folds, pieces):
        for i in range(ref.shape[0]):
            piece = ref[i]
            span = span_of(first + i, fold, count, width)
            wide = piece.astype(F32)
            add_total = jnp.sum(wide, axis=1, keepdims=True)
            add_squares = jnp.sum(wide * wide, axis=1, keepdims=True)
            stacked = jnp.concatenate([piece, extra], axis=0)
            add_own = jnp.dot(stacked, up_own[span, :], preferred_element_type=F32)
            add_other = jnp.dot(stacked, up_other[span, :], preferred_element_type=F32)
            if own is None:
                total, squares, own, other = add_total, add_squares, add_own, add_other
            else:
                total, squares = total + add_total, squares + add_squares
                own, other = own + add_own, other + add_other
    if first > 0:
        upward, sums = refs[:2]
        refs = refs[2:]
        own = own + upward[:, :neurons]
        other = other + upward[:, neurons:]
        total = total + sums[:, 0:1]
        squares = squares + sums[:, 1:2]
    if not last:
        upward, sums = refs
        upward[:, :neurons] = own
        upward[:, neurons:] = other
        lane = lax.broadcasted_iota(jnp.int32, (rows, 128), 1)
        sums[...] = jnp.where(lane == 0, total, squares)
        return
    mask, hidden = refs
    features = count * width
    center = total * (1.0 / features)
    spread = squares * (1.0 / features) - center * center
    scale = lax.rsqrt(spread + EPSILON)
    for start, value in ((0, own), (neurons, other)):
        upward = (value[:rows] - center * value[rows : rows + 1]) * scale
        active = mask[:, start : start + neurons] > 0
        hidden[:, start : start + neurons] = jnp.where(active, jnp.maximum(upward, 0.0), 0.0).astype(BF16)


def up(first, folds, count, width, pieces, ups, state, mask):
    amount, rows, part = pieces[0].shape
    neurons = ups[0].shape[1]
    if part % 128:
        for fold, piece in zip(folds, pieces):
            extra = jnp.ones((ONES, part), BF16)
            for i in range(amount):
                wide = piece[i].astype(F32)
                stacked = jnp.concatenate([piece[i], extra], axis=0)
                add = jnp.concatenate(
                    [
                        jnp.dot(
                            stacked,
                            pick(weight, 0, first + i, fold, count, width),
                            preferred_element_type=F32,
                        )
                        for weight in ups
                    ],
                    axis=1,
                )
                sums = jnp.stack([jnp.sum(wide, axis=1), jnp.sum(wide * wide, axis=1)], axis=1)
                state = (add, sums) if state is None else (state[0] + add, state[1] + sums)
        if mask is None:
            return state
        upward, sums = state
        features = count * width
        center = sums[:, 0:1] / features
        scale = lax.rsqrt(sums[:, 1:2] / features - center * center + EPSILON)
        upward = (upward[:rows] - center * upward[rows : rows + 1]) * scale
        return jnp.where(mask > 0, jax.nn.relu(upward), 0.0).astype(BF16)
    last = mask is not None
    operands = list(pieces) + list(ups) + ([] if state is None else list(state)) + ([mask] if last else [])
    if last:
        out_shape = jax.ShapeDtypeStruct((rows, 2 * neurons), BF16)
    else:
        out_shape = [
            jax.ShapeDtypeStruct((rows + ONES, 2 * neurons), F32),
            jax.ShapeDtypeStruct((rows, 128), F32),
        ]
    return pl.pallas_call(
        functools.partial(up_kernel, first, folds, count, width, last, rows),
        in_specs=whole(len(operands)),
        out_specs=whole(1)[0] if last else whole(2),
        out_shape=out_shape,
        compiler_params=pltpu.CompilerParams(vmem_limit_bytes=12 * MIB),
        cost_estimate=pl.CostEstimate(
            flops=4 * rows * neurons * amount * part * len(folds),
            bytes_accessed=4 * neurons * amount * part * len(folds),
            transcendentals=0,
        ),
        name="up",
    )(*operands)


def down_kernel(first, folds, count, width, hidden, down_own, down_other, *outs):
    neurons = down_own.shape[0]
    own, other = hidden[:, :neurons], hidden[:, neurons:]
    for fold, out in zip(folds, outs):
        for i in range(out.shape[0]):
            span = span_of(first + i, fold, count, width)
            piece = jnp.dot(own, down_own[:, span], preferred_element_type=F32)
            piece += jnp.dot(other, down_other[:, span], preferred_element_type=F32)
            out[i] = piece.astype(out.dtype)


def down(first, amount, folds, kind, count, width, hidden, downs):
    rows = hidden.shape[0]
    part = width // FOLDS
    if part % 128:
        both = jnp.concatenate(downs, axis=0)
        return [
            jnp.stack(
                [
                    jnp.dot(hidden, pick(both, 1, first + i, fold, count, width), preferred_element_type=F32)
                    for i in range(amount)
                ]
            ).astype(kind)
            for fold in folds
        ]
    return pl.pallas_call(
        functools.partial(down_kernel, first, folds, count, width),
        in_specs=whole(3),
        out_specs=whole(len(folds)),
        out_shape=[jax.ShapeDtypeStruct((amount, rows, part), kind) for _ in folds],
        compiler_params=pltpu.CompilerParams(vmem_limit_bytes=12 * MIB),
        cost_estimate=pl.CostEstimate(
            flops=2 * rows * hidden.shape[1] * amount * part * len(folds),
            bytes_accessed=2 * hidden.shape[1] * amount * part * len(folds),
            transcendentals=0,
        ),
        name="down",
    )(hidden, *downs)


def per_device(
    queries, fresh_kv, kv_cache, lengths, stream, out_weight, block_ids, up_weight, down_weight
):
    count = lax.axis_size("tensor")
    cores = lax.axis_size("request")
    rounds = count.bit_length() - 1
    half = count // 2
    width = stream.shape[1]
    orders = [list(range(rounds)) for _ in range(cores)]
    for c in range(cores):
        if c % 2 and rounds > 1:
            orders[c][0], orders[c][1] = orders[c][1], orders[c][0]

    def swap(array, step):
        pairs = [
            (t * cores + c, (t ^ (1 << orders[c][step])) * cores + c)
            for t in range(count)
            for c in range(cores)
        ]
        return lax.ppermute(array, ("tensor", "request"), pairs)

    across = [(c, c ^ 1) for c in range(cores)]
    ups = (up_weight, lax.ppermute(up_weight, "request", across))
    downs = (down_weight, lax.ppermute(down_weight, "request", across))
    folds = tuple(range(FOLDS))
    sends, keeps, mask = head(
        count, queries, fresh_kv, kv_cache, lengths, stream, out_weight, block_ids, up_weight.shape[1]
    )
    for step in range(rounds - 1):
        for fold in folds:
            total = keeps[fold] + swap(sends[fold], step).astype(F32)
            left = total.shape[0] // 2
            if step < rounds - 2:
                keeps[fold], sends[fold] = total[:left], total[left:].astype(BF16)
            else:
                keeps[fold], sends[fold] = total, total.astype(BF16)
    shares, parts = [], []
    for fold in folds:
        mixed = keeps[fold] + swap(sends[fold], rounds - 1)[::-1].astype(F32)
        shares.append(mixed[0])
        parts.append(mixed.astype(BF16))
    for step in range(rounds - 2, 0, -1):
        for fold in folds:
            parts[fold] = jnp.concatenate([parts[fold], swap(parts[fold], step)])
    state = up(0, folds, count, width, parts, ups, None, None)
    for fold in folds:
        got = swap(parts[fold], 0)
        state = up(half, (fold,), count, width, [got], ups, state, mask if fold == FOLDS - 1 else None)
    hidden = state
    sends = [down(half, half, (fold,), BF16, count, width, hidden, downs)[0] for fold in folds]
    keeps = list(down(0, half, folds, F32, count, width, hidden, downs))
    for step in range(rounds):
        for fold in folds:
            total = keeps[fold] + swap(sends[fold], step).astype(F32)
            left = total.shape[0] // 2
            keeps[fold] = total[: max(left, 1)]
            if left:
                sends[fold] = total[left:].astype(BF16)
    outs = [(shares[fold] + keeps[fold][0]).astype(BF16) for fold in folds]
    return jnp.concatenate(outs, axis=1)


def solution(mesh):
    in_specs = (
        P(("groups", "request"), "tensor"),
        P(None, ("groups", "request"), "tensor"),
        P(None, ("groups", "request"), None, "tensor"),
        P(("groups", "request")),
        P(("groups", "request"), "tensor"),
        P("tensor", None),
        P("groups", None),
        P(None, ("tensor", "request")),
        P(("tensor", "request"), None),
    )
    out_specs = P(("groups", "request"), "tensor")
    return jax.shard_map(
        per_device, mesh=mesh, in_specs=in_specs, out_specs=out_specs, check_vma=False
    )
```

time: 213 us -> 62.8 us (0.29)
  waiting for transfers between devices: 168 us -> 26.3 us
  starting transfers between devices: 0.12 us -> 26.6 us
  matrix products: 14.1 us -> 0 us
  between operations: 13.2 us -> 0.17 us
  local copies, waits for them, and re-layouts: 10.3 us -> 1.47 us
  Pallas kernels: 0 us -> 7.08 us
  other arithmetic: 6.8 us -> 1.08 us
    psum x1 -> x0, waiting for transfers between devices: 91.8 us -> none  [per_device(): mixed_full = lax.psum(partial_value + placed, 'tensor')]
    reduce_scatter x1 -> x0, waiting for transfers between devices: 67.6 us -> none  [per_device(): lax.psum_scatter(picked.reshape(own_rows * lax.axis_size(('tensor', 'requ...]
    ppermute x0 -> x18, starting transfers between devices: none -> 26.6 us  [the longest x16 26.1 us: swap(): return lax.ppermute(array, ('tensor', 'request'), pairs)]
    ppermute x0 -> x18, waiting for transfers between devices: none -> 26.3 us  [the longest x16 26.3 us: swap(): return lax.ppermute(array, ('tensor', 'request'), pairs)]
    dot_general x4 -> x0, matrix products: 14.1 us -> none  [the longest x1 5.9 us: per_device(): jnp.dot(hidden, down_weight, preferred_element_type=jnp.float32)]
    all_gather x1 -> x0, waiting for transfers between devices: 9.04 us -> none  [per_device(): normed_all = lax.all_gather(normed, 'request', axis=0, tiled=True)]
    pallas_call x0 -> x7, Pallas kernels: none -> 7.08 us  [the longest x1 4.05 us: head(): pl.pallas_call(functools.partial(head_kernel, count, step), in_specs=[pl....]
    gather x1 -> x0, local copies, waits for them, and re-layouts: 4.3 us -> none  [per_device(): blocked[group_ids % request_count, :, group_ids // request_count, :]]
  transfers between devices with their start and end apart: 3 -> 18, of which waited for: 3 -> 14; matrix products, arithmetic and copies ran while one was open for 0% -> 1% of each run, Pallas kernels for 0% -> 11%
where the time goes in v2:
time: 62.8 us; the launch traced here: 62.7 us
  starting transfers between devices  26.6 us (42%)
  waiting for transfers between devices  26.3 us (42%)
  Pallas kernels  7.08 us (11%)
  local copies, waits for them, and re-layouts  1.47 us (2%)
  other arithmetic  1.08 us (2%)
    ppermute x16, waiting for transfers between devices, swap(): return lax.ppermute(array, ('tensor', 'request'), pairs)  26.3 us
    ppermute x16, starting transfers between devices, swap(): return lax.ppermute(array, ('tensor', 'request'), pairs)  26.1 us
    pallas_call x1, Pallas kernels, head(): pl.pallas_call(functools.partial(head_kernel, count, step), in_specs=[pl....  4.05 us
    pallas_call x3, Pallas kernels, up(): pl.pallas_call(functools.partial(up_kernel, first, folds, count, width, l...  1.64 us
    unnamed x4, local copies, waits for them, and re-layouts  1.4 us
    pallas_call x3, Pallas kernels, down(): pl.pallas_call(functools.partial(down_kernel, first, folds, count, width)...  1.39 us
  transfers between devices with their start and end apart: 18, of which 14 were waited for; matrix products, arithmetic and copies ran while one was open for 1% of the time, Pallas kernels for 11%

profile of v2, /device:TPU:0, one launch (start us, length us, event | category | flops | bytes accessed | tf_op | source)
XLA Modules:
  0.0 62.7 jit_solution(12430133597054351690)
XLA Ops:
  0.0 0.5 collective-permute-start.8
  0.5 0.1 collective-permute-start.11
  0.5 4.1 %head.1 = (bf16[4,64,384]{2,1,0:T(8,128)(2,1)S(1)}, bf16[4,64,384]{2,1,0:T(8,128)(2,1)S(1)}, f32[4,64,384]{2,1,0:T(8,128)S(1)}, f32[4,64,384]{2,1,0:T(8,128)S(1)}, f32[64,512]{1,0:T(8,128)S(1)}) custom-call(s32[64]{0:T(128)} %refs_0_.1, bf16[64,128]{1,0:T(8,128)(2,1)} %refs_1_.3, bf16[2,64,128]{2,1,0:T(8,128)(2,1)} %refs_2_.2, bf16[64,768]{1,0:T(8,128)(2,1)} %refs_3_.1, ...), custom_call_target="tpu_custom_call" | custom-call | flops 104857600 | bytes 5767168 | tf_op jit(solution)/shard_map/head/pallas_call | solution.py:196
  4.6 0.0 copy-start.1
  4.6 3.0 %collective-permute-start = (bf16[4,64,384]{2,1,0:T(8,128)(2,1)S(1)}, bf16[4,64,384]{2,1,0:T(8,128)(2,1)S(1)}, u32[]{:S(2)}, u32[]{:S(2)}) collective-permute-start(bf16[4,64,384]{2,1,0:T(8,128)(2,1)S(1)} %get-tuple-element.17), channel_id=1, source_target_pairs={{0,2},{1,5},{2,0},{3,7},{4,6},{5,1},{6,4},{7,3},{8,10},{9,13},{10,... | collective-permute-start | bytes 589832 | tf_op jit(solution)/shard_map/ppermute | solution.py:384
  7.6 0.1 collective-permute-start.3
  7.7 3.6 %collective-permute-done = bf16[4,64,384]{2,1,0:T(8,128)(2,1)S(1)} collective-permute-done((bf16[4,64,384]{2,1,0:T(8,128)(2,1)S(1)}, bf16[4,64,384]{2,1,0:T(8,128)(2,1)S(1)}, u32[]{:S(2)}, u32[]{:S(2)}) %collective-permute-start) | collective-permute-done | bytes 196640 | tf_op jit(solution)/shard_map/ppermute | solution.py:384
  11.3 2.1 %collective-permute-start.1 = (bf16[2,64,384]{2,1,0:T(8,128)(2,1)S(1)}, bf16[2,64,384]{2,1,0:T(8,128)(2,1)S(1)}, u32[]{:S(2)}, u32[]{:S(2)}) collective-permute-start(bf16[2,64,384]{2,1,0:T(8,128)(2,1)S(1)} %slice.117), channel_id=1, source_target_pairs={{0,4},{1,3},{2,6},{3,1},{4,0},{5,7},{6,2},{7,5},{8,12},{9,11},{10,... | collective-permute-start | bytes 294920 | tf_op jit(solution)/shard_map/ppermute | solution.py:384
  13.5 0.0 collective-permute-done.3
  13.6 2.2 %collective-permute-start.4 = (bf16[2,64,384]{2,1,0:T(8,128)(2,1)S(1)}, bf16[2,64,384]{2,1,0:T(8,128)(2,1)S(1)}, u32[]{:S(2)}, u32[]{:S(2)}) collective-permute-start(bf16[2,64,384]{2,1,0:T(8,128)(2,1)S(1)} %slice.116), channel_id=1, source_target_pairs={{0,4},{1,3},{2,6},{3,1},{4,0},{5,7},{6,2},{7,5},{8,12},{9,11},{10,... | collective-permute-start | bytes 294920 | tf_op jit(solution)/shard_map/ppermute | solution.py:384
  15.8 0.3 collective-permute-done.1
  16.1 3.1 %collective-permute-start.2 = (bf16[2,64,384]{2,1,0:T(8,128)(2,1)S(1)}, bf16[2,64,384]{2,1,0:T(8,128)(2,1)S(1)}, u32[]{:S(2)}, u32[]{:S(2)}) collective-permute-start(bf16[2,64,384]{2,1,0:T(8,128)(2,1)S(1)} %fusion), channel_id=1, source_target_pairs={{0,8},{1,9},{2,10},{3,11},{4,12},{5,13},{6,14},{7,15},{8,0},{9,1},... | collective-permute-start | bytes 294920 | tf_op jit(solution)/shard_map/ppermute | solution.py:384
  19.2 0.0 collective-permute-done.4
  19.2 2.9 %collective-permute-start.5 = (bf16[2,64,384]{2,1,0:T(8,128)(2,1)S(1)}, bf16[2,64,384]{2,1,0:T(8,128)(2,1)S(1)}, u32[]{:S(2)}, u32[]{:S(2)}) collective-permute-start(bf16[2,64,384]{2,1,0:T(8,128)(2,1)S(1)} %fusion.1), channel_id=1, source_target_pairs={{0,8},{1,9},{2,10},{3,11},{4,12},{5,13},{6,14},{7,15},{8,0},{9,1},... | collective-permute-start | bytes 294920 | tf_op jit(solution)/shard_map/ppermute | solution.py:384
  22.1 4.1 %collective-permute-done.2 = bf16[2,64,384]{2,1,0:T(8,128)(2,1)S(1)} collective-permute-done((bf16[2,64,384]{2,1,0:T(8,128)(2,1)S(1)}, bf16[2,64,384]{2,1,0:T(8,128)(2,1)S(1)}, u32[]{:S(2)}, u32[]{:S(2)}) %collective-permute-start.2) | collective-permute-done | bytes 98336 | tf_op jit(solution)/shard_map/ppermute | solution.py:384
  26.3 0.1 collective-permute-start.9
  26.3 0.9 %collective-permute-done.5 = bf16[2,64,384]{2,1,0:T(8,128)(2,1)S(1)} collective-permute-done((bf16[2,64,384]{2,1,0:T(8,128)(2,1)S(1)}, bf16[2,64,384]{2,1,0:T(8,128)(2,1)S(1)}, u32[]{:S(2)}, u32[]{:S(2)}) %collective-permute-start.5) | collective-permute-done | bytes 98336 | tf_op jit(solution)/shard_map/ppermute | solution.py:384
  27.3 1.2 %collective-permute-start.6 = (bf16[2,64,384]{2,1,0:T(8,128)(2,1)S(1)}, bf16[2,64,384]{2,1,0:T(8,128)(2,1)S(1)}, u32[]{:S(2)}, u32[]{:S(2)}) collective-permute-start(bf16[2,64,384]{2,1,0:T(8,128)(2,1)S(1)} %get-tuple-element.29), channel_id=1, source_target_pairs={{0,4},{1,3},{2,6},{3,1},{4,0},{5,7},{6,2},{7,5},{8,12},{9,11},{10,... | collective-permute-start | bytes 294920 | tf_op jit(solution)/shard_map/ppermute | solution.py:384
  28.5 3.2 %collective-permute-done.9 = bf16[2,64,384]{2,1,0:T(8,128)(2,1)S(1)} collective-permute-done((bf16[2,64,384]{2,1,0:T(8,128)(2,1)S(1)}, bf16[2,64,384]{2,1,0:T(8,128)(2,1)S(1)}, u32[]{:S(2)}, u32[]{:S(2)}) %collective-permute-start.9) | collective-permute-done | bytes 98336 | tf_op jit(solution)/shard_map/ppermute | solution.py:384
  31.7 1.8 %collective-permute-start.10 = (bf16[4,64,384]{2,1,0:T(8,128)(2,1)S(1)}, bf16[4,64,384]{2,1,0:T(8,128)(2,1)S(1)}, u32[]{:S(2)}, u32[]{:S(2)}) collective-permute-start(bf16[4,64,384]{2,1,0:T(8,128)(2,1)S(1)} %pad_maximum_fusion.1.refs_0_), channel_id=1, source_target_pairs={{0,2},{1,5},{2,0},{3,7},{4,6},{5,1},{6,4},{7,3},{8,10},{9,13},{10,... | collective-permute-start | bytes 589832 | tf_op jit(solution)/shard_map/ppermute | solution.py:384
  33.5 0.2 collective-permute-done.6
  33.8 1.8 %collective-permute-start.7 = (bf16[4,64,384]{2,1,0:T(8,128)(2,1)S(1)}, bf16[4,64,384]{2,1,0:T(8,128)(2,1)S(1)}, u32[]{:S(2)}, u32[]{:S(2)}) collective-permute-start(bf16[4,64,384]{2,1,0:T(8,128)(2,1)S(1)} %pad_maximum_fusion.refs_1_), channel_id=1, source_target_pairs={{0,2},{1,5},{2,0},{3,7},{4,6},{5,1},{6,4},{7,3},{8,10},{9,13},{10,... | collective-permute-start | bytes 589832 | tf_op jit(solution)/shard_map/ppermute | solution.py:384
  35.6 0.0 collective-permute-done.8.refs_3_.refs_2_
  35.6 0.0 copy-done.1
  35.6 0.7 %up.3 = (f32[80,512]{1,0:T(8,128)S(1)}, f32[64,128]{1,0:T(8,128)S(1)}) custom-call(bf16[4,64,384]{2,1,0:T(8,128)(2,1)S(1)} %pad_maximum_fusion.1.refs_0_, bf16[4,64,384]{2,1,0:T(8,128)(2,1)S(1)} %pad_maximum_fusion.refs_1_, bf16[6144,256]{1,0:T(8,128)(2,1)S(1)} %copy-done.1, bf16[6144,256]{1,0:T(8,128)(2,1)S(1)} %collective-permute-done.8.refs_3_.refs_2_), custom_call_target="tpu_custom_call" | custom-call | flops 201326592 | bytes 3145728 | tf_op jit(solution)/shard_map/up/pallas_call | solution.py:310
  36.4 1.1 %collective-permute-done.10.refs_0_ = bf16[4,64,384]{2,1,0:T(8,128)(2,1)S(1)} collective-permute-done((bf16[4,64,384]{2,1,0:T(8,128)(2,1)S(1)}, bf16[4,64,384]{2,1,0:T(8,128)(2,1)S(1)}, u32[]{:S(2)}, u32[]{:S(2)}) %collective-permute-start.10) | collective-permute-done | bytes 196640 | tf_op jit(solution)/shard_map/ppermute | solution.py:384
  37.4 0.4 up.4
  37.9 1.7 %collective-permute-done.7.refs_0_ = bf16[4,64,384]{2,1,0:T(8,128)(2,1)S(1)} collective-permute-done((bf16[4,64,384]{2,1,0:T(8,128)(2,1)S(1)}, bf16[4,64,384]{2,1,0:T(8,128)(2,1)S(1)}, u32[]{:S(2)}, u32[]{:S(2)}) %collective-permute-start.7) | collective-permute-done | bytes 196640 | tf_op jit(solution)/shard_map/ppermute | solution.py:384
  39.5 0.0 copy-start
  39.5 0.5 up.5.hidden
  40.0 0.0 collective-permute-done.11.down_other
  40.0 1.4 %copy-done = bf16[256,6144]{1,0:T(8,128)(2,1)S(1)} copy-done((bf16[256,6144]{1,0:T(8,128)(2,1)S(1)}, bf16[256,6144]{1,0:T(8,128)(2,1)}, u32[]{:S(2)}) %copy-start) | copy-done | bytes 3145752
  41.4 0.4 down.4
  41.8 1.8 %collective-permute-start.12 = (bf16[4,64,384]{2,1,0:T(8,128)(2,1)S(1)}, bf16[4,64,384]{2,1,0:T(8,128)(2,1)S(1)}, u32[]{:S(2)}, u32[]{:S(2)}) collective-permute-start(bf16[4,64,384]{2,1,0:T(8,128)(2,1)S(1)} %down.4), channel_id=1, source_target_pairs={{0,2},{1,5},{2,0},{3,7},{4,6},{5,1},{6,4},{7,3},{8,10},{9,13},{10,... | collective-permute-start | bytes 589832 | tf_op jit(solution)/shard_map/ppermute | solution.py:384
  43.6 0.4 down.5
  44.0 0.3 collective-permute-start.15
  44.4 0.6 %down.3 = (f32[4,64,384]{2,1,0:T(8,128)S(1)}, f32[4,64,384]{2,1,0:T(8,128)S(1)}) custom-call(bf16[64,512]{1,0:T(8,128)(2,1)S(1)} %up.5.hidden, bf16[256,6144]{1,0:T(8,128)(2,1)S(1)} %copy-done, bf16[256,6144]{1,0:T(8,128)(2,1)S(1)} %collective-permute-done.11.down_other), custom_call_target="tpu_custom_call" | custom-call | flops 201326592 | bytes 3145728 | tf_op jit(solution)/shard_map/down/pallas_call | solution.py:350
  45.0 3.9 %collective-permute-done.12 = bf16[4,64,384]{2,1,0:T(8,128)(2,1)S(1)} collective-permute-done((bf16[4,64,384]{2,1,0:T(8,128)(2,1)S(1)}, bf16[4,64,384]{2,1,0:T(8,128)(2,1)S(1)}, u32[]{:S(2)}, u32[]{:S(2)}) %collective-permute-start.12) | collective-permute-done | bytes 196640 | tf_op jit(solution)/shard_map/ppermute | solution.py:384
  48.9 0.9 %collective-permute-start.13 = (bf16[2,64,384]{2,1,0:T(8,128)(2,1)S(1)}, bf16[2,64,384]{2,1,0:T(8,128)(2,1)S(1)}, u32[]{:S(2)}, u32[]{:S(2)}) collective-permute-start(bf16[2,64,384]{2,1,0:T(8,128)(2,1)S(1)} %slice.115), channel_id=1, source_target_pairs={{0,4},{1,3},{2,6},{3,1},{4,0},{5,7},{6,2},{7,5},{8,12},{9,11},{10,... | collective-permute-start | bytes 294920 | tf_op jit(solution)/shard_map/ppermute | solution.py:384
  49.8 2.0 %collective-permute-done.15 = bf16[4,64,384]{2,1,0:T(8,128)(2,1)S(1)} collective-permute-done((bf16[4,64,384]{2,1,0:T(8,128)(2,1)S(1)}, bf16[4,64,384]{2,1,0:T(8,128)(2,1)S(1)}, u32[]{:S(2)}, u32[]{:S(2)}) %collective-permute-start.15) | collective-permute-done | bytes 196640 | tf_op jit(solution)/shard_map/ppermute | solution.py:384
  51.8 0.5 collective-permute-start.16
  52.3 1.4 %collective-permute-done.13 = bf16[2,64,384]{2,1,0:T(8,128)(2,1)S(1)} collective-permute-done((bf16[2,64,384]{2,1,0:T(8,128)(2,1)S(1)}, bf16[2,64,384]{2,1,0:T(8,128)(2,1)S(1)}, u32[]{:S(2)}, u32[]{:S(2)}) %collective-permute-start.13) | collective-permute-done | bytes 98336 | tf_op jit(solution)/shard_map/ppermute | solution.py:384
  53.8 2.5 %collective-permute-start.14 = (bf16[1,64,384]{2,1,0:T(8,128)(2,1)S(1)}, bf16[1,64,384]{2,1,0:T(8,128)(2,1)S(1)}, u32[]{:S(2)}, u32[]{:S(2)}) collective-permute-start(bf16[1,64,384]{2,1,0:T(8,128)(2,1)S(1)} %slice.119), channel_id=1, source_target_pairs={{0,8},{1,9},{2,10},{3,11},{4,12},{5,13},{6,14},{7,15},{8,0},{9,1},... | collective-permute-start | bytes 147464 | tf_op jit(solution)/shard_map/ppermute | solution.py:384
  56.3 0.2 collective-permute-done.16
  56.6 1.8 %collective-permute-start.17 = (bf16[1,64,384]{2,1,0:T(8,128)(2,1)S(1)}, bf16[1,64,384]{2,1,0:T(8,128)(2,1)S(1)}, u32[]{:S(2)}, u32[]{:S(2)}) collective-permute-start(bf16[1,64,384]{2,1,0:T(8,128)(2,1)S(1)} %slice.118), channel_id=1, source_target_pairs={{0,8},{1,9},{2,10},{3,11},{4,12},{5,13},{6,14},{7,15},{8,0},{9,1},... | collective-permute-start | bytes 147464 | tf_op jit(solution)/shard_map/ppermute | solution.py:384
  58.3 1.0 %collective-permute-done.14 = bf16[1,64,384]{2,1,0:T(8,128)(2,1)S(1)} collective-permute-done((bf16[1,64,384]{2,1,0:T(8,128)(2,1)S(1)}, bf16[1,64,384]{2,1,0:T(8,128)(2,1)S(1)}, u32[]{:S(2)}, u32[]{:S(2)}) %collective-permute-start.14) | collective-permute-done | bytes 49184 | tf_op jit(solution)/shard_map/ppermute | solution.py:384
  59.4 2.6 %collective-permute-done.17 = bf16[1,64,384]{2,1,0:T(8,128)(2,1)S(1)} collective-permute-done((bf16[1,64,384]{2,1,0:T(8,128)(2,1)S(1)}, bf16[1,64,384]{2,1,0:T(8,128)(2,1)S(1)}, u32[]{:S(2)}, u32[]{:S(2)}) %collective-permute-start.17) | collective-permute-done | bytes 49184 | tf_op jit(solution)/shard_map/ppermute | solution.py:384
  62.0 0.7 %pad_maximum_fusion.2 = bf16[64,768]{1,0:T(8,128)(2,1)} fusion(bf16[64,384]{1,0:T(8,128)(2,1)S(1)} %fusion.7, bf16[64,384]{1,0:T(8,128)(2,1)S(1)} %fusion.6), kind=kLoop, calls=%fused_computation.26 | loop fusion | flops 196608 | bytes 196608 | tf_op jit(solution)/shard_map/concatenate | solution.py:424
  (20 shorter events, 0.5 us)
Async XLA Ops:
  0.0 35.6 %collective-permute-start.8 = (bf16[6144,256]{1,0:T(8,128)(2,1)}, bf16[6144,256]{1,0:T(8,128)(2,1)S(1)}, u32[]{:S(2)}, u32[]{:S(2)}) collective-permute-start(bf16[6144,256]{1,0:T(8,128)(2,1)} %refs_1_.5), channel_id=1, source_target_pairs={{0,1},{1,0},{2,3},{3,2},{4,5},{5,4},{6,7},{7,6},{8,9},{9,8},{10,11... | collective-permute-start | bytes 9437192 | tf_op jit(solution)/shard_map/ppermute | solution.py:387
  0.5 39.6 %collective-permute-start.11 = (bf16[256,6144]{1,0:T(8,128)(2,1)}, bf16[256,6144]{1,0:T(8,128)(2,1)S(1)}, u32[]{:S(2)}, u32[]{:S(2)}) collective-permute-start(bf16[256,6144]{1,0:T(8,128)(2,1)} %down_own.5), channel_id=1, source_target_pairs={{0,1},{1,0},{2,3},{3,2},{4,5},{5,4},{6,7},{7,6},{8,9},{9,8},{10,11... | collective-permute-start | bytes 9437192 | tf_op jit(solution)/shard_map/ppermute | solution.py:388
  4.6 31.1 %copy-start.1 = (bf16[6144,256]{1,0:T(8,128)(2,1)S(1)}, bf16[6144,256]{1,0:T(8,128)(2,1)}, u32[]{:S(2)}) copy-start(bf16[6144,256]{1,0:T(8,128)(2,1)} %refs_1_.5) | copy-start | bytes 9437188
  4.6 6.7 %collective-permute-start = (bf16[4,64,384]{2,1,0:T(8,128)(2,1)S(1)}, bf16[4,64,384]{2,1,0:T(8,128)(2,1)S(1)}, u32[]{:S(2)}, u32[]{:S(2)}) collective-permute-start(bf16[4,64,384]{2,1,0:T(8,128)(2,1)S(1)} %get-tuple-element.17), channel_id=1, source_target_pairs={{0,2},{1,5},{2,0},{3,7},{4,6},{5,1},{6,4},{7,3},{8,10},{9,13},{10,... | collective-permute-start | bytes 589832 | tf_op jit(solution)/shard_map/ppermute | solution.py:384
  7.6 5.9 %collective-permute-start.3 = (bf16[4,64,384]{2,1,0:T(8,128)(2,1)S(1)}, bf16[4,64,384]{2,1,0:T(8,128)(2,1)S(1)}, u32[]{:S(2)}, u32[]{:S(2)}) collective-permute-start(bf16[4,64,384]{2,1,0:T(8,128)(2,1)S(1)} %get-tuple-element.19), channel_id=1, source_target_pairs={{0,2},{1,5},{2,0},{3,7},{4,6},{5,1},{6,4},{7,3},{8,10},{9,13},{10,... | collective-permute-start | bytes 589832 | tf_op jit(solution)/shard_map/ppermute | solution.py:384
  11.3 4.7 %collective-permute-start.1 = (bf16[2,64,384]{2,1,0:T(8,128)(2,1)S(1)}, bf16[2,64,384]{2,1,0:T(8,128)(2,1)S(1)}, u32[]{:S(2)}, u32[]{:S(2)}) collective-permute-start(bf16[2,64,384]{2,1,0:T(8,128)(2,1)S(1)} %slice.117), channel_id=1, source_target_pairs={{0,4},{1,3},{2,6},{3,1},{4,0},{5,7},{6,2},{7,5},{8,12},{9,11},{10,... | collective-permute-start | bytes 294920 | tf_op jit(solution)/shard_map/ppermute | solution.py:384
  13.6 5.7 %collective-permute-start.4 = (bf16[2,64,384]{2,1,0:T(8,128)(2,1)S(1)}, bf16[2,64,384]{2,1,0:T(8,128)(2,1)S(1)}, u32[]{:S(2)}, u32[]{:S(2)}) collective-permute-start(bf16[2,64,384]{2,1,0:T(8,128)(2,1)S(1)} %slice.116), channel_id=1, source_target_pairs={{0,4},{1,3},{2,6},{3,1},{4,0},{5,7},{6,2},{7,5},{8,12},{9,11},{10,... | collective-permute-start | bytes 294920 | tf_op jit(solution)/shard_map/ppermute | solution.py:384
  16.1 10.1 %collective-permute-start.2 = (bf16[2,64,384]{2,1,0:T(8,128)(2,1)S(1)}, bf16[2,64,384]{2,1,0:T(8,128)(2,1)S(1)}, u32[]{:S(2)}, u32[]{:S(2)}) collective-permute-start(bf16[2,64,384]{2,1,0:T(8,128)(2,1)S(1)} %fusion), channel_id=1, source_target_pairs={{0,8},{1,9},{2,10},{3,11},{4,12},{5,13},{6,14},{7,15},{8,0},{9,1},... | collective-permute-start | bytes 294920 | tf_op jit(solution)/shard_map/ppermute | solution.py:384
  19.2 8.0 %collective-permute-start.5 = (bf16[2,64,384]{2,1,0:T(8,128)(2,1)S(1)}, bf16[2,64,384]{2,1,0:T(8,128)(2,1)S(1)}, u32[]{:S(2)}, u32[]{:S(2)}) collective-permute-start(bf16[2,64,384]{2,1,0:T(8,128)(2,1)S(1)} %fusion.1), channel_id=1, source_target_pairs={{0,8},{1,9},{2,10},{3,11},{4,12},{5,13},{6,14},{7,15},{8,0},{9,1},... | collective-permute-start | bytes 294920 | tf_op jit(solution)/shard_map/ppermute | solution.py:384
  26.3 5.4 %collective-permute-start.9 = (bf16[2,64,384]{2,1,0:T(8,128)(2,1)S(1)}, bf16[2,64,384]{2,1,0:T(8,128)(2,1)S(1)}, u32[]{:S(2)}, u32[]{:S(2)}) collective-permute-start(bf16[2,64,384]{2,1,0:T(8,128)(2,1)S(1)} %get-tuple-element.27), channel_id=1, source_target_pairs={{0,4},{1,3},{2,6},{3,1},{4,0},{5,7},{6,2},{7,5},{8,12},{9,11},{10,... | collective-permute-start | bytes 294920 | tf_op jit(solution)/shard_map/ppermute | solution.py:384
  27.3 6.5 %collective-permute-start.6 = (bf16[2,64,384]{2,1,0:T(8,128)(2,1)S(1)}, bf16[2,64,384]{2,1,0:T(8,128)(2,1)S(1)}, u32[]{:S(2)}, u32[]{:S(2)}) collective-permute-start(bf16[2,64,384]{2,1,0:T(8,128)(2,1)S(1)} %get-tuple-element.29), channel_id=1, source_target_pairs={{0,4},{1,3},{2,6},{3,1},{4,0},{5,7},{6,2},{7,5},{8,12},{9,11},{10,... | collective-permute-start | bytes 294920 | tf_op jit(solution)/shard_map/ppermute | solution.py:384
  31.7 5.7 %collective-permute-start.10 = (bf16[4,64,384]{2,1,0:T(8,128)(2,1)S(1)}, bf16[4,64,384]{2,1,0:T(8,128)(2,1)S(1)}, u32[]{:S(2)}, u32[]{:S(2)}) collective-permute-start(bf16[4,64,384]{2,1,0:T(8,128)(2,1)S(1)} %pad_maximum_fusion.1.refs_0_), channel_id=1, source_target_pairs={{0,2},{1,5},{2,0},{3,7},{4,6},{5,1},{6,4},{7,3},{8,10},{9,13},{10,... | collective-permute-start | bytes 589832 | tf_op jit(solution)/shard_map/ppermute | solution.py:384
  33.8 5.7 %collective-permute-start.7 = (bf16[4,64,384]{2,1,0:T(8,128)(2,1)S(1)}, bf16[4,64,384]{2,1,0:T(8,128)(2,1)S(1)}, u32[]{:S(2)}, u32[]{:S(2)}) collective-permute-start(bf16[4,64,384]{2,1,0:T(8,128)(2,1)S(1)} %pad_maximum_fusion.refs_1_), channel_id=1, source_target_pairs={{0,2},{1,5},{2,0},{3,7},{4,6},{5,1},{6,4},{7,3},{8,10},{9,13},{10,... | collective-permute-start | bytes 589832 | tf_op jit(solution)/shard_map/ppermute | solution.py:384
  39.5 1.9 %copy-start = (bf16[256,6144]{1,0:T(8,128)(2,1)S(1)}, bf16[256,6144]{1,0:T(8,128)(2,1)}, u32[]{:S(2)}) copy-start(bf16[256,6144]{1,0:T(8,128)(2,1)} %down_own.5) | copy-start | bytes 9437188
  41.8 7.0 %collective-permute-start.12 = (bf16[4,64,384]{2,1,0:T(8,128)(2,1)S(1)}, bf16[4,64,384]{2,1,0:T(8,128)(2,1)S(1)}, u32[]{:S(2)}, u32[]{:S(2)}) collective-permute-start(bf16[4,64,384]{2,1,0:T(8,128)(2,1)S(1)} %down.4), channel_id=1, source_target_pairs={{0,2},{1,5},{2,0},{3,7},{4,6},{5,1},{6,4},{7,3},{8,10},{9,13},{10,... | collective-permute-start | bytes 589832 | tf_op jit(solution)/shard_map/ppermute | solution.py:384
  44.0 7.7 %collective-permute-start.15 = (bf16[4,64,384]{2,1,0:T(8,128)(2,1)S(1)}, bf16[4,64,384]{2,1,0:T(8,128)(2,1)S(1)}, u32[]{:S(2)}, u32[]{:S(2)}) collective-permute-start(bf16[4,64,384]{2,1,0:T(8,128)(2,1)S(1)} %down.5), channel_id=1, source_target_pairs={{0,2},{1,5},{2,0},{3,7},{4,6},{5,1},{6,4},{7,3},{8,10},{9,13},{10,... | collective-permute-start | bytes 589832 | tf_op jit(solution)/shard_map/ppermute | solution.py:384
  48.9 4.8 %collective-permute-start.13 = (bf16[2,64,384]{2,1,0:T(8,128)(2,1)S(1)}, bf16[2,64,384]{2,1,0:T(8,128)(2,1)S(1)}, u32[]{:S(2)}, u32[]{:S(2)}) collective-permute-start(bf16[2,64,384]{2,1,0:T(8,128)(2,1)S(1)} %slice.115), channel_id=1, source_target_pairs={{0,4},{1,3},{2,6},{3,1},{4,0},{5,7},{6,2},{7,5},{8,12},{9,11},{10,... | collective-permute-start | bytes 294920 | tf_op jit(solution)/shard_map/ppermute | solution.py:384
  51.8 4.7 %collective-permute-start.16 = (bf16[2,64,384]{2,1,0:T(8,128)(2,1)S(1)}, bf16[2,64,384]{2,1,0:T(8,128)(2,1)S(1)}, u32[]{:S(2)}, u32[]{:S(2)}) collective-permute-start(bf16[2,64,384]{2,1,0:T(8,128)(2,1)S(1)} %slice.114), channel_id=1, source_target_pairs={{0,4},{1,3},{2,6},{3,1},{4,0},{5,7},{6,2},{7,5},{8,12},{9,11},{10,... | collective-permute-start | bytes 294920 | tf_op jit(solution)/shard_map/ppermute | solution.py:384
  53.8 5.6 %collective-permute-start.14 = (bf16[1,64,384]{2,1,0:T(8,128)(2,1)S(1)}, bf16[1,64,384]{2,1,0:T(8,128)(2,1)S(1)}, u32[]{:S(2)}, u32[]{:S(2)}) collective-permute-start(bf16[1,64,384]{2,1,0:T(8,128)(2,1)S(1)} %slice.119), channel_id=1, source_target_pairs={{0,8},{1,9},{2,10},{3,11},{4,12},{5,13},{6,14},{7,15},{8,0},{9,1},... | collective-permute-start | bytes 147464 | tf_op jit(solution)/shard_map/ppermute | solution.py:384
  56.6 5.5 %collective-permute-start.17 = (bf16[1,64,384]{2,1,0:T(8,128)(2,1)S(1)}, bf16[1,64,384]{2,1,0:T(8,128)(2,1)S(1)}, u32[]{:S(2)}, u32[]{:S(2)}) collective-permute-start(bf16[1,64,384]{2,1,0:T(8,128)(2,1)S(1)} %slice.118), channel_id=1, source_target_pairs={{0,8},{1,9},{2,10},{3,11},{4,12},{5,13},{6,14},{7,15},{8,0},{9,1},... | collective-permute-start | bytes 147464 | tf_op jit(solution)/shard_map/ppermute | solution.py:384

commit v3 on v2

--- a/solution.py
+++ b/solution.py
@@ -11,7 +11,8 @@
 HS = 128
 BLOCK = 128
 EPSILON = 1e-05
-FOLDS = 2
+FOLDS = 1
+SPLIT = (2, 2)
 ONES = 16
 MIB = 1024 * 1024
 F32 = jnp.float32
@@ -105,22 +106,34 @@
     return (result + own_prob * fresh_value.astype(F32)).astype(BF16)
 
 
-def head_kernel(count, step, *refs):
-    sources, refs = refs[:7], refs[7:]
-    sends, keeps, mask, refs = refs[:FOLDS], refs[FOLDS : 2 * FOLDS], refs[2 * FOLDS], refs[2 * FOLDS + 1 :]
+def head_kernel(count, step, begin, *refs):
+    sources, refs = refs[:8], refs[8:]
+    sends, keeps, refs = refs[:FOLDS], refs[FOLDS : 2 * FOLDS], refs[2 * FOLDS :]
+    mask, carried, refs = refs[0], refs[1], refs[2:]
     lengths, queries, fresh, stream, weight, named, cache, turned, sems = refs
     rows, width = stream.shape
+    all_rows = sources[1].shape[0]
+    here = pl.ds(begin, rows)
+    views = (
+        sources[0],
+        sources[1].at[here],
+        sources[2].at[:, here],
+        sources[3].at[here],
+        sources[4],
+        sources[5],
+    )
     small = [
         pltpu.make_async_copy(source, target, sems.at[i])
-        for i, (source, target) in enumerate(zip(sources[:6], (lengths, queries, fresh, stream, weight, named)))
+        for i, (source, target) in enumerate(zip(views, (lengths, queries, fresh, stream, weight, named)))
     ]
     blocks = [
         pltpu.make_async_copy(
-            sources[6].at[:, pl.ds(i * step, step)], cache.at[:, pl.ds(i * step, step)], sems.at[6 + i]
+            sources[6].at[:, pl.ds(begin + i * step, step)], cache.at[:, pl.ds(i * step, step)], sems.at[6 + i]
         )
         for i in range(rows // step)
     ]
-    for copy in small[:3] + blocks + small[3:]:
+    fetch = pltpu.make_async_copy(sources[7], carried, sems.at[6 + len(blocks)])
+    for copy in small[:3] + blocks + small[3:] + [fetch]:
         copy.start()
     for copy in small[:3]:
         copy.wait()
@@ -130,7 +143,7 @@
         span = slice(i * step, (i + 1) * step)
         parts.append(
             attend_block(
-                queries[span, :], fresh[0, span, :], fresh[1, span, :], cache[0, span], cache[1, span], lengths, i * step
+                queries[span, :], fresh[0, span, :], fresh[1, span, :], cache[0, span], cache[1, span], lengths, begin + i * step
             )
         )
     attended = jnp.concatenate(parts, axis=0)
@@ -152,7 +165,7 @@
         ids = jnp.concatenate([ids, jnp.full((spare, batch), -1.0, F32)], axis=0)
     turned[...] = jnp.transpose(ids)
     core, cores = lax.axis_index("request"), lax.axis_size("request")
-    own = turned[pl.ds(pl.multiple_of(core * rows, rows), rows), :]
+    own = turned[pl.ds(pl.multiple_of(core * all_rows + begin, step), rows), :]
     neurons = mask.shape[1] // 2
     lane = lax.broadcasted_iota(jnp.int32, (rows, neurons), 1) // BLOCK
     for start, place in ((0, core), (neurons, lax.bitwise_xor(core, 1))):
@@ -162,63 +175,65 @@
         for k in range(1, acts):
             active = active | (own[:, k : k + 1] == blocks)
         mask[:, start : start + neurons] = jnp.where(active, 1.0, 0.0)
-
-
-def head(count, queries, fresh_kv, kv_cache, lengths, stream, weight, block_ids, neurons):
-    rows, width = stream.shape
+    fetch.wait()
+
+
+def head(count, begin, rows, queries, fresh_kv, kv_cache, lengths, stream, weight, block_ids, neurons, carried):
+    all_rows, width = stream.shape
     positions = kv_cache.shape[2]
     half, part = count // 2, width // FOLDS
     step = 16
     if part % 128 or queries.shape[1] != HS or rows % step or positions % 128:
-        attended = attend_rows(queries, fresh_kv, kv_cache, lengths)
+        here = slice(begin, begin + rows)
+        attended = attend_rows(queries[here], fresh_kv[:, here], kv_cache[:, here], lengths[here])
         sends, keeps = [], []
         for fold in range(FOLDS):
             pieces = [
                 jnp.dot(attended, pick(weight, 1, i, fold, count, width), preferred_element_type=F32)
                 for i in range(count)
             ]
-            pieces[0] = pieces[0] + stream[:, fold * part : (fold + 1) * part].astype(F32)
+            pieces[0] = pieces[0] + stream[here, fold * part : (fold + 1) * part].astype(F32)
             keeps.append(jnp.stack(pieces[:half]))
             sends.append(jnp.stack(pieces[half:]).astype(BF16))
         core, cores = lax.axis_index("request"), lax.axis_size("request")
         local = jnp.arange(neurons, dtype=jnp.int32) // BLOCK
         base = lax.axis_index("tensor") * cores
         owners = jnp.concatenate([(base + place) * (neurons // BLOCK) + local for place in (core, core ^ 1)])
-        named = lax.dynamic_slice_in_dim(block_ids, core * rows, rows, 0)
+        named = lax.dynamic_slice_in_dim(block_ids, core * all_rows + begin, rows, 0)
         mask = jnp.any(named[:, :, None] == owners[None, None, :], axis=1).astype(F32)
-        return sends, keeps, mask
+        return sends, keeps, mask, carried
     shapes = [(half, rows, part)] * FOLDS
     operands = [
         pltpu.with_memory_space_constraint(array, pltpu.HBM)
-        for array in (lengths, queries, fresh_kv, stream, weight, block_ids.T, kv_cache)
+        for array in (lengths, queries, fresh_kv, stream, weight, block_ids.T, kv_cache, carried)
     ]
     batch, acts = block_ids.shape
     outs = pl.pallas_call(
-        functools.partial(head_kernel, count, step),
-        in_specs=[pl.BlockSpec(memory_space=pltpu.HBM)] * 7,
-        out_specs=whole(2 * FOLDS + 1),
+        functools.partial(head_kernel, count, step, begin),
+        in_specs=[pl.BlockSpec(memory_space=pltpu.HBM)] * 8,
+        out_specs=whole(2 * FOLDS + 2),
         out_shape=[jax.ShapeDtypeStruct(shape, kind) for kind in (BF16, F32) for shape in shapes]
-        + [jax.ShapeDtypeStruct((rows, 2 * neurons), F32)],
+        + [jax.ShapeDtypeStruct((rows, 2 * neurons), F32), jax.ShapeDtypeStruct(carried.shape, BF16)],
         scratch_shapes=[
             pltpu.SMEM(lengths.shape, lengths.dtype),
-            pltpu.VMEM(queries.shape, BF16),
-            pltpu.VMEM(fresh_kv.shape, BF16),
-            pltpu.VMEM(stream.shape, BF16),
+            pltpu.VMEM((rows, HS), BF16),
+            pltpu.VMEM((2, rows, HS), BF16),
+            pltpu.VMEM((rows, width), BF16),
             pltpu.VMEM(weight.shape, BF16),
             pltpu.VMEM((acts, batch), block_ids.dtype),
-            pltpu.VMEM(kv_cache.shape, BF16),
+            pltpu.VMEM((2, rows, positions, HS), BF16),
             pltpu.VMEM((batch, -(-acts // 8) * 8), F32),
-            pltpu.SemaphoreType.DMA((6 + rows // step,)),
+            pltpu.SemaphoreType.DMA((7 + rows // step,)),
         ],
         compiler_params=pltpu.CompilerParams(vmem_limit_bytes=16 * MIB),
         cost_estimate=pl.CostEstimate(
             flops=4 * rows * positions * HS + 2 * rows * weight.size,
-            bytes_accessed=2 * (kv_cache.size + weight.size),
+            bytes_accessed=2 * (2 * rows * positions * HS + weight.size),
             transcendentals=rows * positions,
         ),
         name="head",
     )(*operands)
-    return list(outs[:FOLDS]), list(outs[FOLDS : 2 * FOLDS]), outs[2 * FOLDS]
+    return list(outs[:FOLDS]), list(outs[FOLDS : 2 * FOLDS]), outs[2 * FOLDS], outs[2 * FOLDS + 1]
 
 
 def up_kernel(first, folds, count, width, last, rows, *refs):
@@ -384,44 +399,76 @@
         return lax.ppermute(array, ("tensor", "request"), pairs)
 
     across = [(c, c ^ 1) for c in range(cores)]
-    ups = (up_weight, lax.ppermute(up_weight, "request", across))
-    downs = (down_weight, lax.ppermute(down_weight, "request", across))
+    ups = [up_weight, lax.ppermute(up_weight, "request", across)]
+    downs = [down_weight, lax.ppermute(down_weight, "request", across)]
+    all_rows = queries.shape[0]
+    sizes = [all_rows * share // sum(SPLIT) for share in SPLIT]
     folds = tuple(range(FOLDS))
-    sends, keeps, mask = head(
-        count, queries, fresh_kv, kv_cache, lengths, stream, out_weight, block_ids, up_weight.shape[1]
-    )
+    chains = [(chunk, fold) for chunk in range(len(sizes)) for fold in folds]
+    sends, keeps, masks = {}, {}, []
+    for chunk in range(len(sizes)):
+        holder = downs if chunk else ups
+        send, keep, mask, holder[0] = head(
+            count,
+            sum(sizes[:chunk]),
+            sizes[chunk],
+            queries,
+            fresh_kv,
+            kv_cache,
+            lengths,
+            stream,
+            out_weight,
+            block_ids,
+            up_weight.shape[1],
+            holder[0],
+        )
+        masks.append(mask)
+        for fold in folds:
+            sends[chunk, fold], keeps[chunk, fold] = send[fold], keep[fold]
     for step in range(rounds - 1):
-        for fold in folds:
-            total = keeps[fold] + swap(sends[fold], step).astype(F32)
+        for chain in chains:
+            total = keeps[chain] + swap(sends[chain], step).astype(F32)
             left = total.shape[0] // 2
             if step < rounds - 2:
-                keeps[fold], sends[fold] = total[:left], total[left:].astype(BF16)
+                keeps[chain], sends[chain] = total[:left], total[left:].astype(BF16)
             else:
-                keeps[fold], sends[fold] = total, total.astype(BF16)
-    shares, parts = [], []
-    for fold in folds:
-        mixed = keeps[fold] + swap(sends[fold], rounds - 1)[::-1].astype(F32)
-        shares.append(mixed[0])
-        parts.append(mixed.astype(BF16))
+                keeps[chain], sends[chain] = total, total.astype(BF16)
+    shares, parts = {}, {}
+    for chain in chains:
+        mixed = keeps[chain] + swap(sends[chain], rounds - 1)[::-1].astype(F32)
+        shares[chain] = mixed[0]
+        parts[chain] = mixed.astype(BF16)
     for step in range(rounds - 2, 0, -1):
+        for chain in chains:
+            parts[chain] = jnp.concatenate([parts[chain], swap(parts[chain], step)])
+    gots = {chain: swap(parts[chain], 0) for chain in chains}
+    states = [
+        up(0, folds, count, width, [parts[chunk, fold] for fold in folds], ups, None, None)
+        for chunk in range(len(sizes))
+    ]
+    first = {fold: gots[0, fold] for fold in folds}
+    states, first = lax.optimization_barrier((states, first))
+    gots.update({(0, fold): first[fold] for fold in folds})
+    for chunk in range(len(sizes)):
+        state = states[chunk]
         for fold in folds:
-            parts[fold] = jnp.concatenate([parts[fold], swap(parts[fold], step)])
-    state = up(0, folds, count, width, parts, ups, None, None)
-    for fold in folds:
-        got = swap(parts[fold], 0)
-        state = up(half, (fold,), count, width, [got], ups, state, mask if fold == FOLDS - 1 else None)
-    hidden = state
-    sends = [down(half, half, (fold,), BF16, count, width, hidden, downs)[0] for fold in folds]
-    keeps = list(down(0, half, folds, F32, count, width, hidden, downs))
+            mask = masks[chunk] if fold == FOLDS - 1 else None
+            state = up(half, (fold,), count, width, [gots[chunk, fold]], ups, state, mask)
+        for fold in folds:
+            sends[chunk, fold] = down(half, half, (fold,), BF16, count, width, state, downs)[0]
+        for fold, keep in zip(folds, down(0, half, folds, F32, count, width, state, downs)):
+            keeps[chunk, fold] = keep
     for step in range(rounds):
-        for fold in folds:
-            total = keeps[fold] + swap(sends[fold], step).astype(F32)
+        for chain in chains:
+            total = keeps[chain] + swap(sends[chain], step).astype(F32)
             left = total.shape[0] // 2
-            keeps[fold] = total[: max(left, 1)]
+            keeps[chain] = total[: max(left, 1)]
             if left:
-                sends[fold] = total[left:].astype(BF16)
-    outs = [(shares[fold] + keeps[fold][0]).astype(BF16) for fold in folds]
-    return jnp.concatenate(outs, axis=1)
+                sends[chain] = total[left:].astype(BF16)
+    outs = {chain: (shares[chain] + keeps[chain][0]).astype(BF16) for chain in chains}
+    return jnp.concatenate(
+        [jnp.concatenate([outs[chunk, fold] for fold in folds], axis=1) for chunk in range(len(sizes))], axis=0
+    )
 
 
 def solution(mesh):

time: 62.8 us -> 59.4 us (0.946)
  Pallas kernels: 7.08 us -> 11.6 us
  waiting for transfers between devices: 26.3 us -> 22 us
  starting transfers between devices: 26.6 us -> 24.4 us
  local copies, waits for them, and re-layouts: 1.47 us -> 0.07 us
    ppermute x16, waiting for transfers between devices: 26.3 us -> 22 us  [swap(): return lax.ppermute(array, ('tensor', 'request'), pairs)]
    pallas_call x1 -> x2, Pallas kernels: 4.05 us -> 6.3 us  [head(): pl.pallas_call(functools.partial(head_kernel, count, step, begin), in_spe...]
    ppermute x16, starting transfers between devices: 26.1 us -> 23.9 us  [swap(): return lax.ppermute(array, ('tensor', 'request'), pairs)]
    unnamed x4 -> x0, local copies, waits for them, and re-layouts: 1.4 us -> none
    pallas_call x3 -> x4, Pallas kernels: 1.39 us -> 2.62 us  [down(): pl.pallas_call(functools.partial(down_kernel, first, folds, count, width)...]
    pallas_call x3 -> x4, Pallas kernels: 1.64 us -> 2.71 us  [up(): pl.pallas_call(functools.partial(up_kernel, first, folds, count, width, l...]
  transfers between devices with their start and end apart: 18 -> 18, of which waited for: 14 -> 14; matrix products, arithmetic and copies ran while one was open for 1% -> 1% of each run, Pallas kernels for 11% -> 20%
where the time goes in v3:
time: 59.4 us; the launch traced here: 59.3 us
  starting transfers between devices  24.4 us (41%)
  waiting for transfers between devices  22 us (37%)
  Pallas kernels  11.6 us (20%)
  other arithmetic  1.02 us (2%)
    ppermute x16, starting transfers between devices, swap(): return lax.ppermute(array, ('tensor', 'request'), pairs)  23.9 us
    ppermute x16, waiting for transfers between devices, swap(): return lax.ppermute(array, ('tensor', 'request'), pairs)  22 us
    pallas_call x2, Pallas kernels, head(): pl.pallas_call(functools.partial(head_kernel, count, step, begin), in_spe...  6.3 us
    pallas_call x4, Pallas kernels, up(): pl.pallas_call(functools.partial(up_kernel, first, folds, count, width, l...  2.71 us
    pallas_call x4, Pallas kernels, down(): pl.pallas_call(functools.partial(down_kernel, first, folds, count, width)...  2.62 us
  transfers between devices with their start and end apart: 18, of which 14 were waited for; matrix products, arithmetic and copies ran while one was open for 1% of the time, Pallas kernels for 20%

profile of v3, /device:TPU:0, one launch (start us, length us, event | category | flops | bytes accessed | tf_op | source)
XLA Modules:
  0.0 59.3 jit_solution(1894230704059586570)
XLA Ops:
  0.0 0.5 collective-permute-start.4
  0.5 0.1 collective-permute-start.10
  0.5 3.2 %head.2 = (bf16[4,32,768]{2,1,0:T(8,128)(2,1)S(1)}, f32[4,32,768]{2,1,0:T(8,128)S(1)}, f32[32,512]{1,0:T(8,128)S(1)}, bf16[6144,256]{1,0:T(8,128)(2,1)S(1)}) custom-call(s32[64]{0:T(128)} %refs_0_.3, bf16[64,128]{1,0:T(8,128)(2,1)} %refs_1_.3, bf16[2,64,128]{2,1,0:T(8,128)(2,1)} %refs_2_.3, bf16[64,768]{1,0:T(8,128)(2,1)} %refs_3_.3, ...), custom_call_target="tpu_custom_call" | custom-call | flops 52428800 | bytes 3670016 | tf_op jit(solution)/shard_map/head/pallas_call | solution.py:211
  3.7 3.0 %collective-permute-start = (bf16[4,32,768]{2,1,0:T(8,128)(2,1)S(1)}, bf16[4,32,768]{2,1,0:T(8,128)(2,1)S(1)}, u32[]{:S(2)}, u32[]{:S(2)}) collective-permute-start(bf16[4,32,768]{2,1,0:T(8,128)(2,1)S(1)} %get-tuple-element.23), channel_id=1, source_target_pairs={{0,2},{1,5},{2,0},{3,7},{4,6},{5,1},{6,4},{7,3},{8,10},{9,13},{10,... | collective-permute-start | bytes 589832 | tf_op jit(solution)/shard_map/ppermute | solution.py:399
  6.7 3.2 %head.3 = (bf16[4,32,768]{2,1,0:T(8,128)(2,1)S(1)}, f32[4,32,768]{2,1,0:T(8,128)S(1)}, f32[32,512]{1,0:T(8,128)S(1)}, bf16[256,6144]{1,0:T(8,128)(2,1)S(1)}) custom-call(s32[64]{0:T(128)} %refs_0_.3, bf16[64,128]{1,0:T(8,128)(2,1)} %refs_1_.3, bf16[2,64,128]{2,1,0:T(8,128)(2,1)} %refs_2_.3, bf16[64,768]{1,0:T(8,128)(2,1)} %refs_3_.3, ...), custom_call_target="tpu_custom_call" | custom-call | flops 52428800 | bytes 3670016 | tf_op jit(solution)/shard_map/head/pallas_call | solution.py:211
  9.9 0.1 collective-permute-start.5
  10.0 0.4 collective-permute-done
  10.4 2.1 %collective-permute-start.1 = (bf16[2,32,768]{2,1,0:T(8,128)(2,1)S(1)}, bf16[2,32,768]{2,1,0:T(8,128)(2,1)S(1)}, u32[]{:S(2)}, u32[]{:S(2)}) collective-permute-start(bf16[2,32,768]{2,1,0:T(8,128)(2,1)S(1)} %slice.117), channel_id=1, source_target_pairs={{0,4},{1,3},{2,6},{3,1},{4,0},{5,7},{6,2},{7,5},{8,12},{9,11},{10,... | collective-permute-start | bytes 294920 | tf_op jit(solution)/shard_map/ppermute | solution.py:399
  12.6 3.2 %collective-permute-done.5 = bf16[4,32,768]{2,1,0:T(8,128)(2,1)S(1)} collective-permute-done((bf16[4,32,768]{2,1,0:T(8,128)(2,1)S(1)}, bf16[4,32,768]{2,1,0:T(8,128)(2,1)S(1)}, u32[]{:S(2)}, u32[]{:S(2)}) %collective-permute-start.5) | collective-permute-done | bytes 196640 | tf_op jit(solution)/shard_map/ppermute | solution.py:399
  15.8 1.8 %collective-permute-start.6 = (bf16[2,32,768]{2,1,0:T(8,128)(2,1)S(1)}, bf16[2,32,768]{2,1,0:T(8,128)(2,1)S(1)}, u32[]{:S(2)}, u32[]{:S(2)}) collective-permute-start(bf16[2,32,768]{2,1,0:T(8,128)(2,1)S(1)} %slice.116), channel_id=1, source_target_pairs={{0,4},{1,3},{2,6},{3,1},{4,0},{5,7},{6,2},{7,5},{8,12},{9,11},{10,... | collective-permute-start | bytes 294920 | tf_op jit(solution)/shard_map/ppermute | solution.py:399
  17.6 0.0 collective-permute-done.1
  17.6 2.7 %collective-permute-start.2 = (bf16[2,32,768]{2,1,0:T(8,128)(2,1)S(1)}, bf16[2,32,768]{2,1,0:T(8,128)(2,1)S(1)}, u32[]{:S(2)}, u32[]{:S(2)}) collective-permute-start(bf16[2,32,768]{2,1,0:T(8,128)(2,1)S(1)} %fusion), channel_id=1, source_target_pairs={{0,8},{1,9},{2,10},{3,11},{4,12},{5,13},{6,14},{7,15},{8,0},{9,1},... | collective-permute-start | bytes 294920 | tf_op jit(solution)/shard_map/ppermute | solution.py:399
  20.3 0.5 collective-permute-done.6
  20.8 3.4 %collective-permute-start.7 = (bf16[2,32,768]{2,1,0:T(8,128)(2,1)S(1)}, bf16[2,32,768]{2,1,0:T(8,128)(2,1)S(1)}, u32[]{:S(2)}, u32[]{:S(2)}) collective-permute-start(bf16[2,32,768]{2,1,0:T(8,128)(2,1)S(1)} %fusion.1), channel_id=1, source_target_pairs={{0,8},{1,9},{2,10},{3,11},{4,12},{5,13},{6,14},{7,15},{8,0},{9,1},... | collective-permute-start | bytes 294920 | tf_op jit(solution)/shard_map/ppermute | solution.py:399
  24.2 1.9 %collective-permute-done.2 = bf16[2,32,768]{2,1,0:T(8,128)(2,1)S(1)} collective-permute-done((bf16[2,32,768]{2,1,0:T(8,128)(2,1)S(1)}, bf16[2,32,768]{2,1,0:T(8,128)(2,1)S(1)}, u32[]{:S(2)}, u32[]{:S(2)}) %collective-permute-start.2) | collective-permute-done | bytes 98336 | tf_op jit(solution)/shard_map/ppermute | solution.py:399
  26.1 0.1 collective-permute-start.3
  26.2 0.9 %collective-permute-done.7 = bf16[2,32,768]{2,1,0:T(8,128)(2,1)S(1)} collective-permute-done((bf16[2,32,768]{2,1,0:T(8,128)(2,1)S(1)}, bf16[2,32,768]{2,1,0:T(8,128)(2,1)S(1)}, u32[]{:S(2)}, u32[]{:S(2)}) %collective-permute-start.7) | collective-permute-done | bytes 98336 | tf_op jit(solution)/shard_map/ppermute | solution.py:399
  27.1 1.8 %collective-permute-start.8 = (bf16[2,32,768]{2,1,0:T(8,128)(2,1)S(1)}, bf16[2,32,768]{2,1,0:T(8,128)(2,1)S(1)}, u32[]{:S(2)}, u32[]{:S(2)}) collective-permute-start(bf16[2,32,768]{2,1,0:T(8,128)(2,1)S(1)} %get-tuple-element.41), channel_id=1, source_target_pairs={{0,4},{1,3},{2,6},{3,1},{4,0},{5,7},{6,2},{7,5},{8,12},{9,11},{10,... | collective-permute-start | bytes 294920 | tf_op jit(solution)/shard_map/ppermute | solution.py:399
  28.9 2.8 %collective-permute-done.3 = bf16[2,32,768]{2,1,0:T(8,128)(2,1)S(1)} collective-permute-done((bf16[2,32,768]{2,1,0:T(8,128)(2,1)S(1)}, bf16[2,32,768]{2,1,0:T(8,128)(2,1)S(1)}, u32[]{:S(2)}, u32[]{:S(2)}) %collective-permute-start.3) | collective-permute-done | bytes 98336 | tf_op jit(solution)/shard_map/ppermute | solution.py:399
  31.7 1.5 %collective-permute-start.9 = (bf16[4,32,768]{2,1,0:T(8,128)(2,1)S(1)}, bf16[4,32,768]{2,1,0:T(8,128)(2,1)S(1)}, u32[]{:S(2)}, u32[]{:S(2)}) collective-permute-start(bf16[4,32,768]{2,1,0:T(8,128)(2,1)S(1)} %pad_maximum_fusion.refs_0_), channel_id=1, source_target_pairs={{0,2},{1,5},{2,0},{3,7},{4,6},{5,1},{6,4},{7,3},{8,10},{9,13},{10,... | collective-permute-start | bytes 589832 | tf_op jit(solution)/shard_map/ppermute | solution.py:399
  33.2 0.6 %collective-permute-done.8 = bf16[2,32,768]{2,1,0:T(8,128)(2,1)S(1)} collective-permute-done((bf16[2,32,768]{2,1,0:T(8,128)(2,1)S(1)}, bf16[2,32,768]{2,1,0:T(8,128)(2,1)S(1)}, u32[]{:S(2)}, u32[]{:S(2)}) %collective-permute-start.8) | collective-permute-done | bytes 98336 | tf_op jit(solution)/shard_map/ppermute | solution.py:399
  33.8 1.5 %collective-permute-start.14 = (bf16[4,32,768]{2,1,0:T(8,128)(2,1)S(1)}, bf16[4,32,768]{2,1,0:T(8,128)(2,1)S(1)}, u32[]{:S(2)}, u32[]{:S(2)}) collective-permute-start(bf16[4,32,768]{2,1,0:T(8,128)(2,1)S(1)} %pad_maximum_fusion.1.refs_0_), channel_id=1, source_target_pairs={{0,2},{1,5},{2,0},{3,7},{4,6},{5,1},{6,4},{7,3},{8,10},{9,13},{10,... | collective-permute-start | bytes 589832 | tf_op jit(solution)/shard_map/ppermute | solution.py:399
  35.3 0.0 collective-permute-done.4.refs_2_
  35.3 0.7 %up.4 = (f32[48,512]{1,0:T(8,128)S(1)}, f32[32,128]{1,0:T(8,128)S(1)}) custom-call(bf16[4,32,768]{2,1,0:T(8,128)(2,1)S(1)} %pad_maximum_fusion.refs_0_, bf16[6144,256]{1,0:T(8,128)(2,1)S(1)} %get-tuple-element.24.refs_1_, bf16[6144,256]{1,0:T(8,128)(2,1)S(1)} %collective-permute-done.4.refs_2_), custom_call_target="tpu_custom_call" | custom-call | flops 100663296 | bytes 3145728 | tf_op jit(solution)/shard_map/up/pallas_call | solution.py:325
  36.0 0.7 %up.5 = (f32[48,512]{1,0:T(8,128)S(1)}, f32[32,128]{1,0:T(8,128)S(1)}) custom-call(bf16[4,32,768]{2,1,0:T(8,128)(2,1)S(1)} %pad_maximum_fusion.1.refs_0_, bf16[6144,256]{1,0:T(8,128)(2,1)S(1)} %get-tuple-element.24.refs_1_, bf16[6144,256]{1,0:T(8,128)(2,1)S(1)} %collective-permute-done.4.refs_2_), custom_call_target="tpu_custom_call" | custom-call | flops 100663296 | bytes 3145728 | tf_op jit(solution)/shard_map/up/pallas_call | solution.py:325
  36.6 0.8 %collective-permute-done.9.refs_0_ = bf16[4,32,768]{2,1,0:T(8,128)(2,1)S(1)} collective-permute-done((bf16[4,32,768]{2,1,0:T(8,128)(2,1)S(1)}, bf16[4,32,768]{2,1,0:T(8,128)(2,1)S(1)}, u32[]{:S(2)}, u32[]{:S(2)}) %collective-permute-start.9) | collective-permute-done | bytes 196640 | tf_op jit(solution)/shard_map/ppermute | solution.py:399
  37.5 0.7 %up.6.hidden = bf16[32,512]{1,0:T(8,128)(2,1)S(1)} custom-call(bf16[4,32,768]{2,1,0:T(8,128)(2,1)S(1)} %collective-permute-done.9.refs_0_, bf16[6144,256]{1,0:T(8,128)(2,1)S(1)} %get-tuple-element.24.refs_1_, bf16[6144,256]{1,0:T(8,128)(2,1)S(1)} %collective-permute-done.4.refs_2_, f32[48,512]{1,0:T(8,128)S(1)} %get-tuple-element.32.refs_3_, ...), custom_call_target="tpu_custom_call" | custom-call | flops 100663296 | bytes 3145728 | tf_op jit(solution)/shard_map/up/pallas_call | solution.py:325
  38.2 0.0 collective-permute-done.10.down_other
  38.2 0.7 %down.5 = bf16[4,32,768]{2,1,0:T(8,128)(2,1)S(1)} custom-call(bf16[32,512]{1,0:T(8,128)(2,1)S(1)} %up.6.hidden, bf16[256,6144]{1,0:T(8,128)(2,1)S(1)} %get-tuple-element.35.down_own, bf16[256,6144]{1,0:T(8,128)(2,1)S(1)} %collective-permute-done.10.down_other), custom_call_target="tpu_custom_call" | custom-call | flops 100663296 | bytes 3145728 | tf_op jit(solution)/shard_map/down/pallas_call | solution.py:365
  38.8 1.5 %collective-permute-start.11 = (bf16[4,32,768]{2,1,0:T(8,128)(2,1)S(1)}, bf16[4,32,768]{2,1,0:T(8,128)(2,1)S(1)}, u32[]{:S(2)}, u32[]{:S(2)}) collective-permute-start(bf16[4,32,768]{2,1,0:T(8,128)(2,1)S(1)} %down.5), channel_id=1, source_target_pairs={{0,2},{1,5},{2,0},{3,7},{4,6},{5,1},{6,4},{7,3},{8,10},{9,13},{10,... | collective-permute-start | bytes 589832 | tf_op jit(solution)/shard_map/ppermute | solution.py:399
  40.3 0.0 collective-permute-done.14.refs_0_
  40.3 0.7 %up.7.hidden = bf16[32,512]{1,0:T(8,128)(2,1)S(1)} custom-call(bf16[4,32,768]{2,1,0:T(8,128)(2,1)S(1)} %collective-permute-done.14.refs_0_, bf16[6144,256]{1,0:T(8,128)(2,1)S(1)} %get-tuple-element.24.refs_1_, bf16[6144,256]{1,0:T(8,128)(2,1)S(1)} %collective-permute-done.4.refs_2_, f32[48,512]{1,0:T(8,128)S(1)} %get-tuple-element.36.refs_3_, ...), custom_call_target="tpu_custom_call" | custom-call | flops 100663296 | bytes 3145728 | tf_op jit(solution)/shard_map/up/pallas_call | solution.py:325
  41.0 0.7 %down.7 = bf16[4,32,768]{2,1,0:T(8,128)(2,1)S(1)} custom-call(bf16[32,512]{1,0:T(8,128)(2,1)S(1)} %up.7.hidden, bf16[256,6144]{1,0:T(8,128)(2,1)S(1)} %get-tuple-element.35.down_own, bf16[256,6144]{1,0:T(8,128)(2,1)S(1)} %collective-permute-done.10.down_other), custom_call_target="tpu_custom_call" | custom-call | flops 100663296 | bytes 3145728 | tf_op jit(solution)/shard_map/down/pallas_call | solution.py:365
  41.7 0.7 %collective-permute-start.15 = (bf16[4,32,768]{2,1,0:T(8,128)(2,1)S(1)}, bf16[4,32,768]{2,1,0:T(8,128)(2,1)S(1)}, u32[]{:S(2)}, u32[]{:S(2)}) collective-permute-start(bf16[4,32,768]{2,1,0:T(8,128)(2,1)S(1)} %down.7), channel_id=1, source_target_pairs={{0,2},{1,5},{2,0},{3,7},{4,6},{5,1},{6,4},{7,3},{8,10},{9,13},{10,... | collective-permute-start | bytes 589832 | tf_op jit(solution)/shard_map/ppermute | solution.py:399
  42.4 0.6 %down.4 = f32[4,32,768]{2,1,0:T(8,128)S(1)} custom-call(bf16[32,512]{1,0:T(8,128)(2,1)S(1)} %up.6.hidden, bf16[256,6144]{1,0:T(8,128)(2,1)S(1)} %get-tuple-element.35.down_own, bf16[256,6144]{1,0:T(8,128)(2,1)S(1)} %collective-permute-done.10.down_other), custom_call_target="tpu_custom_call" | custom-call | flops 100663296 | bytes 3145728 | tf_op jit(solution)/shard_map/down/pallas_call | solution.py:365
  43.0 0.7 %down.6 = f32[4,32,768]{2,1,0:T(8,128)S(1)} custom-call(bf16[32,512]{1,0:T(8,128)(2,1)S(1)} %up.7.hidden, bf16[256,6144]{1,0:T(8,128)(2,1)S(1)} %get-tuple-element.35.down_own, bf16[256,6144]{1,0:T(8,128)(2,1)S(1)} %collective-permute-done.10.down_other), custom_call_target="tpu_custom_call" | custom-call | flops 100663296 | bytes 3145728 | tf_op jit(solution)/shard_map/down/pallas_call | solution.py:365
  43.7 2.6 %collective-permute-done.11 = bf16[4,32,768]{2,1,0:T(8,128)(2,1)S(1)} collective-permute-done((bf16[4,32,768]{2,1,0:T(8,128)(2,1)S(1)}, bf16[4,32,768]{2,1,0:T(8,128)(2,1)S(1)}, u32[]{:S(2)}, u32[]{:S(2)}) %collective-permute-start.11) | collective-permute-done | bytes 196640 | tf_op jit(solution)/shard_map/ppermute | solution.py:399
  46.4 0.1 collective-permute-start.12
  46.5 2.3 %collective-permute-done.15 = bf16[4,32,768]{2,1,0:T(8,128)(2,1)S(1)} collective-permute-done((bf16[4,32,768]{2,1,0:T(8,128)(2,1)S(1)}, bf16[4,32,768]{2,1,0:T(8,128)(2,1)S(1)}, u32[]{:S(2)}, u32[]{:S(2)}) %collective-permute-start.15) | collective-permute-done | bytes 196640 | tf_op jit(solution)/shard_map/ppermute | solution.py:399
  48.8 0.7 %collective-permute-start.16 = (bf16[2,32,768]{2,1,0:T(8,128)(2,1)S(1)}, bf16[2,32,768]{2,1,0:T(8,128)(2,1)S(1)}, u32[]{:S(2)}, u32[]{:S(2)}) collective-permute-start(bf16[2,32,768]{2,1,0:T(8,128)(2,1)S(1)} %slice.114), channel_id=1, source_target_pairs={{0,4},{1,3},{2,6},{3,1},{4,0},{5,7},{6,2},{7,5},{8,12},{9,11},{10,... | collective-permute-start | bytes 294920 | tf_op jit(solution)/shard_map/ppermute | solution.py:399
  49.5 2.1 %collective-permute-done.12 = bf16[2,32,768]{2,1,0:T(8,128)(2,1)S(1)} collective-permute-done((bf16[2,32,768]{2,1,0:T(8,128)(2,1)S(1)}, bf16[2,32,768]{2,1,0:T(8,128)(2,1)S(1)}, u32[]{:S(2)}, u32[]{:S(2)}) %collective-permute-start.12) | collective-permute-done | bytes 98336 | tf_op jit(solution)/shard_map/ppermute | solution.py:399
  51.6 1.4 %collective-permute-start.13 = (bf16[1,32,768]{2,1,0:T(8,128)(2,1)S(1)}, bf16[1,32,768]{2,1,0:T(8,128)(2,1)S(1)}, u32[]{:S(2)}, u32[]{:S(2)}) collective-permute-start(bf16[1,32,768]{2,1,0:T(8,128)(2,1)S(1)} %slice.119), channel_id=1, source_target_pairs={{0,8},{1,9},{2,10},{3,11},{4,12},{5,13},{6,14},{7,15},{8,0},{9,1},... | collective-permute-start | bytes 147464 | tf_op jit(solution)/shard_map/ppermute | solution.py:399
  53.1 0.4 collective-permute-done.16
  53.6 1.5 %collective-permute-start.17 = (bf16[1,32,768]{2,1,0:T(8,128)(2,1)S(1)}, bf16[1,32,768]{2,1,0:T(8,128)(2,1)S(1)}, u32[]{:S(2)}, u32[]{:S(2)}) collective-permute-start(bf16[1,32,768]{2,1,0:T(8,128)(2,1)S(1)} %slice.118), channel_id=1, source_target_pairs={{0,8},{1,9},{2,10},{3,11},{4,12},{5,13},{6,14},{7,15},{8,0},{9,1},... | collective-permute-start | bytes 147464 | tf_op jit(solution)/shard_map/ppermute | solution.py:399
  55.1 2.0 %collective-permute-done.13 = bf16[1,32,768]{2,1,0:T(8,128)(2,1)S(1)} collective-permute-done((bf16[1,32,768]{2,1,0:T(8,128)(2,1)S(1)}, bf16[1,32,768]{2,1,0:T(8,128)(2,1)S(1)}, u32[]{:S(2)}, u32[]{:S(2)}) %collective-permute-start.13) | collective-permute-done | bytes 49184 | tf_op jit(solution)/shard_map/ppermute | solution.py:399
  57.2 1.5 %collective-permute-done.17 = bf16[1,32,768]{2,1,0:T(8,128)(2,1)S(1)} collective-permute-done((bf16[1,32,768]{2,1,0:T(8,128)(2,1)S(1)}, bf16[1,32,768]{2,1,0:T(8,128)(2,1)S(1)}, u32[]{:S(2)}, u32[]{:S(2)}) %collective-permute-start.17) | collective-permute-done | bytes 49184 | tf_op jit(solution)/shard_map/ppermute | solution.py:399
  58.6 0.6 %pad_maximum_fusion.2 = bf16[64,768]{1,0:T(8,128)(2,1)} fusion(bf16[32,768]{1,0:T(8,128)(2,1)S(1)} %fusion.7, bf16[32,768]{1,0:T(8,128)(2,1)S(1)} %fusion.6), kind=kLoop, calls=%fused_computation.26 | loop fusion | flops 196608 | bytes 196608 | tf_op jit(solution)/shard_map/concatenate | solution.py:469
  (20 shorter events, 0.4 us)
Async XLA Ops:
  0.0 35.3 %collective-permute-start.4 = (bf16[6144,256]{1,0:T(8,128)(2,1)}, bf16[6144,256]{1,0:T(8,128)(2,1)S(1)}, u32[]{:S(2)}, u32[]{:S(2)}) collective-permute-start(bf16[6144,256]{1,0:T(8,128)(2,1)} %refs_7_.2), channel_id=1, source_target_pairs={{0,1},{1,0},{2,3},{3,2},{4,5},{5,4},{6,7},{7,6},{8,9},{9,8},{10,11... | collective-permute-start | bytes 9437192 | tf_op jit(solution)/shard_map/ppermute | solution.py:402
  0.5 37.7 %collective-permute-start.10 = (bf16[256,6144]{1,0:T(8,128)(2,1)}, bf16[256,6144]{1,0:T(8,128)(2,1)S(1)}, u32[]{:S(2)}, u32[]{:S(2)}) collective-permute-start(bf16[256,6144]{1,0:T(8,128)(2,1)} %refs_7_.3), channel_id=1, source_target_pairs={{0,1},{1,0},{2,3},{3,2},{4,5},{5,4},{6,7},{7,6},{8,9},{9,8},{10,11... | collective-permute-start | bytes 9437192 | tf_op jit(solution)/shard_map/ppermute | solution.py:403
  3.7 6.7 %collective-permute-start = (bf16[4,32,768]{2,1,0:T(8,128)(2,1)S(1)}, bf16[4,32,768]{2,1,0:T(8,128)(2,1)S(1)}, u32[]{:S(2)}, u32[]{:S(2)}) collective-permute-start(bf16[4,32,768]{2,1,0:T(8,128)(2,1)S(1)} %get-tuple-element.23), channel_id=1, source_target_pairs={{0,2},{1,5},{2,0},{3,7},{4,6},{5,1},{6,4},{7,3},{8,10},{9,13},{10,... | collective-permute-start | bytes 589832 | tf_op jit(solution)/shard_map/ppermute | solution.py:399
  9.9 5.9 %collective-permute-start.5 = (bf16[4,32,768]{2,1,0:T(8,128)(2,1)S(1)}, bf16[4,32,768]{2,1,0:T(8,128)(2,1)S(1)}, u32[]{:S(2)}, u32[]{:S(2)}) collective-permute-start(bf16[4,32,768]{2,1,0:T(8,128)(2,1)S(1)} %get-tuple-element.28), channel_id=1, source_target_pairs={{0,2},{1,5},{2,0},{3,7},{4,6},{5,1},{6,4},{7,3},{8,10},{9,13},{10,... | collective-permute-start | bytes 589832 | tf_op jit(solution)/shard_map/ppermute | solution.py:399
  10.4 7.2 %collective-permute-start.1 = (bf16[2,32,768]{2,1,0:T(8,128)(2,1)S(1)}, bf16[2,32,768]{2,1,0:T(8,128)(2,1)S(1)}, u32[]{:S(2)}, u32[]{:S(2)}) collective-permute-start(bf16[2,32,768]{2,1,0:T(8,128)(2,1)S(1)} %slice.117), channel_id=1, source_target_pairs={{0,4},{1,3},{2,6},{3,1},{4,0},{5,7},{6,2},{7,5},{8,12},{9,11},{10,... | collective-permute-start | bytes 294920 | tf_op jit(solution)/shard_map/ppermute | solution.py:399
  15.8 5.0 %collective-permute-start.6 = (bf16[2,32,768]{2,1,0:T(8,128)(2,1)S(1)}, bf16[2,32,768]{2,1,0:T(8,128)(2,1)S(1)}, u32[]{:S(2)}, u32[]{:S(2)}) collective-permute-start(bf16[2,32,768]{2,1,0:T(8,128)(2,1)S(1)} %slice.116), channel_id=1, source_target_pairs={{0,4},{1,3},{2,6},{3,1},{4,0},{5,7},{6,2},{7,5},{8,12},{9,11},{10,... | collective-permute-start | bytes 294920 | tf_op jit(solution)/shard_map/ppermute | solution.py:399
  17.6 8.5 %collective-permute-start.2 = (bf16[2,32,768]{2,1,0:T(8,128)(2,1)S(1)}, bf16[2,32,768]{2,1,0:T(8,128)(2,1)S(1)}, u32[]{:S(2)}, u32[]{:S(2)}) collective-permute-start(bf16[2,32,768]{2,1,0:T(8,128)(2,1)S(1)} %fusion), channel_id=1, source_target_pairs={{0,8},{1,9},{2,10},{3,11},{4,12},{5,13},{6,14},{7,15},{8,0},{9,1},... | collective-permute-start | bytes 294920 | tf_op jit(solution)/shard_map/ppermute | solution.py:399
  20.8 6.3 %collective-permute-start.7 = (bf16[2,32,768]{2,1,0:T(8,128)(2,1)S(1)}, bf16[2,32,768]{2,1,0:T(8,128)(2,1)S(1)}, u32[]{:S(2)}, u32[]{:S(2)}) collective-permute-start(bf16[2,32,768]{2,1,0:T(8,128)(2,1)S(1)} %fusion.1), channel_id=1, source_target_pairs={{0,8},{1,9},{2,10},{3,11},{4,12},{5,13},{6,14},{7,15},{8,0},{9,1},... | collective-permute-start | bytes 294920 | tf_op jit(solution)/shard_map/ppermute | solution.py:399
  26.1 5.6 %collective-permute-start.3 = (bf16[2,32,768]{2,1,0:T(8,128)(2,1)S(1)}, bf16[2,32,768]{2,1,0:T(8,128)(2,1)S(1)}, u32[]{:S(2)}, u32[]{:S(2)}) collective-permute-start(bf16[2,32,768]{2,1,0:T(8,128)(2,1)S(1)} %get-tuple-element.39), channel_id=1, source_target_pairs={{0,4},{1,3},{2,6},{3,1},{4,0},{5,7},{6,2},{7,5},{8,12},{9,11},{10,... | collective-permute-start | bytes 294920 | tf_op jit(solution)/shard_map/ppermute | solution.py:399
  27.1 6.7 %collective-permute-start.8 = (bf16[2,32,768]{2,1,0:T(8,128)(2,1)S(1)}, bf16[2,32,768]{2,1,0:T(8,128)(2,1)S(1)}, u32[]{:S(2)}, u32[]{:S(2)}) collective-permute-start(bf16[2,32,768]{2,1,0:T(8,128)(2,1)S(1)} %get-tuple-element.41), channel_id=1, source_target_pairs={{0,4},{1,3},{2,6},{3,1},{4,0},{5,7},{6,2},{7,5},{8,12},{9,11},{10,... | collective-permute-start | bytes 294920 | tf_op jit(solution)/shard_map/ppermute | solution.py:399
  31.7 5.7 %collective-permute-start.9 = (bf16[4,32,768]{2,1,0:T(8,128)(2,1)S(1)}, bf16[4,32,768]{2,1,0:T(8,128)(2,1)S(1)}, u32[]{:S(2)}, u32[]{:S(2)}) collective-permute-start(bf16[4,32,768]{2,1,0:T(8,128)(2,1)S(1)} %pad_maximum_fusion.refs_0_), channel_id=1, source_target_pairs={{0,2},{1,5},{2,0},{3,7},{4,6},{5,1},{6,4},{7,3},{8,10},{9,13},{10,... | collective-permute-start | bytes 589832 | tf_op jit(solution)/shard_map/ppermute | solution.py:399
  33.8 6.5 %collective-permute-start.14 = (bf16[4,32,768]{2,1,0:T(8,128)(2,1)S(1)}, bf16[4,32,768]{2,1,0:T(8,128)(2,1)S(1)}, u32[]{:S(2)}, u32[]{:S(2)}) collective-permute-start(bf16[4,32,768]{2,1,0:T(8,128)(2,1)S(1)} %pad_maximum_fusion.1.refs_0_), channel_id=1, source_target_pairs={{0,2},{1,5},{2,0},{3,7},{4,6},{5,1},{6,4},{7,3},{8,10},{9,13},{10,... | collective-permute-start | bytes 589832 | tf_op jit(solution)/shard_map/ppermute | solution.py:399
  38.8 7.5 %collective-permute-start.11 = (bf16[4,32,768]{2,1,0:T(8,128)(2,1)S(1)}, bf16[4,32,768]{2,1,0:T(8,128)(2,1)S(1)}, u32[]{:S(2)}, u32[]{:S(2)}) collective-permute-start(bf16[4,32,768]{2,1,0:T(8,128)(2,1)S(1)} %down.5), channel_id=1, source_target_pairs={{0,2},{1,5},{2,0},{3,7},{4,6},{5,1},{6,4},{7,3},{8,10},{9,13},{10,... | collective-permute-start | bytes 589832 | tf_op jit(solution)/shard_map/ppermute | solution.py:399
  41.7 7.1 %collective-permute-start.15 = (bf16[4,32,768]{2,1,0:T(8,128)(2,1)S(1)}, bf16[4,32,768]{2,1,0:T(8,128)(2,1)S(1)}, u32[]{:S(2)}, u32[]{:S(2)}) collective-permute-start(bf16[4,32,768]{2,1,0:T(8,128)(2,1)S(1)} %down.7), channel_id=1, source_target_pairs={{0,2},{1,5},{2,0},{3,7},{4,6},{5,1},{6,4},{7,3},{8,10},{9,13},{10,... | collective-permute-start | bytes 589832 | tf_op jit(solution)/shard_map/ppermute | solution.py:399
  46.4 5.2 %collective-permute-start.12 = (bf16[2,32,768]{2,1,0:T(8,128)(2,1)S(1)}, bf16[2,32,768]{2,1,0:T(8,128)(2,1)S(1)}, u32[]{:S(2)}, u32[]{:S(2)}) collective-permute-start(bf16[2,32,768]{2,1,0:T(8,128)(2,1)S(1)} %slice.115), channel_id=1, source_target_pairs={{0,4},{1,3},{2,6},{3,1},{4,0},{5,7},{6,2},{7,5},{8,12},{9,11},{10,... | collective-permute-start | bytes 294920 | tf_op jit(solution)/shard_map/ppermute | solution.py:399
  48.8 4.7 %collective-permute-start.16 = (bf16[2,32,768]{2,1,0:T(8,128)(2,1)S(1)}, bf16[2,32,768]{2,1,0:T(8,128)(2,1)S(1)}, u32[]{:S(2)}, u32[]{:S(2)}) collective-permute-start(bf16[2,32,768]{2,1,0:T(8,128)(2,1)S(1)} %slice.114), channel_id=1, source_target_pairs={{0,4},{1,3},{2,6},{3,1},{4,0},{5,7},{6,2},{7,5},{8,12},{9,11},{10,... | collective-permute-start | bytes 294920 | tf_op jit(solution)/shard_map/ppermute | solution.py:399
  51.6 5.5 %collective-permute-start.13 = (bf16[1,32,768]{2,1,0:T(8,128)(2,1)S(1)}, bf16[1,32,768]{2,1,0:T(8,128)(2,1)S(1)}, u32[]{:S(2)}, u32[]{:S(2)}) collective-permute-start(bf16[1,32,768]{2,1,0:T(8,128)(2,1)S(1)} %slice.119), channel_id=1, source_target_pairs={{0,8},{1,9},{2,10},{3,11},{4,12},{5,13},{6,14},{7,15},{8,0},{9,1},... | collective-permute-start | bytes 147464 | tf_op jit(solution)/shard_map/ppermute | solution.py:399
  53.6 5.1 %collective-permute-start.17 = (bf16[1,32,768]{2,1,0:T(8,128)(2,1)S(1)}, bf16[1,32,768]{2,1,0:T(8,128)(2,1)S(1)}, u32[]{:S(2)}, u32[]{:S(2)}) collective-permute-start(bf16[1,32,768]{2,1,0:T(8,128)(2,1)S(1)} %slice.118), channel_id=1, source_target_pairs={{0,8},{1,9},{2,10},{3,11},{4,12},{5,13},{6,14},{7,15},{8,0},{9,1},... | collective-permute-start | bytes 147464 | tf_op jit(solution)/shard_map/ppermute | solution.py:399

commit v4 on v3

--- a/solution.py
+++ b/solution.py
@@ -53,26 +53,34 @@
     return result.astype(BF16).reshape(row_count, width)
 
 
-def spot(core, p, count):
+LEADS = (((0, 1, 2), (1, 0, 2)), ((0, 1, 2), (1, 2, 0)), ((0, 1, 2), (0, 1, 2)))
+
+
+def order_of(core, phase, count):
+    rounds = count.bit_length() - 1
+    lead = [axis for axis in LEADS[phase][core % 2] if axis < rounds]
+    return lead + [axis for axis in range(rounds) if axis not in lead]
+
+
+def spot(core, p, count, phase):
     rounds = count.bit_length() - 1
     bits = [(p >> (rounds - 1 - j)) & 1 for j in range(rounds)]
-    plain = sum(bit << j for j, bit in enumerate(bits))
-    if rounds < 2:
-        return plain
-    turned = sum(bit << j for j, bit in enumerate([bits[1], bits[0]] + bits[2:]))
-    if plain == turned:
-        return plain
-    return jnp.where(lax.rem(core, 2) == 0, plain, turned)
-
-
-def span_of(p, fold, count, width):
-    place = lax.bitwise_xor(lax.axis_index("tensor"), spot(lax.axis_index("request"), p, count))
+    even, odd = [
+        sum(bit << axis for bit, axis in zip(bits, order_of(parity, phase, count))) for parity in (0, 1)
+    ]
+    if even == odd:
+        return even
+    return jnp.where(lax.rem(core, 2) == 0, even, odd)
+
+
+def span_of(p, fold, count, width, phase=0):
+    place = lax.bitwise_xor(lax.axis_index("tensor"), spot(lax.axis_index("request"), p, count, phase))
     part = width // FOLDS
     return pl.ds(pl.multiple_of(place * width + fold * part, part), part)
 
 
-def pick(array, axis, p, fold, count, width):
-    place = lax.axis_index("tensor") ^ spot(lax.axis_index("request"), p, count)
+def pick(array, axis, p, fold, count, width, phase=0):
+    place = lax.axis_index("tensor") ^ spot(lax.axis_index("request"), p, count, phase)
     part = width // FOLDS
     return lax.dynamic_slice_in_dim(array, place * width + fold * part, part, axis)
 
@@ -107,9 +115,9 @@
 
 
 def head_kernel(count, step, begin, *refs):
-    sources, refs = refs[:8], refs[8:]
+    sources, refs = refs[:7], refs[7:]
     sends, keeps, refs = refs[:FOLDS], refs[FOLDS : 2 * FOLDS], refs[2 * FOLDS :]
-    mask, carried, refs = refs[0], refs[1], refs[2:]
+    mask, refs = refs[0], refs[1:]
     lengths, queries, fresh, stream, weight, named, cache, turned, sems = refs
     rows, width = stream.shape
     all_rows = sources[1].shape[0]
@@ -132,8 +140,7 @@
         )
         for i in range(rows // step)
     ]
-    fetch = pltpu.make_async_copy(sources[7], carried, sems.at[6 + len(blocks)])
-    for copy in small[:3] + blocks + small[3:] + [fetch]:
+    for copy in small[:3] + blocks + small[3:]:
         copy.start()
     for copy in small[:3]:
         copy.wait()
@@ -175,10 +182,9 @@
         for k in range(1, acts):
             active = active | (own[:, k : k + 1] == blocks)
         mask[:, start : start + neurons] = jnp.where(active, 1.0, 0.0)
-    fetch.wait()
-
-
-def head(count, begin, rows, queries, fresh_kv, kv_cache, lengths, stream, weight, block_ids, neurons, carried):
+
+
+def head(count, begin, rows, queries, fresh_kv, kv_cache, lengths, stream, weight, block_ids, neurons):
     all_rows, width = stream.shape
     positions = kv_cache.shape[2]
     half, part = count // 2, width // FOLDS
@@ -201,19 +207,19 @@
         owners = jnp.concatenate([(base + place) * (neurons // BLOCK) + local for place in (core, core ^ 1)])
         named = lax.dynamic_slice_in_dim(block_ids, core * all_rows + begin, rows, 0)
         mask = jnp.any(named[:, :, None] == owners[None, None, :], axis=1).astype(F32)
-        return sends, keeps, mask, carried
+        return sends, keeps, mask
     shapes = [(half, rows, part)] * FOLDS
     operands = [
         pltpu.with_memory_space_constraint(array, pltpu.HBM)
-        for array in (lengths, queries, fresh_kv, stream, weight, block_ids.T, kv_cache, carried)
+        for array in (lengths, queries, fresh_kv, stream, weight, block_ids.T, kv_cache)
     ]
     batch, acts = block_ids.shape
     outs = pl.pallas_call(
         functools.partial(head_kernel, count, step, begin),
-        in_specs=[pl.BlockSpec(memory_space=pltpu.HBM)] * 8,
-        out_specs=whole(2 * FOLDS + 2),
+        in_specs=[pl.BlockSpec(memory_space=pltpu.HBM)] * 7,
+        out_specs=whole(2 * FOLDS + 1),
         out_shape=[jax.ShapeDtypeStruct(shape, kind) for kind in (BF16, F32) for shape in shapes]
-        + [jax.ShapeDtypeStruct((rows, 2 * neurons), F32), jax.ShapeDtypeStruct(carried.shape, BF16)],
+        + [jax.ShapeDtypeStruct((rows, 2 * neurons), F32)],
         scratch_shapes=[
             pltpu.SMEM(lengths.shape, lengths.dtype),
             pltpu.VMEM((rows, HS), BF16),
@@ -223,7 +229,7 @@
             pltpu.VMEM((acts, batch), block_ids.dtype),
             pltpu.VMEM((2, rows, positions, HS), BF16),
             pltpu.VMEM((batch, -(-acts // 8) * 8), F32),
-            pltpu.SemaphoreType.DMA((7 + rows // step,)),
+            pltpu.SemaphoreType.DMA((6 + rows // step,)),
         ],
         compiler_params=pltpu.CompilerParams(vmem_limit_bytes=16 * MIB),
         cost_estimate=pl.CostEstimate(
@@ -233,7 +239,35 @@
         ),
         name="head",
     )(*operands)
-    return list(outs[:FOLDS]), list(outs[FOLDS : 2 * FOLDS]), outs[2 * FOLDS], outs[2 * FOLDS + 1]
+    return list(outs[:FOLDS]), list(outs[FOLDS : 2 * FOLDS]), outs[2 * FOLDS]
+
+
+def fetch_kernel(source, after, target, sems):
+    parts = sems.shape[0]
+    size = source.shape[0] // parts
+    copies = [
+        pltpu.make_async_copy(source.at[pl.ds(i * size, size)], target.at[pl.ds(i * size, size)], sems.at[i])
+        for i in range(parts)
+    ]
+    for copy in copies:
+        copy.start()
+    for copy in copies:
+        copy.wait()
+
+
+def fetch(array, after):
+    if after.shape[-1] % 128:
+        return array
+    return pl.pallas_call(
+        fetch_kernel,
+        in_specs=[pl.BlockSpec(memory_space=pltpu.HBM), pl.BlockSpec(memory_space=pl.ANY)],
+        out_specs=whole(1)[0],
+        out_shape=jax.ShapeDtypeStruct(array.shape, array.dtype),
+        scratch_shapes=[pltpu.SemaphoreType.DMA((8,))],
+        compiler_params=pltpu.CompilerParams(vmem_limit_bytes=8 * MIB),
+        cost_estimate=pl.CostEstimate(flops=0, bytes_accessed=4 * array.size, transcendentals=0),
+        name="fetch",
+    )(pltpu.with_memory_space_constraint(array, pltpu.HBM), after)
 
 
 def up_kernel(first, folds, count, width, last, rows, *refs):
@@ -246,7 +280,7 @@
     for fold, ref in zip(folds, pieces):
         for i in range(ref.shape[0]):
             piece = ref[i]
-            span = span_of(first + i, fold, count, width)
+            span = span_of(first + i, fold, count, width, 2)
             wide = piece.astype(F32)
             add_total = jnp.sum(wide, axis=1, keepdims=True)
             add_squares = jnp.sum(wide * wide, axis=1, keepdims=True)
@@ -296,7 +330,7 @@
                     [
                         jnp.dot(
                             stacked,
-                            pick(weight, 0, first + i, fold, count, width),
+                            pick(weight, 0, first + i, fold, count, width, 2),
                             preferred_element_type=F32,
                         )
                         for weight in ups
@@ -342,7 +376,7 @@
     own, other = hidden[:, :neurons], hidden[:, neurons:]
     for fold, out in zip(folds, outs):
         for i in range(out.shape[0]):
-            span = span_of(first + i, fold, count, width)
+            span = span_of(first + i, fold, count, width, 1)
             piece = jnp.dot(own, down_own[:, span], preferred_element_type=F32)
             piece += jnp.dot(other, down_other[:, span], preferred_element_type=F32)
             out[i] = piece.astype(out.dtype)
@@ -356,7 +390,7 @@
         return [
             jnp.stack(
                 [
-                    jnp.dot(hidden, pick(both, 1, first + i, fold, count, width), preferred_element_type=F32)
+                    jnp.dot(hidden, pick(both, 1, first + i, fold, count, width, 1), preferred_element_type=F32)
                     for i in range(amount)
                 ]
             ).astype(kind)
@@ -385,14 +419,9 @@
     rounds = count.bit_length() - 1
     half = count // 2
     width = stream.shape[1]
-    orders = [list(range(rounds)) for _ in range(cores)]
-    for c in range(cores):
-        if c % 2 and rounds > 1:
-            orders[c][0], orders[c][1] = orders[c][1], orders[c][0]
-
-    def swap(array, step):
+    def swap(array, step, phase=0):
         pairs = [
-            (t * cores + c, (t ^ (1 << orders[c][step])) * cores + c)
+            (t * cores + c, (t ^ (1 << order_of(c, phase, count)[step])) * cores + c)
             for t in range(count)
             for c in range(cores)
         ]
@@ -407,8 +436,7 @@
     chains = [(chunk, fold) for chunk in range(len(sizes)) for fold in folds]
     sends, keeps, masks = {}, {}, []
     for chunk in range(len(sizes)):
-        holder = downs if chunk else ups
-        send, keep, mask, holder[0] = head(
+        send, keep, mask = head(
             count,
             sum(sizes[:chunk]),
             sizes[chunk],
@@ -420,14 +448,18 @@
             out_weight,
             block_ids,
             up_weight.shape[1],
-            holder[0],
         )
         masks.append(mask)
         for fold in folds:
             sends[chunk, fold], keeps[chunk, fold] = send[fold], keep[fold]
     for step in range(rounds - 1):
         for chain in chains:
-            total = keeps[chain] + swap(sends[chain], step).astype(F32)
+            got = swap(sends[chain], step)
+            if step == 0 and chain == chains[0]:
+                downs[0] = fetch(down_weight, got)
+            elif step == 0 and chain == chains[1]:
+                got, downs[0] = lax.optimization_barrier((got, downs[0]))
+            total = keeps[chain] + got.astype(F32)
             left = total.shape[0] // 2
             if step < rounds - 2:
                 keeps[chain], sends[chain] = total[:left], total[left:].astype(BF16)
@@ -440,8 +472,8 @@
         parts[chain] = mixed.astype(BF16)
     for step in range(rounds - 2, 0, -1):
         for chain in chains:
-            parts[chain] = jnp.concatenate([parts[chain], swap(parts[chain], step)])
-    gots = {chain: swap(parts[chain], 0) for chain in chains}
+            parts[chain] = jnp.concatenate([parts[chain], swap(parts[chain], step, 2)])
+    gots = {chain: swap(parts[chain], 0, 2) for chain in chains}
     states = [
         up(0, folds, count, width, [parts[chunk, fold] for fold in folds], ups, None, None)
         for chunk in range(len(sizes))
@@ -460,7 +492,7 @@
             keeps[chunk, fold] = keep
     for step in range(rounds):
         for chain in chains:
-            total = keeps[chain] + swap(sends[chain], step).astype(F32)
+            total = keeps[chain] + swap(sends[chain], step, 1).astype(F32)
             left = total.shape[0] // 2
             keeps[chain] = total[: max(left, 1)]
             if left:

time: 59.4 us -> 57 us (0.960)
  waiting for transfers between devices: 22 us -> 16.6 us
  starting transfers between devices: 24.4 us -> 26.1 us
  Pallas kernels: 11.6 us -> 12.9 us
    ppermute x16, waiting for transfers between devices: 22 us -> 16.6 us  [swap(): return lax.ppermute(array, ('tensor', 'request'), pairs)]
    pallas_call x0 -> x1, Pallas kernels: none -> 1.89 us  [fetch(): pl.pallas_call(fetch_kernel, in_specs=[pl.BlockSpec(memory_space=pltpu.HB...]
    ppermute x16, starting transfers between devices: 23.9 us -> 25.6 us  [swap(): return lax.ppermute(array, ('tensor', 'request'), pairs)]
    pallas_call x2, Pallas kernels: 6.3 us -> 5.65 us  [head(): pl.pallas_call(functools.partial(head_kernel, count, step, begin), in_spe...]
  transfers between devices with their start and end apart: 18 -> 18, of which waited for: 14 -> 12; matrix products, arithmetic and copies ran while one was open for 1% -> 1% of each run, Pallas kernels for 20% -> 23%
where the time goes in v4:
time: 57 us; the launch traced here: 56.8 us
  starting transfers between devices  26.1 us (46%)
  waiting for transfers between devices  16.6 us (29%)
  Pallas kernels  12.9 us (23%)
  other arithmetic  1.01 us (2%)
    ppermute x16, starting transfers between devices, swap(): return lax.ppermute(array, ('tensor', 'request'), pairs)  25.6 us
    ppermute x16, waiting for transfers between devices, swap(): return lax.ppermute(array, ('tensor', 'request'), pairs)  16.6 us
    pallas_call x2, Pallas kernels, head(): pl.pallas_call(functools.partial(head_kernel, count, step, begin), in_spe...  5.65 us
    pallas_call x4, Pallas kernels, up(): pl.pallas_call(functools.partial(up_kernel, first, folds, count, width, l...  2.71 us
    pallas_call x4, Pallas kernels, down(): pl.pallas_call(functools.partial(down_kernel, first, folds, count, width)...  2.62 us
    pallas_call x1, Pallas kernels, fetch(): pl.pallas_call(fetch_kernel, in_specs=[pl.BlockSpec(memory_space=pltpu.HB...  1.89 us
  transfers between devices with their start and end apart: 18, of which 12 were waited for; matrix products, arithmetic and copies ran while one was open for 1% of the time, Pallas kernels for 23%

profile of v4, /device:TPU:0, one launch (start us, length us, event | category | flops | bytes accessed | tf_op | source)
XLA Modules:
  0.0 56.8 jit_solution(18160653473215444588)
XLA Ops:
  0.0 0.5 collective-permute-start.4
  0.5 0.1 collective-permute-start.10
  0.5 2.8 %head.2 = (bf16[4,32,768]{2,1,0:T(8,128)(2,1)S(1)}, f32[4,32,768]{2,1,0:T(8,128)S(1)}, f32[32,512]{1,0:T(8,128)S(1)}) custom-call(s32[64]{0:T(128)} %refs_0_.3, bf16[64,128]{1,0:T(8,128)(2,1)} %refs_1_.8, bf16[2,64,128]{2,1,0:T(8,128)(2,1)} %refs_2_.3, bf16[64,768]{1,0:T(8,128)(2,1)} %refs_3_.3, bf16[128,6144]{1,0:T(8,128)(2,1)} %refs_4_.3, ...), custom_call_target="tpu_custom_call" | custom-call | flops 52428800 | bytes 3670016 | tf_op jit(solution)/shard_map/head/pallas_call | solution.py:217
  3.3 3.0 %collective-permute-start = (bf16[4,32,768]{2,1,0:T(8,128)(2,1)S(1)}, bf16[4,32,768]{2,1,0:T(8,128)(2,1)S(1)}, u32[]{:S(2)}, u32[]{:S(2)}) collective-permute-start(bf16[4,32,768]{2,1,0:T(8,128)(2,1)S(1)} %get-tuple-element.23), channel_id=1, source_target_pairs={{0,2},{1,5},{2,0},{3,7},{4,6},{5,1},{6,4},{7,3},{8,10},{9,13},{10,... | collective-permute-start | bytes 589832 | tf_op jit(solution)/shard_map/ppermute | solution.py:428
  6.4 2.8 %head.3 = (bf16[4,32,768]{2,1,0:T(8,128)(2,1)S(1)}, f32[4,32,768]{2,1,0:T(8,128)S(1)}, f32[32,512]{1,0:T(8,128)S(1)}) custom-call(s32[64]{0:T(128)} %refs_0_.3, bf16[64,128]{1,0:T(8,128)(2,1)} %refs_1_.8, bf16[2,64,128]{2,1,0:T(8,128)(2,1)} %refs_2_.3, bf16[64,768]{1,0:T(8,128)(2,1)} %refs_3_.3, bf16[128,6144]{1,0:T(8,128)(2,1)} %refs_4_.3, ...), custom_call_target="tpu_custom_call" | custom-call | flops 52428800 | bytes 3670016 | tf_op jit(solution)/shard_map/head/pallas_call | solution.py:217
  9.2 0.1 collective-permute-start.5
  9.3 0.7 %collective-permute-done.after = bf16[4,32,768]{2,1,0:T(8,128)(2,1)S(1)} collective-permute-done((bf16[4,32,768]{2,1,0:T(8,128)(2,1)S(1)}, bf16[4,32,768]{2,1,0:T(8,128)(2,1)S(1)}, u32[]{:S(2)}, u32[]{:S(2)}) %collective-permute-start) | collective-permute-done | bytes 196640 | tf_op jit(solution)/shard_map/ppermute | solution.py:428
  10.1 2.1 %collective-permute-start.1 = (bf16[2,32,768]{2,1,0:T(8,128)(2,1)S(1)}, bf16[2,32,768]{2,1,0:T(8,128)(2,1)S(1)}, u32[]{:S(2)}, u32[]{:S(2)}) collective-permute-start(bf16[2,32,768]{2,1,0:T(8,128)(2,1)S(1)} %slice.117), channel_id=1, source_target_pairs={{0,4},{1,3},{2,6},{3,1},{4,0},{5,7},{6,2},{7,5},{8,12},{9,11},{10,... | collective-permute-start | bytes 294920 | tf_op jit(solution)/shard_map/ppermute | solution.py:428
  12.2 1.9 %fetch.1.down_own = bf16[256,6144]{1,0:T(8,128)(2,1)S(1)} custom-call(bf16[256,6144]{1,0:T(8,128)(2,1)} %source.1, bf16[4,32,768]{2,1,0:T(8,128)(2,1)S(1)} %collective-permute-done.after), custom_call_target="tpu_custom_call" | custom-call | bytes 6291456 | tf_op jit(solution)/shard_map/fetch/pallas_call | solution.py:261
  14.1 0.0 copy-start
  14.1 1.3 %collective-permute-done.5 = bf16[4,32,768]{2,1,0:T(8,128)(2,1)S(1)} collective-permute-done((bf16[4,32,768]{2,1,0:T(8,128)(2,1)S(1)}, bf16[4,32,768]{2,1,0:T(8,128)(2,1)S(1)}, u32[]{:S(2)}, u32[]{:S(2)}) %collective-permute-start.5) | collective-permute-done | bytes 196640 | tf_op jit(solution)/shard_map/ppermute | solution.py:428
  15.4 1.8 %collective-permute-start.6 = (bf16[2,32,768]{2,1,0:T(8,128)(2,1)S(1)}, bf16[2,32,768]{2,1,0:T(8,128)(2,1)S(1)}, u32[]{:S(2)}, u32[]{:S(2)}) collective-permute-start(bf16[2,32,768]{2,1,0:T(8,128)(2,1)S(1)} %slice.116), channel_id=1, source_target_pairs={{0,4},{1,3},{2,6},{3,1},{4,0},{5,7},{6,2},{7,5},{8,12},{9,11},{10,... | collective-permute-start | bytes 294920 | tf_op jit(solution)/shard_map/ppermute | solution.py:428
  17.3 0.0 collective-permute-done.1
  17.3 2.7 %collective-permute-start.2 = (bf16[2,32,768]{2,1,0:T(8,128)(2,1)S(1)}, bf16[2,32,768]{2,1,0:T(8,128)(2,1)S(1)}, u32[]{:S(2)}, u32[]{:S(2)}) collective-permute-start(bf16[2,32,768]{2,1,0:T(8,128)(2,1)S(1)} %fusion), channel_id=1, source_target_pairs={{0,8},{1,9},{2,10},{3,11},{4,12},{5,13},{6,14},{7,15},{8,0},{9,1},... | collective-permute-start | bytes 294920 | tf_op jit(solution)/shard_map/ppermute | solution.py:428
  19.9 1.1 %collective-permute-done.6 = bf16[2,32,768]{2,1,0:T(8,128)(2,1)S(1)} collective-permute-done((bf16[2,32,768]{2,1,0:T(8,128)(2,1)S(1)}, bf16[2,32,768]{2,1,0:T(8,128)(2,1)S(1)}, u32[]{:S(2)}, u32[]{:S(2)}) %collective-permute-start.6) | collective-permute-done | bytes 98336 | tf_op jit(solution)/shard_map/ppermute | solution.py:428
  21.1 2.9 %collective-permute-start.7 = (bf16[2,32,768]{2,1,0:T(8,128)(2,1)S(1)}, bf16[2,32,768]{2,1,0:T(8,128)(2,1)S(1)}, u32[]{:S(2)}, u32[]{:S(2)}) collective-permute-start(bf16[2,32,768]{2,1,0:T(8,128)(2,1)S(1)} %fusion.1), channel_id=1, source_target_pairs={{0,8},{1,9},{2,10},{3,11},{4,12},{5,13},{6,14},{7,15},{8,0},{9,1},... | collective-permute-start | bytes 294920 | tf_op jit(solution)/shard_map/ppermute | solution.py:428
  24.0 1.5 %collective-permute-done.2 = bf16[2,32,768]{2,1,0:T(8,128)(2,1)S(1)} collective-permute-done((bf16[2,32,768]{2,1,0:T(8,128)(2,1)S(1)}, bf16[2,32,768]{2,1,0:T(8,128)(2,1)S(1)}, u32[]{:S(2)}, u32[]{:S(2)}) %collective-permute-start.2) | collective-permute-done | bytes 98336 | tf_op jit(solution)/shard_map/ppermute | solution.py:428
  25.6 0.1 collective-permute-start.3
  25.7 1.0 %collective-permute-done.7 = bf16[2,32,768]{2,1,0:T(8,128)(2,1)S(1)} collective-permute-done((bf16[2,32,768]{2,1,0:T(8,128)(2,1)S(1)}, bf16[2,32,768]{2,1,0:T(8,128)(2,1)S(1)}, u32[]{:S(2)}, u32[]{:S(2)}) %collective-permute-start.7) | collective-permute-done | bytes 98336 | tf_op jit(solution)/shard_map/ppermute | solution.py:428
  26.7 1.7 %collective-permute-start.8 = (bf16[2,32,768]{2,1,0:T(8,128)(2,1)S(1)}, bf16[2,32,768]{2,1,0:T(8,128)(2,1)S(1)}, u32[]{:S(2)}, u32[]{:S(2)}) collective-permute-start(bf16[2,32,768]{2,1,0:T(8,128)(2,1)S(1)} %get-tuple-element.41), channel_id=1, source_target_pairs={{0,4},{1,5},{2,6},{3,7},{4,0},{5,1},{6,2},{7,3},{8,12},{9,13},{10,... | collective-permute-start | bytes 294920 | tf_op jit(solution)/shard_map/ppermute | solution.py:428
  28.4 1.9 %collective-permute-done.3 = bf16[2,32,768]{2,1,0:T(8,128)(2,1)S(1)} collective-permute-done((bf16[2,32,768]{2,1,0:T(8,128)(2,1)S(1)}, bf16[2,32,768]{2,1,0:T(8,128)(2,1)S(1)}, u32[]{:S(2)}, u32[]{:S(2)}) %collective-permute-start.3) | collective-permute-done | bytes 98336 | tf_op jit(solution)/shard_map/ppermute | solution.py:428
  30.3 1.3 %collective-permute-start.9 = (bf16[4,32,768]{2,1,0:T(8,128)(2,1)S(1)}, bf16[4,32,768]{2,1,0:T(8,128)(2,1)S(1)}, u32[]{:S(2)}, u32[]{:S(2)}) collective-permute-start(bf16[4,32,768]{2,1,0:T(8,128)(2,1)S(1)} %pad_maximum_fusion.refs_0_), channel_id=1, source_target_pairs={{0,2},{1,3},{2,0},{3,1},{4,6},{5,7},{6,4},{7,5},{8,10},{9,11},{10,... | collective-permute-start | bytes 589832 | tf_op jit(solution)/shard_map/ppermute | solution.py:428
  31.6 0.0 collective-permute-done.8
  31.6 1.0 %collective-permute-start.14 = (bf16[4,32,768]{2,1,0:T(8,128)(2,1)S(1)}, bf16[4,32,768]{2,1,0:T(8,128)(2,1)S(1)}, u32[]{:S(2)}, u32[]{:S(2)}) collective-permute-start(bf16[4,32,768]{2,1,0:T(8,128)(2,1)S(1)} %pad_maximum_fusion.1.refs_0_), channel_id=1, source_target_pairs={{0,2},{1,3},{2,0},{3,1},{4,6},{5,7},{6,4},{7,5},{8,10},{9,11},{10,... | collective-permute-start | bytes 589832 | tf_op jit(solution)/shard_map/ppermute | solution.py:428
  32.7 0.7 %up.5 = (f32[48,512]{1,0:T(8,128)S(1)}, f32[32,128]{1,0:T(8,128)S(1)}) custom-call(bf16[4,32,768]{2,1,0:T(8,128)(2,1)S(1)} %pad_maximum_fusion.1.refs_0_, bf16[6144,256]{1,0:T(8,128)(2,1)S(1)} %copy-done, bf16[6144,256]{1,0:T(8,128)(2,1)S(1)} %collective-permute-done.4.refs_2_), custom_call_target="tpu_custom_call" | custom-call | flops 100663296 | bytes 3145728 | tf_op jit(solution)/shard_map/up/pallas_call | solution.py:359
  33.3 0.7 %up.4 = (f32[48,512]{1,0:T(8,128)S(1)}, f32[32,128]{1,0:T(8,128)S(1)}) custom-call(bf16[4,32,768]{2,1,0:T(8,128)(2,1)S(1)} %pad_maximum_fusion.refs_0_, bf16[6144,256]{1,0:T(8,128)(2,1)S(1)} %copy-done, bf16[6144,256]{1,0:T(8,128)(2,1)S(1)} %collective-permute-done.4.refs_2_), custom_call_target="tpu_custom_call" | custom-call | flops 100663296 | bytes 3145728 | tf_op jit(solution)/shard_map/up/pallas_call | solution.py:359
  34.0 2.0 %collective-permute-done.9.refs_0_ = bf16[4,32,768]{2,1,0:T(8,128)(2,1)S(1)} collective-permute-done((bf16[4,32,768]{2,1,0:T(8,128)(2,1)S(1)}, bf16[4,32,768]{2,1,0:T(8,128)(2,1)S(1)}, u32[]{:S(2)}, u32[]{:S(2)}) %collective-permute-start.9) | collective-permute-done | bytes 196640 | tf_op jit(solution)/shard_map/ppermute | solution.py:428
  36.0 0.7 %up.6.hidden = bf16[32,512]{1,0:T(8,128)(2,1)S(1)} custom-call(bf16[4,32,768]{2,1,0:T(8,128)(2,1)S(1)} %collective-permute-done.9.refs_0_, bf16[6144,256]{1,0:T(8,128)(2,1)S(1)} %copy-done, bf16[6144,256]{1,0:T(8,128)(2,1)S(1)} %collective-permute-done.4.refs_2_, f32[48,512]{1,0:T(8,128)S(1)} %get-tuple-element.32.refs_3_, ...), custom_call_target="tpu_custom_call" | custom-call | flops 100663296 | bytes 3145728 | tf_op jit(solution)/shard_map/up/pallas_call | solution.py:359
  36.7 0.0 collective-permute-done.10.down_other
  36.7 0.7 %down.5 = bf16[4,32,768]{2,1,0:T(8,128)(2,1)S(1)} custom-call(bf16[32,512]{1,0:T(8,128)(2,1)S(1)} %up.6.hidden, bf16[256,6144]{1,0:T(8,128)(2,1)S(1)} %fetch.1.down_own, bf16[256,6144]{1,0:T(8,128)(2,1)S(1)} %collective-permute-done.10.down_other), custom_call_target="tpu_custom_call" | custom-call | flops 100663296 | bytes 3145728 | tf_op jit(solution)/shard_map/down/pallas_call | solution.py:399
  37.4 1.3 %collective-permute-start.11 = (bf16[4,32,768]{2,1,0:T(8,128)(2,1)S(1)}, bf16[4,32,768]{2,1,0:T(8,128)(2,1)S(1)}, u32[]{:S(2)}, u32[]{:S(2)}) collective-permute-start(bf16[4,32,768]{2,1,0:T(8,128)(2,1)S(1)} %down.5), channel_id=1, source_target_pairs={{0,2},{1,5},{2,0},{3,7},{4,6},{5,1},{6,4},{7,3},{8,10},{9,13},{10,... | collective-permute-start | bytes 589832 | tf_op jit(solution)/shard_map/ppermute | solution.py:428
  38.7 0.0 collective-permute-done.14.refs_0_
  38.7 0.7 %up.7.hidden = bf16[32,512]{1,0:T(8,128)(2,1)S(1)} custom-call(bf16[4,32,768]{2,1,0:T(8,128)(2,1)S(1)} %collective-permute-done.14.refs_0_, bf16[6144,256]{1,0:T(8,128)(2,1)S(1)} %copy-done, bf16[6144,256]{1,0:T(8,128)(2,1)S(1)} %collective-permute-done.4.refs_2_, f32[48,512]{1,0:T(8,128)S(1)} %get-tuple-element.36.refs_3_, ...), custom_call_target="tpu_custom_call" | custom-call | flops 100663296 | bytes 3145728 | tf_op jit(solution)/shard_map/up/pallas_call | solution.py:359
  39.4 0.7 %down.7 = bf16[4,32,768]{2,1,0:T(8,128)(2,1)S(1)} custom-call(bf16[32,512]{1,0:T(8,128)(2,1)S(1)} %up.7.hidden, bf16[256,6144]{1,0:T(8,128)(2,1)S(1)} %fetch.1.down_own, bf16[256,6144]{1,0:T(8,128)(2,1)S(1)} %collective-permute-done.10.down_other), custom_call_target="tpu_custom_call" | custom-call | flops 100663296 | bytes 3145728 | tf_op jit(solution)/shard_map/down/pallas_call | solution.py:399
  40.1 0.8 %collective-permute-start.15 = (bf16[4,32,768]{2,1,0:T(8,128)(2,1)S(1)}, bf16[4,32,768]{2,1,0:T(8,128)(2,1)S(1)}, u32[]{:S(2)}, u32[]{:S(2)}) collective-permute-start(bf16[4,32,768]{2,1,0:T(8,128)(2,1)S(1)} %down.7), channel_id=1, source_target_pairs={{0,2},{1,5},{2,0},{3,7},{4,6},{5,1},{6,4},{7,3},{8,10},{9,13},{10,... | collective-permute-start | bytes 589832 | tf_op jit(solution)/shard_map/ppermute | solution.py:428
  40.9 0.6 %down.6 = f32[4,32,768]{2,1,0:T(8,128)S(1)} custom-call(bf16[32,512]{1,0:T(8,128)(2,1)S(1)} %up.7.hidden, bf16[256,6144]{1,0:T(8,128)(2,1)S(1)} %fetch.1.down_own, bf16[256,6144]{1,0:T(8,128)(2,1)S(1)} %collective-permute-done.10.down_other), custom_call_target="tpu_custom_call" | custom-call | flops 100663296 | bytes 3145728 | tf_op jit(solution)/shard_map/down/pallas_call | solution.py:399
  41.5 0.7 %down.4 = f32[4,32,768]{2,1,0:T(8,128)S(1)} custom-call(bf16[32,512]{1,0:T(8,128)(2,1)S(1)} %up.6.hidden, bf16[256,6144]{1,0:T(8,128)(2,1)S(1)} %fetch.1.down_own, bf16[256,6144]{1,0:T(8,128)(2,1)S(1)} %collective-permute-done.10.down_other), custom_call_target="tpu_custom_call" | custom-call | flops 100663296 | bytes 3145728 | tf_op jit(solution)/shard_map/down/pallas_call | solution.py:399
  42.2 0.9 %collective-permute-done.11 = bf16[4,32,768]{2,1,0:T(8,128)(2,1)S(1)} collective-permute-done((bf16[4,32,768]{2,1,0:T(8,128)(2,1)S(1)}, bf16[4,32,768]{2,1,0:T(8,128)(2,1)S(1)}, u32[]{:S(2)}, u32[]{:S(2)}) %collective-permute-start.11) | collective-permute-done | bytes 196640 | tf_op jit(solution)/shard_map/ppermute | solution.py:428
  43.2 1.2 %collective-permute-start.12 = (bf16[2,32,768]{2,1,0:T(8,128)(2,1)S(1)}, bf16[2,32,768]{2,1,0:T(8,128)(2,1)S(1)}, u32[]{:S(2)}, u32[]{:S(2)}) collective-permute-start(bf16[2,32,768]{2,1,0:T(8,128)(2,1)S(1)} %slice.115), channel_id=1, source_target_pairs={{0,4},{1,9},{2,6},{3,11},{4,0},{5,13},{6,2},{7,15},{8,12},{9,1},{1... | collective-permute-start | bytes 294920 | tf_op jit(solution)/shard_map/ppermute | solution.py:428
  44.4 1.4 %collective-permute-done.15 = bf16[4,32,768]{2,1,0:T(8,128)(2,1)S(1)} collective-permute-done((bf16[4,32,768]{2,1,0:T(8,128)(2,1)S(1)}, bf16[4,32,768]{2,1,0:T(8,128)(2,1)S(1)}, u32[]{:S(2)}, u32[]{:S(2)}) %collective-permute-start.15) | collective-permute-done | bytes 196640 | tf_op jit(solution)/shard_map/ppermute | solution.py:428
  45.8 0.7 %collective-permute-start.16 = (bf16[2,32,768]{2,1,0:T(8,128)(2,1)S(1)}, bf16[2,32,768]{2,1,0:T(8,128)(2,1)S(1)}, u32[]{:S(2)}, u32[]{:S(2)}) collective-permute-start(bf16[2,32,768]{2,1,0:T(8,128)(2,1)S(1)} %slice.114), channel_id=1, source_target_pairs={{0,4},{1,9},{2,6},{3,11},{4,0},{5,13},{6,2},{7,15},{8,12},{9,1},{1... | collective-permute-start | bytes 294920 | tf_op jit(solution)/shard_map/ppermute | solution.py:428
  46.5 1.4 %collective-permute-done.12 = bf16[2,32,768]{2,1,0:T(8,128)(2,1)S(1)} collective-permute-done((bf16[2,32,768]{2,1,0:T(8,128)(2,1)S(1)}, bf16[2,32,768]{2,1,0:T(8,128)(2,1)S(1)}, u32[]{:S(2)}, u32[]{:S(2)}) %collective-permute-start.12) | collective-permute-done | bytes 98336 | tf_op jit(solution)/shard_map/ppermute | solution.py:428
  47.9 1.9 %collective-permute-start.13 = (bf16[1,32,768]{2,1,0:T(8,128)(2,1)S(1)}, bf16[1,32,768]{2,1,0:T(8,128)(2,1)S(1)}, u32[]{:S(2)}, u32[]{:S(2)}) collective-permute-start(bf16[1,32,768]{2,1,0:T(8,128)(2,1)S(1)} %slice.119), channel_id=1, source_target_pairs={{0,8},{1,3},{2,10},{3,1},{4,12},{5,7},{6,14},{7,5},{8,0},{9,11},{1... | collective-permute-start | bytes 147464 | tf_op jit(solution)/shard_map/ppermute | solution.py:428
  49.8 0.7 %collective-permute-done.16 = bf16[2,32,768]{2,1,0:T(8,128)(2,1)S(1)} collective-permute-done((bf16[2,32,768]{2,1,0:T(8,128)(2,1)S(1)}, bf16[2,32,768]{2,1,0:T(8,128)(2,1)S(1)}, u32[]{:S(2)}, u32[]{:S(2)}) %collective-permute-start.16) | collective-permute-done | bytes 98336 | tf_op jit(solution)/shard_map/ppermute | solution.py:428
  50.6 2.9 %collective-permute-start.17 = (bf16[1,32,768]{2,1,0:T(8,128)(2,1)S(1)}, bf16[1,32,768]{2,1,0:T(8,128)(2,1)S(1)}, u32[]{:S(2)}, u32[]{:S(2)}) collective-permute-start(bf16[1,32,768]{2,1,0:T(8,128)(2,1)S(1)} %slice.118), channel_id=1, source_target_pairs={{0,8},{1,3},{2,10},{3,1},{4,12},{5,7},{6,14},{7,5},{8,0},{9,11},{1... | collective-permute-start | bytes 147464 | tf_op jit(solution)/shard_map/ppermute | solution.py:428
  53.5 0.0 collective-permute-done.13
  53.5 2.6 %collective-permute-done.17 = bf16[1,32,768]{2,1,0:T(8,128)(2,1)S(1)} collective-permute-done((bf16[1,32,768]{2,1,0:T(8,128)(2,1)S(1)}, bf16[1,32,768]{2,1,0:T(8,128)(2,1)S(1)}, u32[]{:S(2)}, u32[]{:S(2)}) %collective-permute-start.17) | collective-permute-done | bytes 49184 | tf_op jit(solution)/shard_map/ppermute | solution.py:428
  56.2 0.6 %pad_maximum_fusion.2 = bf16[64,768]{1,0:T(8,128)(2,1)} fusion(bf16[32,768]{1,0:T(8,128)(2,1)S(1)} %fusion.7, bf16[32,768]{1,0:T(8,128)(2,1)S(1)} %fusion.6), kind=kLoop, calls=%fused_computation.26 | loop fusion | flops 196608 | bytes 196608 | tf_op jit(solution)/shard_map/concatenate | solution.py:501
  (22 shorter events, 0.4 us)
Async XLA Ops:
  0.0 32.7 %collective-permute-start.4 = (bf16[6144,256]{1,0:T(8,128)(2,1)}, bf16[6144,256]{1,0:T(8,128)(2,1)S(1)}, u32[]{:S(2)}, u32[]{:S(2)}) collective-permute-start(bf16[6144,256]{1,0:T(8,128)(2,1)} %refs_1_.11), channel_id=1, source_target_pairs={{0,1},{1,0},{2,3},{3,2},{4,5},{5,4},{6,7},{7,6},{8,9},{9,8},{10,11... | collective-permute-start | bytes 9437192 | tf_op jit(solution)/shard_map/ppermute | solution.py:431
  0.5 36.3 %collective-permute-start.10 = (bf16[256,6144]{1,0:T(8,128)(2,1)}, bf16[256,6144]{1,0:T(8,128)(2,1)S(1)}, u32[]{:S(2)}, u32[]{:S(2)}) collective-permute-start(bf16[256,6144]{1,0:T(8,128)(2,1)} %source.1), channel_id=1, source_target_pairs={{0,1},{1,0},{2,3},{3,2},{4,5},{5,4},{6,7},{7,6},{8,9},{9,8},{10,11... | collective-permute-start | bytes 9437192 | tf_op jit(solution)/shard_map/ppermute | solution.py:432
  3.3 6.7 %collective-permute-start = (bf16[4,32,768]{2,1,0:T(8,128)(2,1)S(1)}, bf16[4,32,768]{2,1,0:T(8,128)(2,1)S(1)}, u32[]{:S(2)}, u32[]{:S(2)}) collective-permute-start(bf16[4,32,768]{2,1,0:T(8,128)(2,1)S(1)} %get-tuple-element.23), channel_id=1, source_target_pairs={{0,2},{1,5},{2,0},{3,7},{4,6},{5,1},{6,4},{7,3},{8,10},{9,13},{10,... | collective-permute-start | bytes 589832 | tf_op jit(solution)/shard_map/ppermute | solution.py:428
  9.2 6.2 %collective-permute-start.5 = (bf16[4,32,768]{2,1,0:T(8,128)(2,1)S(1)}, bf16[4,32,768]{2,1,0:T(8,128)(2,1)S(1)}, u32[]{:S(2)}, u32[]{:S(2)}) collective-permute-start(bf16[4,32,768]{2,1,0:T(8,128)(2,1)S(1)} %get-tuple-element.27), channel_id=1, source_target_pairs={{0,2},{1,5},{2,0},{3,7},{4,6},{5,1},{6,4},{7,3},{8,10},{9,13},{10,... | collective-permute-start | bytes 589832 | tf_op jit(solution)/shard_map/ppermute | solution.py:428
  10.1 7.2 %collective-permute-start.1 = (bf16[2,32,768]{2,1,0:T(8,128)(2,1)S(1)}, bf16[2,32,768]{2,1,0:T(8,128)(2,1)S(1)}, u32[]{:S(2)}, u32[]{:S(2)}) collective-permute-start(bf16[2,32,768]{2,1,0:T(8,128)(2,1)S(1)} %slice.117), channel_id=1, source_target_pairs={{0,4},{1,3},{2,6},{3,1},{4,0},{5,7},{6,2},{7,5},{8,12},{9,11},{10,... | collective-permute-start | bytes 294920 | tf_op jit(solution)/shard_map/ppermute | solution.py:428
  14.1 18.5 %copy-start = (bf16[6144,256]{1,0:T(8,128)(2,1)S(1)}, bf16[6144,256]{1,0:T(8,128)(2,1)}, u32[]{:S(2)}) copy-start(bf16[6144,256]{1,0:T(8,128)(2,1)} %refs_1_.11) | copy-start | bytes 9437188
  15.4 5.6 %collective-permute-start.6 = (bf16[2,32,768]{2,1,0:T(8,128)(2,1)S(1)}, bf16[2,32,768]{2,1,0:T(8,128)(2,1)S(1)}, u32[]{:S(2)}, u32[]{:S(2)}) collective-permute-start(bf16[2,32,768]{2,1,0:T(8,128)(2,1)S(1)} %slice.116), channel_id=1, source_target_pairs={{0,4},{1,3},{2,6},{3,1},{4,0},{5,7},{6,2},{7,5},{8,12},{9,11},{10,... | collective-permute-start | bytes 294920 | tf_op jit(solution)/shard_map/ppermute | solution.py:428
  17.3 8.3 %collective-permute-start.2 = (bf16[2,32,768]{2,1,0:T(8,128)(2,1)S(1)}, bf16[2,32,768]{2,1,0:T(8,128)(2,1)S(1)}, u32[]{:S(2)}, u32[]{:S(2)}) collective-permute-start(bf16[2,32,768]{2,1,0:T(8,128)(2,1)S(1)} %fusion), channel_id=1, source_target_pairs={{0,8},{1,9},{2,10},{3,11},{4,12},{5,13},{6,14},{7,15},{8,0},{9,1},... | collective-permute-start | bytes 294920 | tf_op jit(solution)/shard_map/ppermute | solution.py:428
  21.1 5.6 %collective-permute-start.7 = (bf16[2,32,768]{2,1,0:T(8,128)(2,1)S(1)}, bf16[2,32,768]{2,1,0:T(8,128)(2,1)S(1)}, u32[]{:S(2)}, u32[]{:S(2)}) collective-permute-start(bf16[2,32,768]{2,1,0:T(8,128)(2,1)S(1)} %fusion.1), channel_id=1, source_target_pairs={{0,8},{1,9},{2,10},{3,11},{4,12},{5,13},{6,14},{7,15},{8,0},{9,1},... | collective-permute-start | bytes 294920 | tf_op jit(solution)/shard_map/ppermute | solution.py:428
  25.6 4.7 %collective-permute-start.3 = (bf16[2,32,768]{2,1,0:T(8,128)(2,1)S(1)}, bf16[2,32,768]{2,1,0:T(8,128)(2,1)S(1)}, u32[]{:S(2)}, u32[]{:S(2)}) collective-permute-start(bf16[2,32,768]{2,1,0:T(8,128)(2,1)S(1)} %get-tuple-element.39), channel_id=1, source_target_pairs={{0,4},{1,5},{2,6},{3,7},{4,0},{5,1},{6,2},{7,3},{8,12},{9,13},{10,... | collective-permute-start | bytes 294920 | tf_op jit(solution)/shard_map/ppermute | solution.py:428
  26.7 4.9 %collective-permute-start.8 = (bf16[2,32,768]{2,1,0:T(8,128)(2,1)S(1)}, bf16[2,32,768]{2,1,0:T(8,128)(2,1)S(1)}, u32[]{:S(2)}, u32[]{:S(2)}) collective-permute-start(bf16[2,32,768]{2,1,0:T(8,128)(2,1)S(1)} %get-tuple-element.41), channel_id=1, source_target_pairs={{0,4},{1,5},{2,6},{3,7},{4,0},{5,1},{6,2},{7,3},{8,12},{9,13},{10,... | collective-permute-start | bytes 294920 | tf_op jit(solution)/shard_map/ppermute | solution.py:428
  30.3 5.7 %collective-permute-start.9 = (bf16[4,32,768]{2,1,0:T(8,128)(2,1)S(1)}, bf16[4,32,768]{2,1,0:T(8,128)(2,1)S(1)}, u32[]{:S(2)}, u32[]{:S(2)}) collective-permute-start(bf16[4,32,768]{2,1,0:T(8,128)(2,1)S(1)} %pad_maximum_fusion.refs_0_), channel_id=1, source_target_pairs={{0,2},{1,3},{2,0},{3,1},{4,6},{5,7},{6,4},{7,5},{8,10},{9,11},{10,... | collective-permute-start | bytes 589832 | tf_op jit(solution)/shard_map/ppermute | solution.py:428
  31.6 7.1 %collective-permute-start.14 = (bf16[4,32,768]{2,1,0:T(8,128)(2,1)S(1)}, bf16[4,32,768]{2,1,0:T(8,128)(2,1)S(1)}, u32[]{:S(2)}, u32[]{:S(2)}) collective-permute-start(bf16[4,32,768]{2,1,0:T(8,128)(2,1)S(1)} %pad_maximum_fusion.1.refs_0_), channel_id=1, source_target_pairs={{0,2},{1,3},{2,0},{3,1},{4,6},{5,7},{6,4},{7,5},{8,10},{9,11},{10,... | collective-permute-start | bytes 589832 | tf_op jit(solution)/shard_map/ppermute | solution.py:428
  37.4 5.7 %collective-permute-start.11 = (bf16[4,32,768]{2,1,0:T(8,128)(2,1)S(1)}, bf16[4,32,768]{2,1,0:T(8,128)(2,1)S(1)}, u32[]{:S(2)}, u32[]{:S(2)}) collective-permute-start(bf16[4,32,768]{2,1,0:T(8,128)(2,1)S(1)} %down.5), channel_id=1, source_target_pairs={{0,2},{1,5},{2,0},{3,7},{4,6},{5,1},{6,4},{7,3},{8,10},{9,13},{10,... | collective-permute-start | bytes 589832 | tf_op jit(solution)/shard_map/ppermute | solution.py:428
  40.1 5.7 %collective-permute-start.15 = (bf16[4,32,768]{2,1,0:T(8,128)(2,1)S(1)}, bf16[4,32,768]{2,1,0:T(8,128)(2,1)S(1)}, u32[]{:S(2)}, u32[]{:S(2)}) collective-permute-start(bf16[4,32,768]{2,1,0:T(8,128)(2,1)S(1)} %down.7), channel_id=1, source_target_pairs={{0,2},{1,5},{2,0},{3,7},{4,6},{5,1},{6,4},{7,3},{8,10},{9,13},{10,... | collective-permute-start | bytes 589832 | tf_op jit(solution)/shard_map/ppermute | solution.py:428
  43.2 4.7 %collective-permute-start.12 = (bf16[2,32,768]{2,1,0:T(8,128)(2,1)S(1)}, bf16[2,32,768]{2,1,0:T(8,128)(2,1)S(1)}, u32[]{:S(2)}, u32[]{:S(2)}) collective-permute-start(bf16[2,32,768]{2,1,0:T(8,128)(2,1)S(1)} %slice.115), channel_id=1, source_target_pairs={{0,4},{1,9},{2,6},{3,11},{4,0},{5,13},{6,2},{7,15},{8,12},{9,1},{1... | collective-permute-start | bytes 294920 | tf_op jit(solution)/shard_map/ppermute | solution.py:428
  45.8 4.7 %collective-permute-start.16 = (bf16[2,32,768]{2,1,0:T(8,128)(2,1)S(1)}, bf16[2,32,768]{2,1,0:T(8,128)(2,1)S(1)}, u32[]{:S(2)}, u32[]{:S(2)}) collective-permute-start(bf16[2,32,768]{2,1,0:T(8,128)(2,1)S(1)} %slice.114), channel_id=1, source_target_pairs={{0,4},{1,9},{2,6},{3,11},{4,0},{5,13},{6,2},{7,15},{8,12},{9,1},{1... | collective-permute-start | bytes 294920 | tf_op jit(solution)/shard_map/ppermute | solution.py:428
  47.9 5.6 %collective-permute-start.13 = (bf16[1,32,768]{2,1,0:T(8,128)(2,1)S(1)}, bf16[1,32,768]{2,1,0:T(8,128)(2,1)S(1)}, u32[]{:S(2)}, u32[]{:S(2)}) collective-permute-start(bf16[1,32,768]{2,1,0:T(8,128)(2,1)S(1)} %slice.119), channel_id=1, source_target_pairs={{0,8},{1,3},{2,10},{3,1},{4,12},{5,7},{6,14},{7,5},{8,0},{9,11},{1... | collective-permute-start | bytes 147464 | tf_op jit(solution)/shard_map/ppermute | solution.py:428
  50.6 5.6 %collective-permute-start.17 = (bf16[1,32,768]{2,1,0:T(8,128)(2,1)S(1)}, bf16[1,32,768]{2,1,0:T(8,128)(2,1)S(1)}, u32[]{:S(2)}, u32[]{:S(2)}) collective-permute-start(bf16[1,32,768]{2,1,0:T(8,128)(2,1)S(1)} %slice.118), channel_id=1, source_target_pairs={{0,8},{1,3},{2,10},{3,1},{4,12},{5,7},{6,14},{7,5},{8,0},{9,11},{1... | collective-permute-start | bytes 147464 | tf_op jit(solution)/shard_map/ppermute | solution.py:428

commit v5 on v4

--- a/solution.py
+++ b/solution.py
@@ -157,7 +157,8 @@
     for copy in small[3:]:
         copy.wait()
     half, part = count // 2, width // FOLDS
-    for first, outs in ((half, sends), (0, keeps)):
+    keeps[0][...] = attended
+    for first, outs in ((half, sends),):
         for fold, out in enumerate(outs):
             for i in range(half):
                 span = span_of(first + i, fold, count, width)
@@ -182,6 +183,28 @@
         for k in range(1, acts):
             active = active | (own[:, k : k + 1] == blocks)
         mask[:, start : start + neurons] = jnp.where(active, 1.0, 0.0)
+
+
+def hold_kernel(count, begin, attended, weight, stream, keep):
+    half, rows, width = keep.shape
+    for i in range(half):
+        piece = jnp.dot(attended[...], weight[:, span_of(i, 0, count, width)], preferred_element_type=F32)
+        if i == 0:
+            piece = piece + stream[begin : begin + rows, :].astype(F32)
+        keep[i] = piece
+
+
+def hold(count, begin, attended, weight, stream):
+    rows, width = attended.shape[0], stream.shape[1]
+    return pl.pallas_call(
+        functools.partial(hold_kernel, count, begin),
+        in_specs=whole(3),
+        out_specs=whole(1)[0],
+        out_shape=jax.ShapeDtypeStruct((count // 2, rows, width), F32),
+        compiler_params=pltpu.CompilerParams(vmem_limit_bytes=8 * MIB),
+        cost_estimate=pl.CostEstimate(flops=rows * weight.size, bytes_accessed=weight.size, transcendentals=0),
+        name="hold",
+    )(attended, weight, stream)
 
 
 def head(count, begin, rows, queries, fresh_kv, kv_cache, lengths, stream, weight, block_ids, neurons):
@@ -218,7 +241,7 @@
         functools.partial(head_kernel, count, step, begin),
         in_specs=[pl.BlockSpec(memory_space=pltpu.HBM)] * 7,
         out_specs=whole(2 * FOLDS + 1),
-        out_shape=[jax.ShapeDtypeStruct(shape, kind) for kind in (BF16, F32) for shape in shapes]
+        out_shape=[jax.ShapeDtypeStruct(shape, BF16) for shape in shapes + [(rows, HS)]]
         + [jax.ShapeDtypeStruct((rows, 2 * neurons), F32)],
         scratch_shapes=[
             pltpu.SMEM(lengths.shape, lengths.dtype),
@@ -239,7 +262,7 @@
         ),
         name="head",
     )(*operands)
-    return list(outs[:FOLDS]), list(outs[FOLDS : 2 * FOLDS]), outs[2 * FOLDS]
+    return list(outs[:FOLDS]), [hold(count, begin, outs[FOLDS], weight, stream)], outs[2 * FOLDS]
 
 
 def fetch_kernel(source, after, target, sems):

time: 57 us -> 56.3 us (0.988)
  waiting for transfers between devices: 16.6 us -> 15.2 us
    ppermute x16, waiting for transfers between devices: 16.6 us -> 15.2 us  [swap(): return lax.ppermute(array, ('tensor', 'request'), pairs)]
where the time goes in v5:
time: 56.3 us; the launch traced here: 56.1 us
  starting transfers between devices  26.4 us (47%)
  waiting for transfers between devices  15.2 us (27%)
  Pallas kernels  13.2 us (23%)
  other arithmetic  1.05 us (2%)
    ppermute x16, starting transfers between devices, swap(): return lax.ppermute(array, ('tensor', 'request'), pairs)  25.9 us
    ppermute x16, waiting for transfers between devices, swap(): return lax.ppermute(array, ('tensor', 'request'), pairs)  15.2 us
    pallas_call x2, Pallas kernels, head(): pl.pallas_call(functools.partial(head_kernel, count, step, begin), in_spe...  5.47 us
    pallas_call x4, Pallas kernels, up(): pl.pallas_call(functools.partial(up_kernel, first, folds, count, width, l...  2.71 us
    pallas_call x4, Pallas kernels, down(): pl.pallas_call(functools.partial(down_kernel, first, folds, count, width)...  2.62 us
    pallas_call x1, Pallas kernels, fetch(): pl.pallas_call(fetch_kernel, in_specs=[pl.BlockSpec(memory_space=pltpu.HB...  1.89 us
  transfers between devices with their start and end apart: 18, of which 12 were waited for; matrix products, arithmetic and copies ran while one was open for 1% of the time, Pallas kernels for 23%

profile of v5, /device:TPU:0, one launch (start us, length us, event | category | flops | bytes accessed | tf_op | source)
XLA Modules:
  0.0 56.1 jit_solution(12662068325353202950)
XLA Ops:
  0.0 0.5 collective-permute-start.4
  0.5 0.1 collective-permute-start.10
  0.5 2.7 %head.2 = (bf16[4,32,768]{2,1,0:T(8,128)(2,1)S(1)}, bf16[32,128]{1,0:T(8,128)(2,1)S(1)}, f32[32,512]{1,0:T(8,128)S(1)}) custom-call(s32[64]{0:T(128)} %refs_0_.3, bf16[64,128]{1,0:T(8,128)(2,1)} %refs_1_.8, bf16[2,64,128]{2,1,0:T(8,128)(2,1)} %refs_2_.3, bf16[64,768]{1,0:T(8,128)(2,1)} %stream.3, bf16[128,6144]{1,0:T(8,128)(2,1)} %weight.3, ...), custom_call_target="tpu_custom_call" | custom-call | flops 52428800 | bytes 3670016 | tf_op jit(solution)/shard_map/head/pallas_call | solution.py:240
  3.3 0.0 copy-start.1
  3.3 0.0 copy-start.2
  3.3 3.0 %collective-permute-start = (bf16[4,32,768]{2,1,0:T(8,128)(2,1)S(1)}, bf16[4,32,768]{2,1,0:T(8,128)(2,1)S(1)}, u32[]{:S(2)}, u32[]{:S(2)}) collective-permute-start(bf16[4,32,768]{2,1,0:T(8,128)(2,1)S(1)} %get-tuple-element.23), channel_id=1, source_target_pairs={{0,2},{1,5},{2,0},{3,7},{4,6},{5,1},{6,4},{7,3},{8,10},{9,13},{10,... | collective-permute-start | bytes 589832 | tf_op jit(solution)/shard_map/ppermute | solution.py:451
  6.3 2.7 %head.3 = (bf16[4,32,768]{2,1,0:T(8,128)(2,1)S(1)}, bf16[32,128]{1,0:T(8,128)(2,1)S(1)}, f32[32,512]{1,0:T(8,128)S(1)}) custom-call(s32[64]{0:T(128)} %refs_0_.3, bf16[64,128]{1,0:T(8,128)(2,1)} %refs_1_.8, bf16[2,64,128]{2,1,0:T(8,128)(2,1)} %refs_2_.3, bf16[64,768]{1,0:T(8,128)(2,1)} %stream.3, bf16[128,6144]{1,0:T(8,128)(2,1)} %weight.3, ...), custom_call_target="tpu_custom_call" | custom-call | flops 52428800 | bytes 3670016 | tf_op jit(solution)/shard_map/head/pallas_call | solution.py:240
  9.1 0.2 collective-permute-start.5
  9.3 0.2 hold.2
  9.5 0.2 hold.3
  9.7 0.2 collective-permute-done.after
  10.0 2.1 %collective-permute-start.1 = (bf16[2,32,768]{2,1,0:T(8,128)(2,1)S(1)}, bf16[2,32,768]{2,1,0:T(8,128)(2,1)S(1)}, u32[]{:S(2)}, u32[]{:S(2)}) collective-permute-start(bf16[2,32,768]{2,1,0:T(8,128)(2,1)S(1)} %slice.117), channel_id=1, source_target_pairs={{0,4},{1,3},{2,6},{3,1},{4,0},{5,7},{6,2},{7,5},{8,12},{9,11},{10,... | collective-permute-start | bytes 294920 | tf_op jit(solution)/shard_map/ppermute | solution.py:451
  12.2 1.9 %fetch.1.down_own = bf16[256,6144]{1,0:T(8,128)(2,1)S(1)} custom-call(bf16[256,6144]{1,0:T(8,128)(2,1)} %source.1, bf16[4,32,768]{2,1,0:T(8,128)(2,1)S(1)} %collective-permute-done.after), custom_call_target="tpu_custom_call" | custom-call | bytes 6291456 | tf_op jit(solution)/shard_map/fetch/pallas_call | solution.py:284
  14.1 0.0 copy-start
  14.1 1.3 %collective-permute-done.5 = bf16[4,32,768]{2,1,0:T(8,128)(2,1)S(1)} collective-permute-done((bf16[4,32,768]{2,1,0:T(8,128)(2,1)S(1)}, bf16[4,32,768]{2,1,0:T(8,128)(2,1)S(1)}, u32[]{:S(2)}, u32[]{:S(2)}) %collective-permute-start.5) | collective-permute-done | bytes 196640 | tf_op jit(solution)/shard_map/ppermute | solution.py:451
  15.5 1.7 %collective-permute-start.6 = (bf16[2,32,768]{2,1,0:T(8,128)(2,1)S(1)}, bf16[2,32,768]{2,1,0:T(8,128)(2,1)S(1)}, u32[]{:S(2)}, u32[]{:S(2)}) collective-permute-start(bf16[2,32,768]{2,1,0:T(8,128)(2,1)S(1)} %slice.116), channel_id=1, source_target_pairs={{0,4},{1,3},{2,6},{3,1},{4,0},{5,7},{6,2},{7,5},{8,12},{9,11},{10,... | collective-permute-start | bytes 294920 | tf_op jit(solution)/shard_map/ppermute | solution.py:451
  17.2 2.7 %collective-permute-start.2 = (bf16[2,32,768]{2,1,0:T(8,128)(2,1)S(1)}, bf16[2,32,768]{2,1,0:T(8,128)(2,1)S(1)}, u32[]{:S(2)}, u32[]{:S(2)}) collective-permute-start(bf16[2,32,768]{2,1,0:T(8,128)(2,1)S(1)} %fusion), channel_id=1, source_target_pairs={{0,8},{1,9},{2,10},{3,11},{4,12},{5,13},{6,14},{7,15},{8,0},{9,1},... | collective-permute-start | bytes 294920 | tf_op jit(solution)/shard_map/ppermute | solution.py:451
  19.9 1.0 %collective-permute-done.6 = bf16[2,32,768]{2,1,0:T(8,128)(2,1)S(1)} collective-permute-done((bf16[2,32,768]{2,1,0:T(8,128)(2,1)S(1)}, bf16[2,32,768]{2,1,0:T(8,128)(2,1)S(1)}, u32[]{:S(2)}, u32[]{:S(2)}) %collective-permute-start.6) | collective-permute-done | bytes 98336 | tf_op jit(solution)/shard_map/ppermute | solution.py:451
  20.9 3.0 %collective-permute-start.7 = (bf16[2,32,768]{2,1,0:T(8,128)(2,1)S(1)}, bf16[2,32,768]{2,1,0:T(8,128)(2,1)S(1)}, u32[]{:S(2)}, u32[]{:S(2)}) collective-permute-start(bf16[2,32,768]{2,1,0:T(8,128)(2,1)S(1)} %fusion.1), channel_id=1, source_target_pairs={{0,8},{1,9},{2,10},{3,11},{4,12},{5,13},{6,14},{7,15},{8,0},{9,1},... | collective-permute-start | bytes 294920 | tf_op jit(solution)/shard_map/ppermute | solution.py:451
  24.0 1.4 %collective-permute-done.2 = bf16[2,32,768]{2,1,0:T(8,128)(2,1)S(1)} collective-permute-done((bf16[2,32,768]{2,1,0:T(8,128)(2,1)S(1)}, bf16[2,32,768]{2,1,0:T(8,128)(2,1)S(1)}, u32[]{:S(2)}, u32[]{:S(2)}) %collective-permute-start.2) | collective-permute-done | bytes 98336 | tf_op jit(solution)/shard_map/ppermute | solution.py:451
  25.4 0.1 collective-permute-start.3
  25.5 1.2 %collective-permute-done.7 = bf16[2,32,768]{2,1,0:T(8,128)(2,1)S(1)} collective-permute-done((bf16[2,32,768]{2,1,0:T(8,128)(2,1)S(1)}, bf16[2,32,768]{2,1,0:T(8,128)(2,1)S(1)}, u32[]{:S(2)}, u32[]{:S(2)}) %collective-permute-start.7) | collective-permute-done | bytes 98336 | tf_op jit(solution)/shard_map/ppermute | solution.py:451
  26.7 1.8 %collective-permute-start.8 = (bf16[2,32,768]{2,1,0:T(8,128)(2,1)S(1)}, bf16[2,32,768]{2,1,0:T(8,128)(2,1)S(1)}, u32[]{:S(2)}, u32[]{:S(2)}) collective-permute-start(bf16[2,32,768]{2,1,0:T(8,128)(2,1)S(1)} %get-tuple-element.41), channel_id=1, source_target_pairs={{0,4},{1,5},{2,6},{3,7},{4,0},{5,1},{6,2},{7,3},{8,12},{9,13},{10,... | collective-permute-start | bytes 294920 | tf_op jit(solution)/shard_map/ppermute | solution.py:451
  28.5 1.6 %collective-permute-done.3 = bf16[2,32,768]{2,1,0:T(8,128)(2,1)S(1)} collective-permute-done((bf16[2,32,768]{2,1,0:T(8,128)(2,1)S(1)}, bf16[2,32,768]{2,1,0:T(8,128)(2,1)S(1)}, u32[]{:S(2)}, u32[]{:S(2)}) %collective-permute-start.3) | collective-permute-done | bytes 98336 | tf_op jit(solution)/shard_map/ppermute | solution.py:451
  30.1 1.3 %collective-permute-start.9 = (bf16[4,32,768]{2,1,0:T(8,128)(2,1)S(1)}, bf16[4,32,768]{2,1,0:T(8,128)(2,1)S(1)}, u32[]{:S(2)}, u32[]{:S(2)}) collective-permute-start(bf16[4,32,768]{2,1,0:T(8,128)(2,1)S(1)} %pad_maximum_fusion.refs_0_), channel_id=1, source_target_pairs={{0,2},{1,3},{2,0},{3,1},{4,6},{5,7},{6,4},{7,5},{8,10},{9,11},{10,... | collective-permute-start | bytes 589832 | tf_op jit(solution)/shard_map/ppermute | solution.py:451
  31.5 0.0 collective-permute-done.8
  31.5 1.0 %collective-permute-start.14 = (bf16[4,32,768]{2,1,0:T(8,128)(2,1)S(1)}, bf16[4,32,768]{2,1,0:T(8,128)(2,1)S(1)}, u32[]{:S(2)}, u32[]{:S(2)}) collective-permute-start(bf16[4,32,768]{2,1,0:T(8,128)(2,1)S(1)} %pad_maximum_fusion.1.refs_0_), channel_id=1, source_target_pairs={{0,2},{1,3},{2,0},{3,1},{4,6},{5,7},{6,4},{7,5},{8,10},{9,11},{10,... | collective-permute-start | bytes 589832 | tf_op jit(solution)/shard_map/ppermute | solution.py:451
  32.5 0.7 %up.5 = (f32[48,512]{1,0:T(8,128)S(1)}, f32[32,128]{1,0:T(8,128)S(1)}) custom-call(bf16[4,32,768]{2,1,0:T(8,128)(2,1)S(1)} %pad_maximum_fusion.1.refs_0_, bf16[6144,256]{1,0:T(8,128)(2,1)S(1)} %copy-done, bf16[6144,256]{1,0:T(8,128)(2,1)S(1)} %collective-permute-done.4.refs_2_), custom_call_target="tpu_custom_call" | custom-call | flops 100663296 | bytes 3145728 | tf_op jit(solution)/shard_map/up/pallas_call | solution.py:382
  33.2 0.7 %up.4 = (f32[48,512]{1,0:T(8,128)S(1)}, f32[32,128]{1,0:T(8,128)S(1)}) custom-call(bf16[4,32,768]{2,1,0:T(8,128)(2,1)S(1)} %pad_maximum_fusion.refs_0_, bf16[6144,256]{1,0:T(8,128)(2,1)S(1)} %copy-done, bf16[6144,256]{1,0:T(8,128)(2,1)S(1)} %collective-permute-done.4.refs_2_), custom_call_target="tpu_custom_call" | custom-call | flops 100663296 | bytes 3145728 | tf_op jit(solution)/shard_map/up/pallas_call | solution.py:382
  33.8 2.0 %collective-permute-done.9.refs_0_ = bf16[4,32,768]{2,1,0:T(8,128)(2,1)S(1)} collective-permute-done((bf16[4,32,768]{2,1,0:T(8,128)(2,1)S(1)}, bf16[4,32,768]{2,1,0:T(8,128)(2,1)S(1)}, u32[]{:S(2)}, u32[]{:S(2)}) %collective-permute-start.9) | collective-permute-done | bytes 196640 | tf_op jit(solution)/shard_map/ppermute | solution.py:451
  35.9 0.7 %up.6.hidden = bf16[32,512]{1,0:T(8,128)(2,1)S(1)} custom-call(bf16[4,32,768]{2,1,0:T(8,128)(2,1)S(1)} %collective-permute-done.9.refs_0_, bf16[6144,256]{1,0:T(8,128)(2,1)S(1)} %copy-done, bf16[6144,256]{1,0:T(8,128)(2,1)S(1)} %collective-permute-done.4.refs_2_, f32[48,512]{1,0:T(8,128)S(1)} %get-tuple-element.32.refs_3_, ...), custom_call_target="tpu_custom_call" | custom-call | flops 100663296 | bytes 3145728 | tf_op jit(solution)/shard_map/up/pallas_call | solution.py:382
  36.6 0.7 %down.5 = bf16[4,32,768]{2,1,0:T(8,128)(2,1)S(1)} custom-call(bf16[32,512]{1,0:T(8,128)(2,1)S(1)} %up.6.hidden, bf16[256,6144]{1,0:T(8,128)(2,1)S(1)} %fetch.1.down_own, bf16[256,6144]{1,0:T(8,128)(2,1)S(1)} %collective-permute-done.10.down_other), custom_call_target="tpu_custom_call" | custom-call | flops 100663296 | bytes 3145728 | tf_op jit(solution)/shard_map/down/pallas_call | solution.py:422
  37.2 1.3 %collective-permute-start.11 = (bf16[4,32,768]{2,1,0:T(8,128)(2,1)S(1)}, bf16[4,32,768]{2,1,0:T(8,128)(2,1)S(1)}, u32[]{:S(2)}, u32[]{:S(2)}) collective-permute-start(bf16[4,32,768]{2,1,0:T(8,128)(2,1)S(1)} %down.5), channel_id=1, source_target_pairs={{0,2},{1,5},{2,0},{3,7},{4,6},{5,1},{6,4},{7,3},{8,10},{9,13},{10,... | collective-permute-start | bytes 589832 | tf_op jit(solution)/shard_map/ppermute | solution.py:451
  38.5 0.7 %up.7.hidden = bf16[32,512]{1,0:T(8,128)(2,1)S(1)} custom-call(bf16[4,32,768]{2,1,0:T(8,128)(2,1)S(1)} %collective-permute-done.14.refs_0_, bf16[6144,256]{1,0:T(8,128)(2,1)S(1)} %copy-done, bf16[6144,256]{1,0:T(8,128)(2,1)S(1)} %collective-permute-done.4.refs_2_, f32[48,512]{1,0:T(8,128)S(1)} %get-tuple-element.36.refs_3_, ...), custom_call_target="tpu_custom_call" | custom-call | flops 100663296 | bytes 3145728 | tf_op jit(solution)/shard_map/up/pallas_call | solution.py:382
  39.3 0.7 %down.7 = bf16[4,32,768]{2,1,0:T(8,128)(2,1)S(1)} custom-call(bf16[32,512]{1,0:T(8,128)(2,1)S(1)} %up.7.hidden, bf16[256,6144]{1,0:T(8,128)(2,1)S(1)} %fetch.1.down_own, bf16[256,6144]{1,0:T(8,128)(2,1)S(1)} %collective-permute-done.10.down_other), custom_call_target="tpu_custom_call" | custom-call | flops 100663296 | bytes 3145728 | tf_op jit(solution)/shard_map/down/pallas_call | solution.py:422
  39.9 0.8 %collective-permute-start.15 = (bf16[4,32,768]{2,1,0:T(8,128)(2,1)S(1)}, bf16[4,32,768]{2,1,0:T(8,128)(2,1)S(1)}, u32[]{:S(2)}, u32[]{:S(2)}) collective-permute-start(bf16[4,32,768]{2,1,0:T(8,128)(2,1)S(1)} %down.7), channel_id=1, source_target_pairs={{0,2},{1,5},{2,0},{3,7},{4,6},{5,1},{6,4},{7,3},{8,10},{9,13},{10,... | collective-permute-start | bytes 589832 | tf_op jit(solution)/shard_map/ppermute | solution.py:451
  40.7 0.6 %down.6 = f32[4,32,768]{2,1,0:T(8,128)S(1)} custom-call(bf16[32,512]{1,0:T(8,128)(2,1)S(1)} %up.7.hidden, bf16[256,6144]{1,0:T(8,128)(2,1)S(1)} %fetch.1.down_own, bf16[256,6144]{1,0:T(8,128)(2,1)S(1)} %collective-permute-done.10.down_other), custom_call_target="tpu_custom_call" | custom-call | flops 100663296 | bytes 3145728 | tf_op jit(solution)/shard_map/down/pallas_call | solution.py:422
  41.4 0.7 %down.4 = f32[4,32,768]{2,1,0:T(8,128)S(1)} custom-call(bf16[32,512]{1,0:T(8,128)(2,1)S(1)} %up.6.hidden, bf16[256,6144]{1,0:T(8,128)(2,1)S(1)} %fetch.1.down_own, bf16[256,6144]{1,0:T(8,128)(2,1)S(1)} %collective-permute-done.10.down_other), custom_call_target="tpu_custom_call" | custom-call | flops 100663296 | bytes 3145728 | tf_op jit(solution)/shard_map/down/pallas_call | solution.py:422
  42.0 0.9 %collective-permute-done.11 = bf16[4,32,768]{2,1,0:T(8,128)(2,1)S(1)} collective-permute-done((bf16[4,32,768]{2,1,0:T(8,128)(2,1)S(1)}, bf16[4,32,768]{2,1,0:T(8,128)(2,1)S(1)}, u32[]{:S(2)}, u32[]{:S(2)}) %collective-permute-start.11) | collective-permute-done | bytes 196640 | tf_op jit(solution)/shard_map/ppermute | solution.py:451
  43.0 1.3 %collective-permute-start.12 = (bf16[2,32,768]{2,1,0:T(8,128)(2,1)S(1)}, bf16[2,32,768]{2,1,0:T(8,128)(2,1)S(1)}, u32[]{:S(2)}, u32[]{:S(2)}) collective-permute-start(bf16[2,32,768]{2,1,0:T(8,128)(2,1)S(1)} %slice.115), channel_id=1, source_target_pairs={{0,4},{1,9},{2,6},{3,11},{4,0},{5,13},{6,2},{7,15},{8,12},{9,1},{1... | collective-permute-start | bytes 294920 | tf_op jit(solution)/shard_map/ppermute | solution.py:451
  44.4 1.3 %collective-permute-done.15 = bf16[4,32,768]{2,1,0:T(8,128)(2,1)S(1)} collective-permute-done((bf16[4,32,768]{2,1,0:T(8,128)(2,1)S(1)}, bf16[4,32,768]{2,1,0:T(8,128)(2,1)S(1)}, u32[]{:S(2)}, u32[]{:S(2)}) %collective-permute-start.15) | collective-permute-done | bytes 196640 | tf_op jit(solution)/shard_map/ppermute | solution.py:451
  45.7 0.8 %collective-permute-start.16 = (bf16[2,32,768]{2,1,0:T(8,128)(2,1)S(1)}, bf16[2,32,768]{2,1,0:T(8,128)(2,1)S(1)}, u32[]{:S(2)}, u32[]{:S(2)}) collective-permute-start(bf16[2,32,768]{2,1,0:T(8,128)(2,1)S(1)} %slice.114), channel_id=1, source_target_pairs={{0,4},{1,9},{2,6},{3,11},{4,0},{5,13},{6,2},{7,15},{8,12},{9,1},{1... | collective-permute-start | bytes 294920 | tf_op jit(solution)/shard_map/ppermute | solution.py:451
  46.5 1.2 %collective-permute-done.12 = bf16[2,32,768]{2,1,0:T(8,128)(2,1)S(1)} collective-permute-done((bf16[2,32,768]{2,1,0:T(8,128)(2,1)S(1)}, bf16[2,32,768]{2,1,0:T(8,128)(2,1)S(1)}, u32[]{:S(2)}, u32[]{:S(2)}) %collective-permute-start.12) | collective-permute-done | bytes 98336 | tf_op jit(solution)/shard_map/ppermute | solution.py:451
  47.8 2.0 %collective-permute-start.13 = (bf16[1,32,768]{2,1,0:T(8,128)(2,1)S(1)}, bf16[1,32,768]{2,1,0:T(8,128)(2,1)S(1)}, u32[]{:S(2)}, u32[]{:S(2)}) collective-permute-start(bf16[1,32,768]{2,1,0:T(8,128)(2,1)S(1)} %slice.119), channel_id=1, source_target_pairs={{0,8},{1,3},{2,10},{3,1},{4,12},{5,7},{6,14},{7,5},{8,0},{9,11},{1... | collective-permute-start | bytes 147464 | tf_op jit(solution)/shard_map/ppermute | solution.py:451
  49.7 0.7 %collective-permute-done.16 = bf16[2,32,768]{2,1,0:T(8,128)(2,1)S(1)} collective-permute-done((bf16[2,32,768]{2,1,0:T(8,128)(2,1)S(1)}, bf16[2,32,768]{2,1,0:T(8,128)(2,1)S(1)}, u32[]{:S(2)}, u32[]{:S(2)}) %collective-permute-start.16) | collective-permute-done | bytes 98336 | tf_op jit(solution)/shard_map/ppermute | solution.py:451
  50.4 2.7 %collective-permute-start.17 = (bf16[1,32,768]{2,1,0:T(8,128)(2,1)S(1)}, bf16[1,32,768]{2,1,0:T(8,128)(2,1)S(1)}, u32[]{:S(2)}, u32[]{:S(2)}) collective-permute-start(bf16[1,32,768]{2,1,0:T(8,128)(2,1)S(1)} %slice.118), channel_id=1, source_target_pairs={{0,8},{1,3},{2,10},{3,1},{4,12},{5,7},{6,14},{7,5},{8,0},{9,11},{1... | collective-permute-start | bytes 147464 | tf_op jit(solution)/shard_map/ppermute | solution.py:451
  53.1 2.3 %collective-permute-done.17 = bf16[1,32,768]{2,1,0:T(8,128)(2,1)S(1)} collective-permute-done((bf16[1,32,768]{2,1,0:T(8,128)(2,1)S(1)}, bf16[1,32,768]{2,1,0:T(8,128)(2,1)S(1)}, u32[]{:S(2)}, u32[]{:S(2)}) %collective-permute-start.17) | collective-permute-done | bytes 49184 | tf_op jit(solution)/shard_map/ppermute | solution.py:451
  55.5 0.6 %pad_maximum_fusion.2 = bf16[64,768]{1,0:T(8,128)(2,1)} fusion(bf16[32,768]{1,0:T(8,128)(2,1)S(1)} %fusion.7, bf16[32,768]{1,0:T(8,128)(2,1)S(1)} %fusion.6), kind=kLoop, calls=%fused_computation.26 | loop fusion | flops 196608 | bytes 196608 | tf_op jit(solution)/shard_map/concatenate | solution.py:524
  (28 shorter events, 0.5 us)
Async XLA Ops:
  0.0 32.5 %collective-permute-start.4 = (bf16[6144,256]{1,0:T(8,128)(2,1)}, bf16[6144,256]{1,0:T(8,128)(2,1)S(1)}, u32[]{:S(2)}, u32[]{:S(2)}) collective-permute-start(bf16[6144,256]{1,0:T(8,128)(2,1)} %refs_1_.11), channel_id=1, source_target_pairs={{0,1},{1,0},{2,3},{3,2},{4,5},{5,4},{6,7},{7,6},{8,9},{9,8},{10,11... | collective-permute-start | bytes 9437192 | tf_op jit(solution)/shard_map/ppermute | solution.py:454
  0.5 36.1 %collective-permute-start.10 = (bf16[256,6144]{1,0:T(8,128)(2,1)}, bf16[256,6144]{1,0:T(8,128)(2,1)S(1)}, u32[]{:S(2)}, u32[]{:S(2)}) collective-permute-start(bf16[256,6144]{1,0:T(8,128)(2,1)} %source.1), channel_id=1, source_target_pairs={{0,1},{1,0},{2,3},{3,2},{4,5},{5,4},{6,7},{7,6},{8,9},{9,8},{10,11... | collective-permute-start | bytes 9437192 | tf_op jit(solution)/shard_map/ppermute | solution.py:455
  3.3 6.0 %copy-start.1 = (bf16[128,6144]{1,0:T(8,128)(2,1)S(1)}, bf16[128,6144]{1,0:T(8,128)(2,1)}, u32[]{:S(2)}) copy-start(bf16[128,6144]{1,0:T(8,128)(2,1)} %weight.3) | copy-start | bytes 4718596
  3.3 6.0 %copy-start.2 = (bf16[64,768]{1,0:T(8,128)(2,1)S(1)}, bf16[64,768]{1,0:T(8,128)(2,1)}, u32[]{:S(2)}) copy-start(bf16[64,768]{1,0:T(8,128)(2,1)} %stream.3) | copy-start | bytes 294916
  3.3 6.7 %collective-permute-start = (bf16[4,32,768]{2,1,0:T(8,128)(2,1)S(1)}, bf16[4,32,768]{2,1,0:T(8,128)(2,1)S(1)}, u32[]{:S(2)}, u32[]{:S(2)}) collective-permute-start(bf16[4,32,768]{2,1,0:T(8,128)(2,1)S(1)} %get-tuple-element.23), channel_id=1, source_target_pairs={{0,2},{1,5},{2,0},{3,7},{4,6},{5,1},{6,4},{7,3},{8,10},{9,13},{10,... | collective-permute-start | bytes 589832 | tf_op jit(solution)/shard_map/ppermute | solution.py:451
  9.1 6.4 %collective-permute-start.5 = (bf16[4,32,768]{2,1,0:T(8,128)(2,1)S(1)}, bf16[4,32,768]{2,1,0:T(8,128)(2,1)S(1)}, u32[]{:S(2)}, u32[]{:S(2)}) collective-permute-start(bf16[4,32,768]{2,1,0:T(8,128)(2,1)S(1)} %get-tuple-element.27), channel_id=1, source_target_pairs={{0,2},{1,5},{2,0},{3,7},{4,6},{5,1},{6,4},{7,3},{8,10},{9,13},{10,... | collective-permute-start | bytes 589832 | tf_op jit(solution)/shard_map/ppermute | solution.py:451
  10.0 7.2 %collective-permute-start.1 = (bf16[2,32,768]{2,1,0:T(8,128)(2,1)S(1)}, bf16[2,32,768]{2,1,0:T(8,128)(2,1)S(1)}, u32[]{:S(2)}, u32[]{:S(2)}) collective-permute-start(bf16[2,32,768]{2,1,0:T(8,128)(2,1)S(1)} %slice.117), channel_id=1, source_target_pairs={{0,4},{1,3},{2,6},{3,1},{4,0},{5,7},{6,2},{7,5},{8,12},{9,11},{10,... | collective-permute-start | bytes 294920 | tf_op jit(solution)/shard_map/ppermute | solution.py:451
  14.1 18.4 %copy-start = (bf16[6144,256]{1,0:T(8,128)(2,1)S(1)}, bf16[6144,256]{1,0:T(8,128)(2,1)}, u32[]{:S(2)}) copy-start(bf16[6144,256]{1,0:T(8,128)(2,1)} %refs_1_.11) | copy-start | bytes 9437188
  15.5 5.4 %collective-permute-start.6 = (bf16[2,32,768]{2,1,0:T(8,128)(2,1)S(1)}, bf16[2,32,768]{2,1,0:T(8,128)(2,1)S(1)}, u32[]{:S(2)}, u32[]{:S(2)}) collective-permute-start(bf16[2,32,768]{2,1,0:T(8,128)(2,1)S(1)} %slice.116), channel_id=1, source_target_pairs={{0,4},{1,3},{2,6},{3,1},{4,0},{5,7},{6,2},{7,5},{8,12},{9,11},{10,... | collective-permute-start | bytes 294920 | tf_op jit(solution)/shard_map/ppermute | solution.py:451
  17.2 8.2 %collective-permute-start.2 = (bf16[2,32,768]{2,1,0:T(8,128)(2,1)S(1)}, bf16[2,32,768]{2,1,0:T(8,128)(2,1)S(1)}, u32[]{:S(2)}, u32[]{:S(2)}) collective-permute-start(bf16[2,32,768]{2,1,0:T(8,128)(2,1)S(1)} %fusion), channel_id=1, source_target_pairs={{0,8},{1,9},{2,10},{3,11},{4,12},{5,13},{6,14},{7,15},{8,0},{9,1},... | collective-permute-start | bytes 294920 | tf_op jit(solution)/shard_map/ppermute | solution.py:451
  20.9 5.7 %collective-permute-start.7 = (bf16[2,32,768]{2,1,0:T(8,128)(2,1)S(1)}, bf16[2,32,768]{2,1,0:T(8,128)(2,1)S(1)}, u32[]{:S(2)}, u32[]{:S(2)}) collective-permute-start(bf16[2,32,768]{2,1,0:T(8,128)(2,1)S(1)} %fusion.1), channel_id=1, source_target_pairs={{0,8},{1,9},{2,10},{3,11},{4,12},{5,13},{6,14},{7,15},{8,0},{9,1},... | collective-permute-start | bytes 294920 | tf_op jit(solution)/shard_map/ppermute | solution.py:451
  25.4 4.7 %collective-permute-start.3 = (bf16[2,32,768]{2,1,0:T(8,128)(2,1)S(1)}, bf16[2,32,768]{2,1,0:T(8,128)(2,1)S(1)}, u32[]{:S(2)}, u32[]{:S(2)}) collective-permute-start(bf16[2,32,768]{2,1,0:T(8,128)(2,1)S(1)} %get-tuple-element.39), channel_id=1, source_target_pairs={{0,4},{1,5},{2,6},{3,7},{4,0},{5,1},{6,2},{7,3},{8,12},{9,13},{10,... | collective-permute-start | bytes 294920 | tf_op jit(solution)/shard_map/ppermute | solution.py:451
  26.7 4.8 %collective-permute-start.8 = (bf16[2,32,768]{2,1,0:T(8,128)(2,1)S(1)}, bf16[2,32,768]{2,1,0:T(8,128)(2,1)S(1)}, u32[]{:S(2)}, u32[]{:S(2)}) collective-permute-start(bf16[2,32,768]{2,1,0:T(8,128)(2,1)S(1)} %get-tuple-element.41), channel_id=1, source_target_pairs={{0,4},{1,5},{2,6},{3,7},{4,0},{5,1},{6,2},{7,3},{8,12},{9,13},{10,... | collective-permute-start | bytes 294920 | tf_op jit(solution)/shard_map/ppermute | solution.py:451
  30.1 5.7 %collective-permute-start.9 = (bf16[4,32,768]{2,1,0:T(8,128)(2,1)S(1)}, bf16[4,32,768]{2,1,0:T(8,128)(2,1)S(1)}, u32[]{:S(2)}, u32[]{:S(2)}) collective-permute-start(bf16[4,32,768]{2,1,0:T(8,128)(2,1)S(1)} %pad_maximum_fusion.refs_0_), channel_id=1, source_target_pairs={{0,2},{1,3},{2,0},{3,1},{4,6},{5,7},{6,4},{7,5},{8,10},{9,11},{10,... | collective-permute-start | bytes 589832 | tf_op jit(solution)/shard_map/ppermute | solution.py:451
  31.5 7.1 %collective-permute-start.14 = (bf16[4,32,768]{2,1,0:T(8,128)(2,1)S(1)}, bf16[4,32,768]{2,1,0:T(8,128)(2,1)S(1)}, u32[]{:S(2)}, u32[]{:S(2)}) collective-permute-start(bf16[4,32,768]{2,1,0:T(8,128)(2,1)S(1)} %pad_maximum_fusion.1.refs_0_), channel_id=1, source_target_pairs={{0,2},{1,3},{2,0},{3,1},{4,6},{5,7},{6,4},{7,5},{8,10},{9,11},{10,... | collective-permute-start | bytes 589832 | tf_op jit(solution)/shard_map/ppermute | solution.py:451
  37.2 5.7 %collective-permute-start.11 = (bf16[4,32,768]{2,1,0:T(8,128)(2,1)S(1)}, bf16[4,32,768]{2,1,0:T(8,128)(2,1)S(1)}, u32[]{:S(2)}, u32[]{:S(2)}) collective-permute-start(bf16[4,32,768]{2,1,0:T(8,128)(2,1)S(1)} %down.5), channel_id=1, source_target_pairs={{0,2},{1,5},{2,0},{3,7},{4,6},{5,1},{6,4},{7,3},{8,10},{9,13},{10,... | collective-permute-start | bytes 589832 | tf_op jit(solution)/shard_map/ppermute | solution.py:451
  39.9 5.7 %collective-permute-start.15 = (bf16[4,32,768]{2,1,0:T(8,128)(2,1)S(1)}, bf16[4,32,768]{2,1,0:T(8,128)(2,1)S(1)}, u32[]{:S(2)}, u32[]{:S(2)}) collective-permute-start(bf16[4,32,768]{2,1,0:T(8,128)(2,1)S(1)} %down.7), channel_id=1, source_target_pairs={{0,2},{1,5},{2,0},{3,7},{4,6},{5,1},{6,4},{7,3},{8,10},{9,13},{10,... | collective-permute-start | bytes 589832 | tf_op jit(solution)/shard_map/ppermute | solution.py:451
  43.0 4.7 %collective-permute-start.12 = (bf16[2,32,768]{2,1,0:T(8,128)(2,1)S(1)}, bf16[2,32,768]{2,1,0:T(8,128)(2,1)S(1)}, u32[]{:S(2)}, u32[]{:S(2)}) collective-permute-start(bf16[2,32,768]{2,1,0:T(8,128)(2,1)S(1)} %slice.115), channel_id=1, source_target_pairs={{0,4},{1,9},{2,6},{3,11},{4,0},{5,13},{6,2},{7,15},{8,12},{9,1},{1... | collective-permute-start | bytes 294920 | tf_op jit(solution)/shard_map/ppermute | solution.py:451
  45.7 4.7 %collective-permute-start.16 = (bf16[2,32,768]{2,1,0:T(8,128)(2,1)S(1)}, bf16[2,32,768]{2,1,0:T(8,128)(2,1)S(1)}, u32[]{:S(2)}, u32[]{:S(2)}) collective-permute-start(bf16[2,32,768]{2,1,0:T(8,128)(2,1)S(1)} %slice.114), channel_id=1, source_target_pairs={{0,4},{1,9},{2,6},{3,11},{4,0},{5,13},{6,2},{7,15},{8,12},{9,1},{1... | collective-permute-start | bytes 294920 | tf_op jit(solution)/shard_map/ppermute | solution.py:451
  47.8 5.4 %collective-permute-start.13 = (bf16[1,32,768]{2,1,0:T(8,128)(2,1)S(1)}, bf16[1,32,768]{2,1,0:T(8,128)(2,1)S(1)}, u32[]{:S(2)}, u32[]{:S(2)}) collective-permute-start(bf16[1,32,768]{2,1,0:T(8,128)(2,1)S(1)} %slice.119), channel_id=1, source_target_pairs={{0,8},{1,3},{2,10},{3,1},{4,12},{5,7},{6,14},{7,5},{8,0},{9,11},{1... | collective-permute-start | bytes 147464 | tf_op jit(solution)/shard_map/ppermute | solution.py:451
  50.4 5.1 %collective-permute-start.17 = (bf16[1,32,768]{2,1,0:T(8,128)(2,1)S(1)}, bf16[1,32,768]{2,1,0:T(8,128)(2,1)S(1)}, u32[]{:S(2)}, u32[]{:S(2)}) collective-permute-start(bf16[1,32,768]{2,1,0:T(8,128)(2,1)S(1)} %slice.118), channel_id=1, source_target_pairs={{0,8},{1,3},{2,10},{3,1},{4,12},{5,7},{6,14},{7,5},{8,0},{9,11},{1... | collective-permute-start | bytes 147464 | tf_op jit(solution)/shard_map/ppermute | solution.py:451
